TPU v7x, 32 devices: a whole 2x2x4 slice. The times are simulated.
32 devices in a mesh: seq: 2 (over y), fsdp: 16 (over z, x, core).
Axes of the slice: x: 2, y: 2, z: 4, core: 2. Of those that a mesh axis runs over, the one named last changes fastest.
Arguments:
- inputs: bfloat16 [16, 256, 1536], P('fsdp', 'seq'), may hold values from -6 to 6
- positions: int32 [16, 256], P('fsdp', 'seq'), may hold values from 0 to 255, as said below
- segments: int32 [16, 256], P('fsdp'), may hold values from 0 to 3, as said below
- gain_one: float32 [1536], replicated, may hold values from 0.1 to 1.9
- qkv_weight: bfloat16 [1536, 2048], P('fsdp'), may hold values from -0.21875 to 0.21875
- qkv_bias: float32 [2048], replicated, may hold values from -3 to 3
- out_weight: bfloat16 [1536, 1536], P('fsdp'), may hold values from -0.625 to 0.625
- gain_two: float32 [1536], replicated, may hold values from 0.1 to 1.9
- gate_up_weight: bfloat16 [1536, 17920], P('fsdp'), may hold values from -0.15625 to 0.15625
- down_weight: bfloat16 [8960, 1536], P('fsdp'), may hold values from -0.09375 to 0.09375
- cotangent: bfloat16 [16, 256, 1536], P('fsdp', 'seq'), may hold values from -6 to 6
Outputs:
- output: bfloat16 [16, 256, 1536], P('fsdp', 'seq')
- input_grad: float32 [16, 256, 1536], P('fsdp', 'seq')
- gain_one_grad: float32 [1536], replicated
- qkv_weight_grad: float32 [1536, 2048], P('fsdp')
- qkv_bias_grad: float32 [2048], replicated
- out_weight_grad: float32 [1536, 1536], P('fsdp')
- gain_two_grad: float32 [1536], replicated
- gate_up_weight_grad: float32 [1536, 17920], P('fsdp')
- down_weight_grad: float32 [8960, 1536], P('fsdp')
Inputs may be any that keep to these rules, and one draw needn't show every extreme that they name: `positions`: the number of earlier tokens of the same segment in the same sequence. `segments`: in each sequence the segment numbers start at 0 at its first token, never fall, and rise by at most one from a token to the next; the first sequence is a single document, every other sequence holds exactly 4 documents.
All inputs are finite; a program needn't handle non-finite values.
Results may differ from a plain program's by a relative error of at most 0.013.
The roundings to bfloat16 on the way count: a program that leaves them out, or rounds other values in their place, can miss the bound.
Values may be sent and summed in bfloat16 or wider, within the bound.
No kernel may reach another device: no remote copies, remote signals or barrier semaphores. Data moves between devices by JAX's collectives and lax.ppermute only.
A program may use at most 448 MiB of HBM per device.

v0:
```python
import jax
import jax.numpy as jnp
from jax import lax
from jax.sharding import PartitionSpec as P

D = 1536
FF = 8960
HQ = 12
KV = 2
HD = 128


rope_base = 1000000.0
norm_eps = 1e-06


def rope_angles(positions):
    steps_half = jnp.arange(HD // 2, dtype=jnp.float32)
    inverse = rope_base ** (-2.0 * steps_half / HD)
    angles = positions.astype(jnp.float32)[..., None] * inverse
    return (jnp.cos(angles), jnp.sin(angles))


def rotate(values, cosines, sines):
    half_size = values.shape[-1] // 2
    front_half = values[..., :half_size]
    back_half = values[..., half_size:]
    cos_heads = cosines[..., None, :]
    sin_heads = sines[..., None, :]
    return jnp.concatenate(
        [
            front_half * cos_heads - back_half * sin_heads,
            back_half * cos_heads + front_half * sin_heads,
        ],
        axis=-1,
    )


def unrotate(grads, cosines, sines):
    half_size = grads.shape[-1] // 2
    front_half = grads[..., :half_size]
    back_half = grads[..., half_size:]
    cos_heads = cosines[..., None, :]
    sin_heads = sines[..., None, :]
    return jnp.concatenate(
        [
            front_half * cos_heads + back_half * sin_heads,
            back_half * cos_heads - front_half * sin_heads,
        ],
        axis=-1,
    )


def rms_scale(values):
    return lax.rsqrt(jnp.mean(values * values, axis=-1, keepdims=True) + norm_eps)


def norm_backward(grad_normed, values, scale_rows, gain):
    scaled = grad_normed * gain
    gain_part = jnp.sum(grad_normed * values * scale_rows, axis=0)
    grad_values = scale_rows * scaled - values * scale_rows**3 * jnp.mean(
        scaled * values, axis=-1, keepdims=True
    )
    return (grad_values, gain_part)


def contract_rows(left, weight):
    return jnp.dot(
        left, lax.all_gather(weight, "fsdp", axis=0, tiled=True), preferred_element_type=jnp.float32
    )


def back_rows(grad, weight):
    return lax.dot_general(
        grad,
        lax.all_gather(weight, "fsdp", axis=0, tiled=True),
        (((1,), (1,)), ((), ())),
        preferred_element_type=jnp.float32,
    )


def forward_product(left, weight):
    return contract_rows(left, weight)


def backward_product(grad, weight):
    return back_rows(grad, weight)


def weight_grad(left, grad):
    return lax.psum_scatter(
        lax.dot_general(left, grad, (((0,), (0,)), ((), ())), preferred_element_type=jnp.float32),
        "fsdp",
        scatter_dimension=0,
        tiled=True,
    )


def allowed_pairs(segments):
    length = segments.shape[1]
    row_index = lax.broadcasted_iota(jnp.int32, (length, length), 0)
    col_index = lax.broadcasted_iota(jnp.int32, (length, length), 1)
    same_doc = segments[:, :, None] == segments[:, None, :]
    return ((row_index >= col_index)[None] & same_doc)[:, None, None]


def attention_scores(grouped, key_rows, segments):
    head_size = grouped.shape[-1]
    scores = jnp.einsum(
        "blgqd,bmgd->bgqlm", grouped, key_rows, preferred_element_type=jnp.float32
    ) * head_size ** (-0.5)
    return jnp.where(allowed_pairs(segments), scores, -1e30)


def group_heads(queries, kv_here):
    shards, length, heads, head_size = queries.shape
    return queries.reshape(shards, length, kv_here, heads // kv_here, head_size)


def attend_forward(queries, key_rows, value_rows, segments):
    grouped = group_heads(queries, key_rows.shape[2])
    scores = attention_scores(grouped, key_rows, segments)
    peak = jnp.max(scores, axis=-1, keepdims=True)
    log_total = peak + jnp.log(jnp.sum(jnp.exp(scores - peak), axis=-1, keepdims=True))
    probs = jnp.exp(scores - log_total).astype(jnp.bfloat16)
    attended = jnp.einsum(
        "bgqlm,bmgd->blgqd", probs, value_rows, preferred_element_type=jnp.float32
    )
    return (attended.reshape(queries.shape).astype(jnp.bfloat16), log_total)


def attend_backward(queries, key_rows, value_rows, segments, log_total, grad_out):
    kv_here = key_rows.shape[2]
    head_size = queries.shape[-1]
    grouped = group_heads(queries, kv_here)
    grad_grouped = group_heads(grad_out, kv_here)
    scores = attention_scores(grouped, key_rows, segments)
    probs = jnp.exp(scores - log_total)
    grad_probs = jnp.einsum(
        "blgqd,bmgd->bgqlm", grad_grouped, value_rows, preferred_element_type=jnp.float32
    )
    grad_values = jnp.einsum(
        "bgqlm,blgqd->bmgd",
        probs.astype(jnp.bfloat16),
        grad_grouped,
        preferred_element_type=jnp.float32,
    )
    balance = jnp.sum(probs * grad_probs, axis=-1, keepdims=True)
    grad_scores = (probs * (grad_probs - balance)).astype(jnp.bfloat16)
    factor = head_size ** (-0.5)
    grad_queries = (
        jnp.einsum("bgqlm,bmgd->blgqd", grad_scores, key_rows, preferred_element_type=jnp.float32)
        * factor
    )
    grad_keys = (
        jnp.einsum("bgqlm,blgqd->bmgd", grad_scores, grouped, preferred_element_type=jnp.float32)
        * factor
    )
    return (
        grad_queries.reshape(queries.shape).astype(jnp.bfloat16),
        grad_keys.astype(jnp.bfloat16),
        grad_values.astype(jnp.bfloat16),
    )


def body(
    inputs,
    positions,
    segments,
    gain_one,
    qkv_weight,
    qkv_bias,
    out_weight,
    gain_two,
    gate_up_weight,
    down_weight,
    cotangent,
):
    shards = inputs.shape[0]
    local_rows = inputs.shape[1]
    tokens = shards * local_rows
    query_width = HQ * HD
    key_width = KV * HD
    copies = max(1, lax.axis_size("seq") // KV)
    residual_in = inputs.reshape(tokens, D).astype(jnp.float32)
    cosines, sines = rope_angles(positions.reshape(tokens))
    scale_one = rms_scale(residual_in)
    normed = (residual_in * scale_one * gain_one).astype(jnp.bfloat16)
    projected = forward_product(normed, qkv_weight) + qkv_bias
    queries = projected[:, :query_width].reshape(tokens, HQ, HD)
    key_rows = projected[:, query_width : query_width + key_width].reshape(tokens, KV, HD)
    value_rows = projected[:, query_width + key_width :].reshape(tokens, KV, HD)
    queries = (
        rotate(queries, cosines, sines).astype(jnp.bfloat16).reshape(shards, local_rows, HQ, HD)
    )
    key_rows = (
        rotate(key_rows, cosines, sines).astype(jnp.bfloat16).reshape(shards, local_rows, KV, HD)
    )
    value_rows = value_rows.astype(jnp.bfloat16).reshape(shards, local_rows, KV, HD)
    head_queries, head_keys, head_values = (
        lax.all_to_all(queries, "seq", split_axis=2, concat_axis=1, tiled=True),
        lax.all_to_all(key_rows, "seq", split_axis=2, concat_axis=1, tiled=True),
        lax.all_to_all(value_rows, "seq", split_axis=2, concat_axis=1, tiled=True),
    )
    head_out, log_total = attend_forward(head_queries, head_keys, head_values, segments)
    token_out = lax.all_to_all(head_out, "seq", split_axis=1, concat_axis=2, tiled=True)
    attended = token_out.reshape(tokens, query_width)
    middle = residual_in + forward_product(attended, out_weight)
    scale_two = rms_scale(middle)
    normed_two = (middle * scale_two * gain_two).astype(jnp.bfloat16)
    gate_up = forward_product(normed_two, gate_up_weight)
    gate = gate_up[:, :FF]
    up_part = gate_up[:, FF:]
    sigmoid_gate = jax.nn.sigmoid(gate)
    silu_gate = gate * sigmoid_gate
    hidden = (silu_gate * up_part).astype(jnp.bfloat16)
    result = middle + forward_product(hidden, down_weight)
    output = result.astype(jnp.bfloat16).reshape(shards, local_rows, D)
    grad_rows = cotangent.reshape(tokens, D)
    grad_hidden = backward_product(grad_rows, down_weight)
    down_part = weight_grad(hidden, grad_rows)
    grad_gate = grad_hidden * up_part * sigmoid_gate * (1.0 + gate * (1.0 - sigmoid_gate))
    grad_up = grad_hidden * silu_gate
    grad_gate_up = jnp.concatenate([grad_gate, grad_up], axis=1).astype(jnp.bfloat16)
    grad_normed_two = backward_product(grad_gate_up, gate_up_weight)
    gate_up_part = weight_grad(normed_two, grad_gate_up)
    grad_norm_two, gain_two_part = norm_backward(grad_normed_two, middle, scale_two, gain_two)
    grad_middle = grad_rows.astype(jnp.float32) + grad_norm_two
    grad_branch = grad_middle.astype(jnp.bfloat16)
    grad_attended = backward_product(grad_branch, out_weight).astype(jnp.bfloat16)
    out_part = weight_grad(attended, grad_branch)
    grad_heads = lax.all_to_all(
        grad_attended.reshape(shards, local_rows, HQ, HD),
        "seq",
        split_axis=2,
        concat_axis=1,
        tiled=True,
    )
    grad_head_q, grad_head_k, grad_head_v = attend_backward(
        head_queries, head_keys, head_values, segments, log_total, grad_heads
    )
    grad_q, grad_k, grad_v = (
        lax.all_to_all(grad_head_q, "seq", split_axis=1, concat_axis=2, tiled=True),
        lax.all_to_all(grad_head_k, "seq", split_axis=1, concat_axis=2, tiled=True),
        lax.all_to_all(grad_head_v, "seq", split_axis=1, concat_axis=2, tiled=True),
    )
    grad_q = unrotate(grad_q.reshape(tokens, HQ, HD).astype(jnp.float32), cosines, sines).reshape(
        tokens, query_width
    )
    grad_k = jnp.sum(grad_k.astype(jnp.float32).reshape(tokens, KV, copies, HD), axis=2)
    grad_v = jnp.sum(grad_v.astype(jnp.float32).reshape(tokens, KV, copies, HD), axis=2)
    grad_k = unrotate(grad_k, cosines, sines).reshape(tokens, key_width)
    grad_v = grad_v.reshape(tokens, key_width)
    grad_projected = jnp.concatenate([grad_q, grad_k, grad_v], axis=1).astype(jnp.bfloat16)
    bias_part = jnp.sum(grad_projected.astype(jnp.float32), axis=0)
    grad_normed = backward_product(grad_projected, qkv_weight)
    qkv_part = weight_grad(normed, grad_projected)
    grad_norm_one, gain_one_part = norm_backward(grad_normed, residual_in, scale_one, gain_one)
    input_grad = (grad_middle + grad_norm_one).reshape(shards, local_rows, D)
    qkv_total, out_total, gate_up_total, down_total = lax.psum(
        (qkv_part, out_part, gate_up_part, down_part), "seq"
    )
    gain_one_total, bias_total, gain_two_total = lax.psum(
        (gain_one_part, bias_part, gain_two_part), ("seq", "fsdp")
    )
    return (
        output,
        input_grad,
        gain_one_total,
        qkv_total,
        bias_total,
        out_total,
        gain_two_total,
        gate_up_total,
        down_total,
    )


def solution(mesh):
    placed = (
        P("fsdp", "seq", None),
        P("fsdp", "seq"),
        P("fsdp", None),
        P(),
        P("fsdp", None),
        P(),
        P("fsdp", None),
        P(),
        P("fsdp", None),
        P("fsdp", None),
        P("fsdp", "seq", None),
    )
    return jax.shard_map(
        body,
        mesh=mesh,
        in_specs=placed,
        out_specs=(
            P("fsdp", "seq", None),
            P("fsdp", "seq", None),
            P(),
            P("fsdp", None),
            P(),
            P("fsdp", None),
            P(),
            P("fsdp", None),
            P("fsdp", None),
        ),
        check_vma=False,
    )
```

profile of v0, /device:TPU:0, one launch (start us, length us, event | category | flops | bytes accessed | tf_op | source)
XLA Modules:
  0.0 2638.4 jit_solution(10790584259065832357)
XLA Ops:
  11.3 63.6 %all-gather.5.cloned.1.call-done = bf16[1536,2048]{1,0:T(8,128)(2,1)} async-done(((bf16[96,2048]{1,0:T(8,128)(2,1)}), bf16[1536,2048]{1,0:T(8,128)(2,1)}) %all-gather.5.cloned.1.call-update) | async-done | bytes 6291472 | tf_op jit(solution)/shard_map/all_gather | solution.py:69
  74.9 3.8 convolution_add_fusion.2
  80.1 3.5 all-to-all-start.2
  84.6 6.3 all-to-all-done.2
  90.9 3.3 all-to-all-start.1
  95.2 3.0 all-to-all-done.1
  98.3 3.3 all-to-all-start
  102.3 3.4 all-to-all-done
  107.1 9.0 all_to_all.102
  116.4 12.7 all-gather.7.cloned.1.call-done
  129.1 3.2 multiply_reduce_fusion.2
  132.8 265.7 %all-gather.9.cloned.1.call-done = bf16[1536,17920]{1,0:T(8,128)(2,1)} async-done(((bf16[96,17920]{1,0:T(8,128)(2,1)}), bf16[1536,17920]{1,0:T(8,128)(2,1)}) %all-gather.9.cloned.1.call-update) | async-done | bytes 55050256 | tf_op jit(solution)/shard_map/all_gather | solution.py:69
  398.6 24.6 fusion.48
  423.2 116.6 %all-gather.11.cloned.1.call-done = bf16[8960,1536]{1,0:T(8,128)(2,1)} async-done(((bf16[560,1536]{1,0:T(8,128)(2,1)}), bf16[8960,1536]{1,0:T(8,128)(2,1)}) %all-gather.11.cloned.1.call-update) | async-done | bytes 27525136 | tf_op jit(solution)/shard_map/all_gather | solution.py:69
  539.7 18.5 multiply_convert_fusion.1
  558.3 26.0 multiply_reduce_fusion
  584.3 1.5 subtract_add_fusion
  585.8 6.4 fusion.38
  592.2 4.7 convolution_convert_fusion
  596.9 1.3 copy.104
  598.3 9.7 all_to_all.103
  608.2 1.5 fusion.5
  611.2 1.6 copy.118
  613.3 2.6 reduce.4
  615.9 1.5 reshape.445
  617.4 3.9 all-to-all-start.6
  621.3 2.0 fusion.15
  623.4 1.1 fusion.10
  628.2 3.3 all-to-all-start.7
  632.6 3.1 all-to-all-done.7
  635.7 3.5 all-to-all-start.5
  640.7 5.5 all-to-all-done.5
  648.1 6.4 fusion.41
  654.6 1.6 copy-done
  656.2 22.7 fusion.29
  679.5 42.4 %fusion.1 = f32[1536,17920]{1,0:T(8,128)} fusion(bf16[128,8960]{1,0:T(8,128)(2,1)} %get-tuple-element.21, bf16[128,8960]{1,0:T(8,128)(2,1)} %get-tuple-element.20, f32[128,1536]{1,0:T(8,128)S(1)} %get-tuple-element.44, f32[1536]{0:T(1024)S(1)} %copy-done.12, f32[128]{0:T(128)S(1)} %copy-done.24), kind=kOutput, calls=%fused_computation.6 | convolution fusion | flops 7056195584 | bytes 115481088 | tf_op jit(solution)/shard_map/dot_general | solution.py:92
  722.1 120.5 %reduce-scatter.5.cloned.1.call-done = f32[96,2048]{1,0:T(8,128)} async-done(((f32[1536,2048]{1,0:T(8,128)}), f32[96,2048]{1,0:T(8,128)}) %reduce-scatter.5.cloned.1.call-update) | async-done | bytes 786448 | tf_op jit(solution)/shard_map/reduce_scatter | solution.py:91
  842.5 510.4 %reduce-scatter.11.cloned.1.call-done = f32[560,1536]{1,0:T(8,128)} async-done(((f32[8960,1536]{1,0:T(8,128)}), f32[560,1536]{1,0:T(8,128)}) %reduce-scatter.11.cloned.1.call-update) | async-done | bytes 3440656 | tf_op jit(solution)/shard_map/reduce_scatter | solution.py:91
  1353.0 992.3 %reduce-scatter.9.cloned.1.call-done = f32[96,17920]{1,0:T(8,128)} async-done(((f32[1536,17920]{1,0:T(8,128)}), f32[96,17920]{1,0:T(8,128)}) %reduce-scatter.9.cloned.1.call-update) | async-done | bytes 6881296 | tf_op jit(solution)/shard_map/reduce_scatter | solution.py:91
  2345.4 13.1 fusion.4
  2358.7 5.2 fusion.28
  2363.9 39.5 %all-reduce = (f32[1536]{0:T(1024)}, f32[2048]{0:T(1024)}, f32[1536]{0:T(1024)}) all-reduce(f32[1536]{0:T(1024)S(1)} %get-tuple-element.11, f32[2048]{0:T(1024)S(1)} %convert_reduce_fusion, f32[1536]{0:T(1024)S(1)} %copy-done.28), channel_id=1, replica_groups=mesh['seq'=2,'fsdp'=16] {'seq','fsdp'}, use_global_device_ids=true, to_apply=%region_8.9 | all-reduce | flops 5120 | bytes 40960 | tf_op jit(solution)/shard_map/psum | solution.py:263
  2403.4 1.2 fusion.25
  2404.6 215.1 %all-reduce.4.cloned.1.call-done = (f32[96,2048]{1,0:T(8,128)}, f32[96,1536]{1,0:T(8,128)}, f32[96,17920]{1,0:T(8,128)}, f32[560,1536]{1,0:T(8,128)}) async-done(((f32[96,2048]{1,0:T(8,128)}, f32[96,1536]{1,0:T(8,128)}, f32[96,17920]{1,0:T(8,128)}, f32[560,1536]{1,0:T(8,128)}), (f32[96,2048]{1,0:T(8,128)}, f32[96,1536]{1,0:T(8,128)}, f32[96,17920]{1,0:T(8,128)}, ...) | async-done | bytes 11698192 | tf_op jit(solution)/shard_map/psum | solution.py:260
  2619.7 2.1 copy.155
  2621.8 1.9 copy.156
  2623.7 6.4 copy.157
  2630.1 1.8 copy.158
  (147 shorter events, 21.5 us)
Async XLA Ops:
  7.2 2.9 copy-start.34
  7.2 3.3 copy-start.3
  7.2 67.7 %copy-start.29 = (f32[2048]{0:T(1024)S(1)}, f32[2048]{0:T(1024)}, u32[]{:S(2)}) copy-start(f32[2048]{0:T(1024)} %param.16) | copy-start | bytes 24580
  7.2 67.7 %copy-start.25 = (f32[1536]{0:T(1024)S(1)}, f32[1536]{0:T(1024)}, u32[]{:S(2)}) copy-start(f32[1536]{0:T(1024)} %param.14) | copy-start | bytes 18436
  7.2 67.7 %all-gather.5.cloned.1.call-start = ((), (), s32[]{:S(2)}) async-start(), calls=%async_computation.12 | async-start | bytes 6684672 | tf_op jit(solution)/shard_map/all_gather | solution.py:69
  8.0 121.1 %all-gather.7.cloned.1.call-start = ((), (), s32[]{:S(2)}) async-start(), calls=%async_computation.13 | async-start | bytes 5013504 | tf_op jit(solution)/shard_map/all_gather | solution.py:69
  8.7 389.9 %all-gather.9.cloned.1.call-start = ((), (), s32[]{:S(2)}) async-start(), calls=%async_computation.14 | async-start | bytes 58490880 | tf_op jit(solution)/shard_map/all_gather | solution.py:69
  9.4 530.3 %all-gather.11.cloned.1.call-start = ((), (), s32[]{:S(2)}) async-start(), calls=%async_computation.15 | async-start | bytes 29245440 | tf_op jit(solution)/shard_map/all_gather | solution.py:69
  10.2 68.9 %copy-start.19 = (f32[128,64]{0,1:T(8,128)}, f32[128,64]{0,1:T(8,128)S(1)}, u32[]{:S(2)}) copy-start(f32[128,64]{0,1:T(8,128)S(1)} %get-tuple-element.35) | copy-start | bytes 98308
  10.3 68.9 %copy-start.21 = (f32[128,64]{0,1:T(8,128)}, f32[128,64]{0,1:T(8,128)S(1)}, u32[]{:S(2)}) copy-start(f32[128,64]{0,1:T(8,128)S(1)} %get-tuple-element.36) | copy-start | bytes 98308
  10.4 73.4 %copy-start.17 = (f32[128,64]{1,0:T(8,128)}, f32[128,64]{1,0:T(8,128)S(1)}, u32[]{:S(2)}) copy-start(f32[128,64]{1,0:T(8,128)S(1)} %copy.94) | copy-start | bytes 98308
  10.5 73.3 %copy-start.18 = (f32[128,64]{1,0:T(8,128)}, f32[128,64]{1,0:T(8,128)S(1)}, u32[]{:S(2)}) copy-start(f32[128,64]{1,0:T(8,128)S(1)} %copy.92) | copy-start | bytes 98308
  11.3 63.7 %copy-start.30 = (f32[128]{0:T(128)}, f32[128]{0:T(128)S(1)}, u32[]{:S(2)}) copy-start(f32[128]{0:T(128)S(1)} %get-tuple-element.38) | copy-start | bytes 1540
  78.7 15.4 copy-start.32
  80.1 10.7 all-to-all-start.2
  90.9 7.4 all-to-all-start.1
  95.2 21.1 copy-start.5
  98.3 7.4 copy-start.16
  98.3 7.4 all-to-all-start
  101.6 620.5 %reduce-scatter.7.cloned.1.call-start = ((), (), s32[]{:S(2)}) async-start(), calls=%async_computation.17 | async-start | bytes 10027008 | tf_op jit(solution)/shard_map/reduce_scatter | solution.py:91
  107.1 291.5 %copy-start.12 = (f32[1536]{0:T(1024)S(1)}, f32[1536]{0:T(1024)}, u32[]{:S(2)}) copy-start(f32[1536]{0:T(1024)} %param.18) | copy-start | bytes 18436
  116.4 306.8 %copy-start.4 = (bf16[1,128,2,6,128]{1,4,3,2,0:T(8,128)(2,1)}, bf16[1,128,2,6,128]{1,4,3,2,0:T(8,128)(2,1)S(1)}, u32[]{:S(2)}) copy-start(bf16[1,128,2,6,128]{1,4,3,2,0:T(8,128)(2,1)S(1)} %copy.103) | copy-start | bytes 1179652
  398.6 141.2 %copy-start.11 = (bf16[1,128,1536]{2,1,0:T(8,128)(2,1)S(1)}, bf16[1,128,1536]{2,1,0:T(8,128)(2,1)}, u32[]{:S(2)}) copy-start(bf16[1,128,1536]{2,1,0:T(8,128)(2,1)} %param.21) | copy-start | bytes 1179652
  539.7 18.5 copy-start.23
  585.8 6.4 copy-start.1
  608.2 2.0 copy-start.6
  608.2 1.5 copy-start.7
  617.4 10.9 all-to-all-start.6
  628.2 7.4 all-to-all-start.7
  635.7 10.5 all-to-all-start.5
  639.2 203.4 %reduce-scatter.5.cloned.1.call-start = ((), (), s32[]{:S(2)}) async-start(), calls=%async_computation.16 | async-start | bytes 13369344 | tf_op jit(solution)/shard_map/reduce_scatter | solution.py:91
  640.6 6.8 copy-start.14
  640.6 6.6 copy-start.20
  640.7 6.6 copy-start.22
  646.3 1.8 copy-start.26
  646.3 1.8 copy-start.31
  647.4 0.7 copy-start.8
  654.5 1.6 copy-start
  654.6 698.4 %reduce-scatter.11.cloned.1.call-start = ((), (), s32[]{:S(2)}) async-start(), calls=%async_computation.19 | async-start | bytes 58490880 | tf_op jit(solution)/shard_map/reduce_scatter | solution.py:91
  678.9 1666.4 %reduce-scatter.9.cloned.1.call-start = ((), (), s32[]{:S(2)}) async-start(), calls=%async_computation.18 | async-start | bytes 116981760 | tf_op jit(solution)/shard_map/reduce_scatter | solution.py:91
  722.0 1897.7 %all-reduce.4.cloned.1.call-start = ((), (), s32[]{:S(2)}) async-start(), calls=%async_computation.20 | async-start | bytes 23396352 | tf_op jit(solution)/shard_map/psum | solution.py:260
  2345.4 13.1 copy-start.9
  2345.4 13.1 copy-start.15
  2345.4 13.3 copy-start.27
  2358.5 5.4 copy-start.28
  2358.5 45.0 %copy-start.2 = (f32[128,1536]{1,0:T(8,128)S(1)}, f32[128,1536]{1,0:T(8,128)}, u32[]{:S(2)}) copy-start(f32[128,1536]{1,0:T(8,128)} %copy-done.1) | copy-start | bytes 2359300
  2358.5 45.0 %copy-start.33 = (f32[128]{0:T(128)S(1)}, f32[128]{0:T(128)}, u32[]{:S(2)}) copy-start(f32[128]{0:T(128)} %get-tuple-element.37) | copy-start | bytes 1540
  2623.7 6.4 copy-start.10
  (2 other events, 1.3 us)
Sparse Core Ops, SparseCore 0:
  10.3 64.5 all-gather.4
  77.2 51.8 all-gather.6
  130.7 267.8 all-gather.8
  400.0 139.6 all-gather.10
  592.3 111.3 reduce-scatter.6
  708.1 134.3 reduce-scatter.4
  847.4 505.5 reduce-scatter.10
  1357.2 988.0 reduce-scatter.8
  2348.2 271.4 all-reduce.3
where the time goes:
time: 2640 us
  waiting for transfers between devices  2320 us (88%)
  matrix products  183 us (7%)
  blocking collectives  58.2 us (2%)
  local copies, waits for them, and re-layouts  27.9 us (1%)
    reduce_scatter x4, waiting for transfers between devices, weight_grad(): lax.psum_scatter(lax.dot_general(left, grad, (((0,), (0,)), ((), ())), pr...  1620 us
    all_gather x4, waiting for transfers between devices, contract_rows(): lax.all_gather(weight, 'fsdp', axis=0, tiled=True)  459 us
    psum x1, waiting for transfers between devices, body(): lax.psum((qkv_part, out_part, gate_up_part, down_part), 'seq')  215 us
    dot_general x4, matrix products, weight_grad(): lax.dot_general(left, grad, (((0,), (0,)), ((), ())), preferred_element_t...  77.9 us
    dot_general x4, matrix products, back_rows(): lax.dot_general(grad, lax.all_gather(weight, 'fsdp', axis=0, tiled=True),...  54.4 us
  transfers between devices with their start and end apart: 15, of which 13 were waited for; matrix products, arithmetic and copies ran while one was open for 6% of the time, Pallas kernels for 0%

commit v1 on v0

v1 whole, which is shorter than its diff:
```python
import functools

import jax
import jax.numpy as jnp
from jax import lax
from jax.experimental import pallas as pl
from jax.experimental.pallas import tpu as pltpu
from jax.sharding import PartitionSpec as P

D = 1536
FF = 8960
HQ = 12
KV = 2
HD = 128
GROUP = HQ // KV
QW = HQ * HD
KW = KV * HD

rope_base = 1000000.0
norm_eps = 1e-06
bf16 = jnp.bfloat16
f32 = jnp.float32


def flip(value, k):
    size = lax.axis_size("fsdp")
    return lax.ppermute(value, "fsdp", [(i, i ^ k) for i in range(size)])


def swap(value):
    return lax.ppermute(value, "seq", [(0, 1), (1, 0)])


def add(left, right):
    return left.astype(f32) + right.astype(f32)


def dot(left, right):
    return jnp.dot(left, right, preferred_element_type=f32)


def dot_t(left, right):
    return lax.dot_general(left, right, (((1,), (1,)), ((), ())), preferred_element_type=f32)


def t_dot(left, right):
    return lax.dot_general(left, right, (((0,), (0,)), ((), ())), preferred_element_type=f32)


def gather_tokens(rows):
    blocks = []
    for dz in range(lax.axis_size("fsdp") // 4):
        own = flip(rows, 4 * dz) if dz else rows
        pair = jnp.concatenate([own, flip(own, 2)], axis=0)
        blocks.append(jnp.concatenate([pair, flip(pair, 1)], axis=0))
    return blocks


def scatter_tokens(near, far, dz):
    tokens = near.shape[0] // 2
    both = add(near, flip(far, 1))
    mine = add(both[:tokens], flip(both[tokens:].astype(bf16), 2))
    return flip(mine.astype(bf16), 4 * dz) if dz else mine


def place_kernel(count, where, *refs):
    out = refs[-1]
    at = 0
    for ref in refs[:-1]:
        for i in range(ref.shape[0]):
            out[where[at]] = ref[i]
            at += 1


def place_blocks(pieces, where):
    count = sum(p.shape[0] for p in pieces)
    shape = (count,) + pieces[0].shape[1:]
    return pl.pallas_call(
        functools.partial(place_kernel, count),
        out_shape=jax.ShapeDtypeStruct(shape, pieces[0].dtype),
        in_specs=[pl.BlockSpec(memory_space=pltpu.SMEM)]
        + [pl.BlockSpec(memory_space=pltpu.VMEM)] * len(pieces),
        out_specs=pl.BlockSpec(memory_space=pltpu.VMEM),
        compiler_params=pltpu.CompilerParams(vmem_limit_bytes=40 * 1024 * 1024),
    )(where, *pieces)


def gather_weight(shard, me, s):
    size = lax.axis_size("fsdp")
    half = shard.shape[0] // 2
    own = lax.dynamic_slice_in_dim(shard, s * half, half, axis=0)
    pieces, where = [], []
    for dz in range(size // 4):
        first = flip(own, 4 * dz) if dz else own
        pair = jnp.stack([first, flip(first, 2)])
        four = jnp.concatenate([pair, swap(pair)], axis=0)
        pieces += [four, flip(four, 1)]
        for dc in range(2):
            for h in range(2):
                for dx in range(2):
                    where.append((me ^ (4 * dz + 2 * dx + dc)) * 2 + (s ^ h))
    placed = place_blocks(pieces, jnp.stack(where).astype(jnp.int32))
    return placed.reshape(size * 2 * half, shard.shape[1])


def scatter_weight(left, right, me, s):
    size = lax.axis_size("fsdp")
    steps = size // 4
    width = left.shape[1]
    half = width // size // 2
    turned = left.T.reshape(size * 2, half, left.shape[0])
    where = []
    for place in range(size):
        for h in range(2):
            k = me ^ place
            dz, dx, dc = k // 4, (k // 2) % 2, k % 2
            where.append(((dc * 2 + dx) * 2 + (s ^ h)) * steps + dz)
    turned = place_blocks([turned], jnp.stack(where).astype(jnp.int32)).reshape(
        2, width // 2, left.shape[0]
    )
    far = flip(dot(turned[1], right).astype(bf16), 1)
    total = add(dot(turned[0], right), far)
    quarter = width // 4
    total = add(total[:quarter], flip(total[quarter:].astype(bf16), 2))
    eighth = width // 8
    total = add(total[:eighth], swap(total[eighth:].astype(bf16)))
    mine = total[:half]
    for dz in range(1, steps):
        mine = add(mine, flip(total[dz * half : (dz + 1) * half].astype(bf16), 4 * dz))
    return join_halves(mine.astype(bf16), s)


def join_halves(mine, s):
    other = swap(mine)
    low = jnp.where(s == 0, mine, other)
    high = jnp.where(s == 0, other, mine)
    return jnp.concatenate([low, high], axis=0).astype(f32)


def sum_everywhere(value):
    bit = 1
    while bit < lax.axis_size("fsdp"):
        value = value + flip(value, bit)
        bit *= 2
    return value + swap(value)


def rope_angles(positions):
    steps_half = jnp.arange(HD // 2, dtype=f32)
    inverse = rope_base ** (-2.0 * steps_half / HD)
    angles = positions.astype(f32)[..., None] * inverse
    return (jnp.cos(angles), jnp.sin(angles))


def rotate(values, cosines, sines):
    half_size = values.shape[-1] // 2
    front_half = values[..., :half_size]
    back_half = values[..., half_size:]
    cos_heads = cosines[..., None, :]
    sin_heads = sines[..., None, :]
    return jnp.concatenate(
        [
            front_half * cos_heads - back_half * sin_heads,
            back_half * cos_heads + front_half * sin_heads,
        ],
        axis=-1,
    )


def rms_scale(values):
    return lax.rsqrt(jnp.mean(values * values, axis=-1, keepdims=True) + norm_eps)


def norm_backward(grad_normed, values, scale_rows, gain):
    scaled = grad_normed * gain
    gain_part = jnp.sum(grad_normed * values * scale_rows, axis=0)
    grad_values = scale_rows * scaled - values * scale_rows**3 * jnp.mean(
        scaled * values, axis=-1, keepdims=True
    )
    return (grad_values, gain_part)


def attention_probs(queries, keys, allowed):
    tokens = queries.shape[0]
    grouped = queries.reshape(tokens, KV, GROUP, HD)
    scores = jnp.einsum("tgqd,sgd->gqts", grouped, keys, preferred_element_type=f32) * HD ** (-0.5)
    scores = jnp.where(allowed, scores, -1e30)
    peak = jnp.max(scores, axis=-1, keepdims=True)
    weights = jnp.exp(scores - peak)
    return weights / jnp.sum(weights, axis=-1, keepdims=True)


def attend_forward(probs, values):
    tokens = probs.shape[2]
    out = jnp.einsum("gqts,sgd->tgqd", probs.astype(bf16), values, preferred_element_type=f32)
    return out.reshape(tokens, QW).astype(bf16)


def attend_backward(queries, keys, values, probs, grad_out):
    tokens = queries.shape[0]
    grouped = queries.reshape(tokens, KV, GROUP, HD)
    grad_grouped = grad_out.reshape(tokens, KV, GROUP, HD)
    grad_probs = jnp.einsum("tgqd,sgd->gqts", grad_grouped, values, preferred_element_type=f32)
    grad_values = jnp.einsum(
        "gqts,tgqd->sgd", probs.astype(bf16), grad_grouped, preferred_element_type=f32
    )
    balance = jnp.sum(probs * grad_probs, axis=-1, keepdims=True)
    grad_scores = (probs * (grad_probs - balance)).astype(bf16)
    factor = HD ** (-0.5)
    grad_queries = (
        jnp.einsum("gqts,sgd->tgqd", grad_scores, keys, preferred_element_type=f32) * factor
    )
    grad_keys = (
        jnp.einsum("gqts,tgqd->sgd", grad_scores, grouped, preferred_element_type=f32) * factor
    )
    return (grad_queries.reshape(tokens, HQ, HD), grad_keys, grad_values)


def shuffle_gate_up(shard, me, s):
    size = lax.axis_size("fsdp")
    half = shard.shape[0] // 2
    unit = FF // size
    own = lax.dynamic_slice_in_dim(shard, s * half, half, axis=0)
    blocks = jnp.transpose(own.reshape(half, 2, size, unit), (2, 0, 1, 3)).reshape(
        size, half, 2 * unit
    )
    pieces = [lax.dynamic_index_in_dim(blocks, me, 0)]
    where = [me]
    for k in range(1, size):
        pieces.append(flip(lax.dynamic_index_in_dim(blocks, me ^ k, 0), k))
        where.append(me ^ k)
    mine = place_blocks(pieces, jnp.stack(where).astype(jnp.int32))
    other = swap(mine)
    low = jnp.where(s == 0, mine, other)
    high = jnp.where(s == 0, other, mine)
    whole = jnp.stack([low, high], axis=1).reshape(size * 2 * half, 2, unit)
    padded = -(-unit // 128) * 128
    whole = jnp.pad(whole, ((0, 0), (0, 0), (0, padded - unit)))
    return whole.reshape(size * 2 * half, 2 * padded)


def unshuffle_gate_up(grad, me, s):
    size = lax.axis_size("fsdp")
    unit = FF // size
    padded = grad.shape[1] // 2
    half = grad.shape[0] // size // 2
    grad = jnp.concatenate([grad[:, :unit], grad[:, padded : padded + unit]], axis=1)
    parts = grad.reshape(size, 2, half, 2 * unit)
    keep = lax.dynamic_index_in_dim(parts, s, 1, keepdims=False)
    give = lax.dynamic_index_in_dim(parts, 1 - s, 1, keepdims=False).astype(bf16)
    total = add(keep, swap(give)).astype(bf16)
    pieces = [lax.dynamic_index_in_dim(total, me, 0)]
    where = [me]
    for k in range(1, size):
        pieces.append(flip(lax.dynamic_index_in_dim(total, me ^ k, 0), k))
        where.append(me ^ k)
    mine = place_blocks(pieces, jnp.stack(where).astype(jnp.int32))
    mine = jnp.transpose(mine.reshape(size, half, 2, unit), (1, 2, 0, 3)).reshape(half, 2 * FF)
    return join_halves(mine, s)


def body(
    inputs,
    positions,
    segments,
    gain_one,
    qkv_weight,
    qkv_bias,
    out_weight,
    gain_two,
    gate_up_weight,
    down_weight,
    cotangent,
):
    tokens = inputs.shape[0] * inputs.shape[1]
    size = lax.axis_size("fsdp")
    steps = size // 4
    me = lax.axis_index("fsdp")
    s = lax.axis_index("seq")
    unit = FF // size
    padded = -(-unit // 128) * 128

    qkv_full = gather_weight(qkv_weight, me, s)
    out_full = gather_weight(out_weight, me, s)
    gate_up_full = shuffle_gate_up(gate_up_weight, me, s)
    down_full = jnp.pad(down_weight, ((0, padded - unit), (0, 0)))
    grad_rows = cotangent.reshape(tokens, D)
    cot_blocks = gather_tokens(grad_rows)

    residual_in = inputs.reshape(tokens, D).astype(f32)
    cosines, sines = rope_angles(positions.reshape(tokens))
    scale_one = rms_scale(residual_in)
    normed = (residual_in * scale_one * gain_one).astype(bf16)
    projected = dot(normed, qkv_full) + qkv_bias
    queries = rotate(projected[:, :QW].reshape(tokens, HQ, HD), cosines, sines).astype(bf16)
    key_rows = rotate(projected[:, QW : QW + KW].reshape(tokens, KV, HD), cosines, sines)
    mine_kv = jnp.concatenate(
        [key_rows.astype(bf16).reshape(tokens, KW), projected[:, QW + KW :].astype(bf16)], axis=1
    )
    all_kv = jnp.concatenate([mine_kv, swap(mine_kv)], axis=0)
    keys = all_kv[:, :KW].reshape(2 * tokens, KV, HD)
    values = all_kv[:, KW:].reshape(2 * tokens, KV, HD)
    ids = segments.reshape(2, tokens)
    mine_ids = lax.dynamic_index_in_dim(ids, s, 0, keepdims=False)
    other_ids = lax.dynamic_index_in_dim(ids, 1 - s, 0, keepdims=False)
    row_index = lax.broadcasted_iota(jnp.int32, (tokens, tokens), 0)
    col_index = lax.broadcasted_iota(jnp.int32, (tokens, tokens), 1)
    near = (mine_ids[:, None] == mine_ids[None, :]) & (row_index >= col_index)
    far = (mine_ids[:, None] == other_ids[None, :]) & (s == 1)
    allowed = jnp.concatenate([near, far], axis=1)[None, None]
    probs = attention_probs(queries, keys, allowed)
    attended = attend_forward(probs, values)
    middle = residual_in + dot(attended, out_full)
    scale_two = rms_scale(middle)
    normed_two = (middle * scale_two * gain_two).astype(bf16)

    token_blocks = gather_tokens(normed_two)
    hidden_blocks, grad_blocks = [], []
    back_total, out_total = [], []
    for dz in range(steps):
        gate_up = dot(token_blocks[dz], gate_up_full)
        gate, up_part = gate_up[:, :padded], gate_up[:, padded:]
        sigmoid_gate = jax.nn.sigmoid(gate)
        silu_gate = gate * sigmoid_gate
        hidden = (silu_gate * up_part).astype(bf16)
        grad_hidden = dot_t(cot_blocks[dz], down_full)
        grad_gate = grad_hidden * up_part * sigmoid_gate * (1.0 + gate * (1.0 - sigmoid_gate))
        grad_up = grad_hidden * silu_gate
        grad_gate_up = jnp.concatenate([grad_gate, grad_up], axis=1).astype(bf16)
        hidden_blocks.append(hidden)
        grad_blocks.append(grad_gate_up)
        low = 2 * tokens
        back_far = dot_t(grad_gate_up[low:], gate_up_full).astype(bf16)
        back_near = dot_t(grad_gate_up[:low], gate_up_full)
        back_total.append(scatter_tokens(back_near, back_far, dz))
        out_far = dot(hidden[low:], down_full).astype(bf16)
        out_near = dot(hidden[:low], down_full)
        out_total.append(scatter_tokens(out_near, out_far, dz))
    grad_normed_two = functools.reduce(add, back_total)
    result = middle + functools.reduce(add, out_total)
    output = result.astype(bf16).reshape(inputs.shape)

    hidden_all = jnp.concatenate(hidden_blocks, axis=0)
    grad_all = jnp.concatenate(grad_blocks, axis=0)
    cot_all = jnp.concatenate(cot_blocks, axis=0)
    tokens_all = jnp.concatenate(token_blocks, axis=0)
    gate_up_part = t_dot(tokens_all, grad_all)
    down_part = t_dot(hidden_all, cot_all)[:unit].astype(bf16)
    gate_up_total = unshuffle_gate_up(gate_up_part, me, s)
    down_total = add(down_part, swap(down_part))

    grad_norm_two, gain_two_part = norm_backward(grad_normed_two, middle, scale_two, gain_two)
    grad_middle = grad_rows.astype(f32) + grad_norm_two
    grad_branch = grad_middle.astype(bf16)
    grad_attended = dot_t(grad_branch, out_full).astype(bf16)
    out_weight_total = scatter_weight(attended, grad_branch, me, s)
    grad_q, grad_k, grad_v = attend_backward(queries, keys, values, probs, grad_attended)
    give = jnp.concatenate(
        [grad_k[tokens:].reshape(tokens, KW), grad_v[tokens:].reshape(tokens, KW)], axis=1
    )
    keep = jnp.concatenate(
        [grad_k[:tokens].reshape(tokens, KW), grad_v[:tokens].reshape(tokens, KW)], axis=1
    )
    grad_kv = add(keep, swap(give.astype(bf16))).astype(bf16)
    grad_q = rotate(grad_q.astype(bf16).astype(f32), cosines, -sines).reshape(tokens, QW)
    grad_k = rotate(
        grad_kv[:, :KW].astype(f32).reshape(tokens, KV, HD), cosines, -sines
    ).reshape(tokens, KW)
    grad_projected = jnp.concatenate(
        [grad_q.astype(bf16), grad_k.astype(bf16), grad_kv[:, KW:]], axis=1
    )
    bias_part = jnp.sum(grad_projected.astype(f32), axis=0)
    grad_normed = dot_t(grad_projected, qkv_full)
    qkv_weight_total = scatter_weight(normed, grad_projected, me, s)
    grad_norm_one, gain_one_part = norm_backward(grad_normed, residual_in, scale_one, gain_one)
    input_grad = (grad_middle + grad_norm_one).reshape(inputs.shape)
    sums = sum_everywhere(jnp.concatenate([gain_one_part, bias_part, gain_two_part]))
    width = bias_part.shape[0]
    return (
        output,
        input_grad,
        sums[:D],
        qkv_weight_total,
        sums[D : D + width],
        out_weight_total,
        sums[D + width :],
        gate_up_total,
        down_total,
    )


def solution(mesh):
    placed = (
        P("fsdp", "seq", None),
        P("fsdp", "seq"),
        P("fsdp", None),
        P(),
        P("fsdp", None),
        P(),
        P("fsdp", None),
        P(),
        P("fsdp", None),
        P("fsdp", None),
        P("fsdp", "seq", None),
    )
    return jax.shard_map(
        body,
        mesh=mesh,
        in_specs=placed,
        out_specs=(
            P("fsdp", "seq", None),
            P("fsdp", "seq", None),
            P(),
            P("fsdp", None),
            P(),
            P("fsdp", None),
            P(),
            P("fsdp", None),
            P("fsdp", None),
        ),
        check_vma=False,
    )
```

time: 2640 us -> 749 us (0.28)
  waiting for transfers between devices: 2320 us -> 358 us
  starting transfers between devices: 21.4 us -> 141 us
  matrix products: 183 us -> 100 us
  local copies, waits for them, and re-layouts: 27.9 us -> 99.6 us
  blocking collectives: 58.2 us -> 0 us
    reduce_scatter x4 -> x0, waiting for transfers between devices: 1620 us -> none  [weight_grad(): lax.psum_scatter(lax.dot_general(left, grad, (((0,), (0,)), ((), ())), pr...]
    all_gather x4 -> x0, waiting for transfers between devices: 459 us -> none  [contract_rows(): lax.all_gather(weight, 'fsdp', axis=0, tiled=True)]
    ppermute x0 -> x129, waiting for transfers between devices: none -> 358 us  [the longest x110 256 us: flip(): return lax.ppermute(value, 'fsdp', [(i, i ^ k) for i in range(size)])]
    psum x1 -> x0, waiting for transfers between devices: 215 us -> none  [body(): lax.psum((qkv_part, out_part, gate_up_part, down_part), 'seq')]
    ppermute x0 -> x129, starting transfers between devices: none -> 141 us  [the longest x110 120 us: flip(): return lax.ppermute(value, 'fsdp', [(i, i ^ k) for i in range(size)])]
    dot_general x18 -> x39, matrix products: 183 us -> 98.1 us  [the longest x14 35.9 us: dot_t(): lax.dot_general(left, right, (((1,), (1,)), ((), ())), preferred_element_...]
    psum x1 -> x0, blocking collectives: 39.5 us -> none  [body(): lax.psum((gain_one_part, bias_part, gain_two_part), ('seq', 'fsdp'))]
  transfers between devices with their start and end apart: 15 -> 129, of which waited for: 13 -> 52; matrix products, arithmetic and copies ran while one was open for 6% -> 28% of each run, Pallas kernels for 0% -> 1%
where the time goes in v1:
time: 749 us; the launch traced here: 744 us
  waiting for transfers between devices  358 us (48%)
  starting transfers between devices  141 us (19%)
  matrix products  100 us (13%)
  local copies, waits for them, and re-layouts  99.6 us (13%)
  other arithmetic  36.5 us (5%)
    ppermute x110, waiting for transfers between devices, flip(): return lax.ppermute(value, 'fsdp', [(i, i ^ k) for i in range(size)])  256 us
    ppermute x110, starting transfers between devices, flip(): return lax.ppermute(value, 'fsdp', [(i, i ^ k) for i in range(size)])  120 us
    ppermute x19, waiting for transfers between devices, swap(): return lax.ppermute(value, 'seq', [(0, 1), (1, 0)])  102 us
    dot_general x14, matrix products, dot_t(): lax.dot_general(left, right, (((1,), (1,)), ((), ())), preferred_element_...  35.9 us
    dot_general x18, matrix products, dot(): return jnp.dot(left, right, preferred_element_type=f32)  34.8 us
    unnamed x259, local copies, waits for them, and re-layouts  26.3 us
    dot_general x2, matrix products, t_dot(): lax.dot_general(left, right, (((0,), (0,)), ((), ())), preferred_element_...  23.1 us
    ppermute x19, starting transfers between devices, swap(): return lax.ppermute(value, 'seq', [(0, 1), (1, 0)])  21.4 us
  transfers between devices with their start and end apart: 129, of which 52 were waited for; matrix products, arithmetic and copies ran while one was open for 28% of the time, Pallas kernels for 1%

profile of v1, /device:TPU:0, one launch (start us, length us, event | category | flops | bytes accessed | tf_op | source)
XLA Modules:
  0.0 744.4 jit_solution(8286725849253542428)
XLA Ops:
  3.9 4.4 reshape.280
  11.1 4.2 reshape.281
  43.6 6.9 collective-permute-start.44
  59.0 4.8 collective-permute-start.47
  69.0 5.0 collective-permute-start.7
  79.0 8.4 %collective-permute-done.19 = bf16[48,1536]{1,0:T(8,128)(2,1)S(1)} collective-permute-done((bf16[48,1536]{1,0:T(8,128)(2,1)}, bf16[48,1536]{1,0:T(8,128)(2,1)S(1)}, u32[]{:S(2)}, u32[]{:S(2)}) %collective-permute-start.19) | collective-permute-done | bytes 147488 | tf_op jit(solution)/shard_map/ppermute | solution.py:27
  90.9 6.6 collective-permute-done.23
  106.8 10.4 %collective-permute-done.28 = bf16[48,1536]{1,0:T(8,128)(2,1)S(1)} collective-permute-done((bf16[48,1536]{1,0:T(8,128)(2,1)S(1)}, bf16[48,1536]{1,0:T(8,128)(2,1)S(1)}, u32[]{:S(2)}, u32[]{:S(2)}) %collective-permute-start.28) | collective-permute-done | bytes 147488 | tf_op jit(solution)/shard_map/ppermute | solution.py:27
  128.7 4.3 collective-permute-done.8
  141.8 8.9 %collective-permute-done.1 = bf16[2,48,2048]{2,1,0:T(8,128)(2,1)S(1)} collective-permute-done((bf16[2,48,2048]{2,1,0:T(8,128)(2,1)S(1)}, bf16[2,48,2048]{2,1,0:T(8,128)(2,1)S(1)}, u32[]{:S(2)}, u32[]{:S(2)}) %collective-permute-start.1) | collective-permute-done | bytes 393248 | tf_op jit(solution)/shard_map/ppermute | solution.py:31
  152.7 4.3 collective-permute-done.21
  159.0 4.4 collective-permute-done.25
  165.3 4.4 collective-permute-done.29
  173.9 4.2 collective-permute-done.5
  179.7 4.7 collective-permute-done.9
  218.1 23.1 %collective-permute-done.15 = bf16[128,512]{1,0:T(8,128)(2,1)} collective-permute-done((bf16[128,512]{1,0:T(8,128)(2,1)S(1)}, bf16[128,512]{1,0:T(8,128)(2,1)}, u32[]{:S(2)}, u32[]{:S(2)}) %collective-permute-start.15) | collective-permute-done | bytes 131104 | tf_op jit(solution)/shard_map/ppermute | solution.py:31
  262.8 9.4 %reshape.282 = bf16[1536,2,560]{2,1,0:T(2,128)(2,1)} reshape(bf16[16,2,48,1120]{3,2,1,0:T(8,128)(2,1)} %copy.48) | data formatting | bytes 6881280 | tf_op jit(solution)/shard_map/reshape | solution.py:236
  272.2 6.5 pad.8
  282.1 6.5 collective-permute-done.57
  291.9 8.8 %collective-permute-done.58 = bf16[128,1536]{1,0:T(8,128)(2,1)S(1)} collective-permute-done((bf16[128,1536]{1,0:T(8,128)(2,1)S(1)}, bf16[128,1536]{1,0:T(8,128)(2,1)S(1)}, u32[]{:S(2)}, u32[]{:S(2)}) %collective-permute-start.58) | collective-permute-done | bytes 393248 | tf_op jit(solution)/shard_map/ppermute | solution.py:27
  300.8 7.3 collective-permute-done.52
  347.5 15.2 %fusion.1 = f32[1536,1280]{0,1:T(8,128)} fusion(bf16[2048,1536]{1,0:T(8,128)(2,1)S(1)} %constant_dynamic-update-slice_fusion, bf16[512,640]{1,0:T(8,128)(2,1)} %copy-done.103, bf16[512,640]{1,0:T(8,128)(2,1)} %copy-done.101, bf16[512,640]{1,0:T(8,128)(2,1)} %copy-done.111, bf16[512,640]{1,0:T(8,128)(2,1)} %copy-done.109, bf16[512,640]{1,0:T(8,128)(2,1)} %copy-done.107, ...), kind=kOutput, calls=%fused_computation.3 | convolution fusion | flops 8095006720 | bytes 19398656 | tf_op jit(solution)/shard_map/dot_general | solution.py:47
  369.7 8.2 %copy.62 = f32[1536,1120]{1,0:T(8,128)} copy(f32[1536,1120]{0,1:T(8,128)} %pad_maximum_fusion) | data formatting | bytes 13762560 | tf_op jit(solution)/shard_map/concatenate | solution.py:247
  377.9 7.9 %fusion.18 = bf16[640,1536]{1,0:T(8,128)(2,1)S(1)} fusion(bf16[2048,1536]{1,0:T(8,128)(2,1)} %constant_dynamic-update-slice_fusion.12, bf16[512,640]{1,0:T(8,128)(2,1)} %get-tuple-element.37, bf16[512,640]{1,0:T(8,128)(2,1)} %copy-done.72, bf16[512,640]{1,0:T(8,128)(2,1)} %get-tuple-element.35, bf16[512,640]{1,0:T(8,128)(2,1)} %copy-done.76), kind=kOutput, calls=%fused_computation.31 | convolution fusion | flops 4037017600 | bytes 10878976 | tf_op jit(solution)/shard_map/dot_general | solution.py:47
  415.4 11.1 %collective-permute-done.89 = bf16[128,1536]{1,0:T(8,128)(2,1)S(1)} collective-permute-done((bf16[128,1536]{1,0:T(8,128)(2,1)S(1)}, bf16[128,1536]{1,0:T(8,128)(2,1)S(1)}, u32[]{:S(2)}, u32[]{:S(2)}) %collective-permute-start.89) | collective-permute-done | bytes 393248 | tf_op jit(solution)/shard_map/ppermute | solution.py:27
  427.4 7.6 %collective-permute-done.83 = bf16[128,1536]{1,0:T(8,128)(2,1)S(1)} collective-permute-done((bf16[128,1536]{1,0:T(8,128)(2,1)S(1)}, bf16[128,1536]{1,0:T(8,128)(2,1)S(1)}, u32[]{:S(2)}, u32[]{:S(2)}) %collective-permute-start.83) | collective-permute-done | bytes 393248 | tf_op jit(solution)/shard_map/ppermute | solution.py:27
  435.8 7.5 %collective-permute-done.77 = bf16[128,1536]{1,0:T(8,128)(2,1)S(1)} collective-permute-done((bf16[128,1536]{1,0:T(8,128)(2,1)S(1)}, bf16[128,1536]{1,0:T(8,128)(2,1)S(1)}, u32[]{:S(2)}, u32[]{:S(2)}) %collective-permute-start.77) | collective-permute-done | bytes 393248 | tf_op jit(solution)/shard_map/ppermute | solution.py:27
  444.3 7.5 %collective-permute-done.67 = bf16[128,1536]{1,0:T(8,128)(2,1)S(1)} collective-permute-done((bf16[128,1536]{1,0:T(8,128)(2,1)S(1)}, bf16[128,1536]{1,0:T(8,128)(2,1)S(1)}, u32[]{:S(2)}, u32[]{:S(2)}) %collective-permute-start.67) | collective-permute-done | bytes 393248 | tf_op jit(solution)/shard_map/ppermute | solution.py:27
  453.2 7.0 collective-permute-done.61
  460.9 6.8 collective-permute-done.55
  470.7 30.1 %collective-permute-done.84 = bf16[128,1536]{1,0:T(8,128)(2,1)S(1)} collective-permute-done((bf16[128,1536]{1,0:T(8,128)(2,1)S(1)}, bf16[128,1536]{1,0:T(8,128)(2,1)S(1)}, u32[]{:S(2)}, u32[]{:S(2)}) %collective-permute-start.84) | collective-permute-done | bytes 393248 | tf_op jit(solution)/shard_map/ppermute | solution.py:27
  503.6 16.5 %collective-permute-done.62 = bf16[128,1536]{1,0:T(8,128)(2,1)S(1)} collective-permute-done((bf16[128,1536]{1,0:T(8,128)(2,1)S(1)}, bf16[128,1536]{1,0:T(8,128)(2,1)S(1)}, u32[]{:S(2)}, u32[]{:S(2)}) %collective-permute-start.62) | collective-permute-done | bytes 393248 | tf_op jit(solution)/shard_map/ppermute | solution.py:27
  532.0 5.4 collective-permute-done.91
  538.5 5.1 fusion.100
  566.0 5.1 collective-permute-done.113.refs_2_
  572.2 4.8 collective-permute-done.115.refs_4_
  577.7 5.5 collective-permute-done.117.refs_6_
  585.4 9.3 %collective-permute-done.119.refs_8_ = bf16[1,48,1120]{2,1,0:T(8,128)(2,1)S(1)} collective-permute-done((bf16[1,48,1120]{2,1,0:T(8,128)(2,1)S(1)}, bf16[1,48,1120]{2,1,0:T(8,128)(2,1)S(1)}, u32[]{:S(2)}, u32[]{:S(2)}) %collective-permute-start.119) | collective-permute-done | bytes 107552 | tf_op jit(solution)/shard_map/ppermute | solution.py:27
  594.8 11.2 %collective-permute-done.121.refs_10_ = bf16[1,48,1120]{2,1,0:T(8,128)(2,1)S(1)} collective-permute-done((bf16[1,48,1120]{2,1,0:T(8,128)(2,1)S(1)}, bf16[1,48,1120]{2,1,0:T(8,128)(2,1)S(1)}, u32[]{:S(2)}, u32[]{:S(2)}) %collective-permute-start.121) | collective-permute-done | bytes 107552 | tf_op jit(solution)/shard_map/ppermute | solution.py:27
  615.0 5.6 collective-permute-done.125.refs_14_
  645.7 18.5 %collective-permute-done.105 = bf16[384,1536]{1,0:T(8,128)(2,1)S(1)} collective-permute-done((bf16[384,1536]{1,0:T(8,128)(2,1)S(1)}, bf16[384,1536]{1,0:T(8,128)(2,1)S(1)}, u32[]{:S(2)}, u32[]{:S(2)}) %collective-permute-start.105) | collective-permute-done | bytes 1179680 | tf_op jit(solution)/shard_map/ppermute | solution.py:27
  664.7 6.2 collective-permute-done.127
  671.1 12.4 %collective-permute-done.106 = bf16[192,1536]{1,0:T(8,128)(2,1)S(1)} collective-permute-done((bf16[192,1536]{1,0:T(8,128)(2,1)S(1)}, bf16[192,1536]{1,0:T(8,128)(2,1)S(1)}, u32[]{:S(2)}, u32[]{:S(2)}) %collective-permute-start.106) | collective-permute-done | bytes 589856 | tf_op jit(solution)/shard_map/ppermute | solution.py:31
  689.1 7.7 %collective-permute-done.98 = bf16[384,2048]{1,0:T(8,128)(2,1)S(1)} collective-permute-done((bf16[384,2048]{1,0:T(8,128)(2,1)S(1)}, bf16[384,2048]{1,0:T(8,128)(2,1)S(1)}, u32[]{:S(2)}, u32[]{:S(2)}) %collective-permute-start.98) | collective-permute-done | bytes 1572896 | tf_op jit(solution)/shard_map/ppermute | solution.py:27
  703.1 14.8 %collective-permute-done.99 = bf16[192,2048]{1,0:T(8,128)(2,1)S(1)} collective-permute-done((bf16[192,2048]{1,0:T(8,128)(2,1)S(1)}, bf16[192,2048]{1,0:T(8,128)(2,1)S(1)}, u32[]{:S(2)}, u32[]{:S(2)}) %collective-permute-start.99) | collective-permute-done | bytes 786464 | tf_op jit(solution)/shard_map/ppermute | solution.py:31
  722.7 5.2 collective-permute-done.102
  727.9 8.4 %collective-permute-done.101 = bf16[48,2048]{1,0:T(8,128)(2,1)S(1)} collective-permute-done((bf16[48,2048]{1,0:T(8,128)(2,1)S(1)}, bf16[48,2048]{1,0:T(8,128)(2,1)S(1)}, u32[]{:S(2)}, u32[]{:S(2)}) %collective-permute-start.101) | collective-permute-done | bytes 196640 | tf_op jit(solution)/shard_map/ppermute | solution.py:27
  738.4 4.7 collective-permute-done.103
  (664 shorter events, 338.1 us)
Async XLA Ops:
  33.1 21.6 %collective-permute-start.42 = (bf16[1,48,1120]{2,1,0:T(8,128)(2,1)S(1)}, bf16[1,48,1120]{2,1,0:T(8,128)(2,1)S(1)}, u32[]{:S(2)}, u32[]{:S(2)}) collective-permute-start(bf16[1,48,1120]{2,1,0:T(8,128)(2,1)S(1)} %copy-done.81), channel_id=1, source_target_pairs={{0,10},{1,11},{2,8},{3,9},{4,14},{5,15},{6,12},{7,13},{8,2},{9,3},... | collective-permute-start | bytes 322568 | tf_op jit(solution)/shard_map/ppermute | solution.py:27
  36.6 22.4 %collective-permute-start.43 = (bf16[1,48,1120]{2,1,0:T(8,128)(2,1)S(1)}, bf16[1,48,1120]{2,1,0:T(8,128)(2,1)S(1)}, u32[]{:S(2)}, u32[]{:S(2)}) collective-permute-start(bf16[1,48,1120]{2,1,0:T(8,128)(2,1)S(1)} %get-tuple-element.58), channel_id=1, source_target_pairs={{0,11},{1,10},{2,9},{3,8},{4,15},{5,14},{6,13},{7,12},{8,3},{9,2},... | collective-permute-start | bytes 322568 | tf_op jit(solution)/shard_map/ppermute | solution.py:27
  39.3 36.9 %collective-permute-start.16 = (bf16[48,1536]{1,0:T(8,128)(2,1)}, bf16[48,1536]{1,0:T(8,128)(2,1)}, u32[]{:S(2)}, u32[]{:S(2)}) collective-permute-start(bf16[48,1536]{1,0:T(8,128)(2,1)} %constant_dynamic-slice_fusion.33), channel_id=1, source_target_pairs={{0,2},{1,3},{2,0},{3,1},{4,6},{5,7},{6,4},{7,5},{8,10},{9,11},{10,... | collective-permute-start | bytes 442376 | tf_op jit(solution)/shard_map/ppermute | solution.py:27
  43.6 20.8 %collective-permute-start.44 = (bf16[1,48,1120]{2,1,0:T(8,128)(2,1)}, bf16[1,48,1120]{2,1,0:T(8,128)(2,1)S(1)}, u32[]{:S(2)}, u32[]{:S(2)}) collective-permute-start(bf16[1,48,1120]{2,1,0:T(8,128)(2,1)} %get-tuple-element.57), channel_id=1, source_target_pairs={{0,12},{1,13},{2,14},{3,15},{4,8},{5,9},{6,10},{7,11},{8,4},{9,5},... | collective-permute-start | bytes 322568 | tf_op jit(solution)/shard_map/ppermute | solution.py:27
  64.4 24.7 %collective-permute-start = (bf16[48,2048]{1,0:T(8,128)(2,1)}, bf16[48,2048]{1,0:T(8,128)(2,1)S(1)}, u32[]{:S(2)}, u32[]{:S(2)}) collective-permute-start(bf16[48,2048]{1,0:T(8,128)(2,1)} %constant_dynamic-slice_fusion.36), channel_id=1, source_target_pairs={{0,2},{1,3},{2,0},{3,1},{4,6},{5,7},{6,4},{7,5},{8,10},{9,11},{10,... | collective-permute-start | bytes 589832 | tf_op jit(solution)/shard_map/ppermute | solution.py:27
  65.6 52.9 %collective-permute-start.3 = (bf16[48,2048]{1,0:T(8,128)(2,1)}, bf16[48,2048]{1,0:T(8,128)(2,1)S(1)}, u32[]{:S(2)}, u32[]{:S(2)}) collective-permute-start(bf16[48,2048]{1,0:T(8,128)(2,1)} %constant_dynamic-slice_fusion.36), channel_id=1, source_target_pairs={{0,4},{1,5},{2,6},{3,7},{4,0},{5,1},{6,2},{7,3},{8,12},{9,13},{10,... | collective-permute-start | bytes 589832 | tf_op jit(solution)/shard_map/ppermute | solution.py:27
  69.0 51.6 %collective-permute-start.7 = (bf16[48,2048]{1,0:T(8,128)(2,1)}, bf16[48,2048]{1,0:T(8,128)(2,1)S(1)}, u32[]{:S(2)}, u32[]{:S(2)}) collective-permute-start(bf16[48,2048]{1,0:T(8,128)(2,1)} %constant_dynamic-slice_fusion.36), channel_id=1, source_target_pairs={{0,8},{1,9},{2,10},{3,11},{4,12},{5,13},{6,14},{7,15},{8,0},{9,1},... | collective-permute-start | bytes 589832 | tf_op jit(solution)/shard_map/ppermute | solution.py:27
  74.0 53.1 %collective-permute-start.11 = (bf16[48,2048]{1,0:T(8,128)(2,1)}, bf16[48,2048]{1,0:T(8,128)(2,1)S(1)}, u32[]{:S(2)}, u32[]{:S(2)}) collective-permute-start(bf16[48,2048]{1,0:T(8,128)(2,1)} %constant_dynamic-slice_fusion.36), channel_id=1, source_target_pairs={{0,12},{1,13},{2,14},{3,15},{4,8},{5,9},{6,10},{7,11},{8,4},{9,5},... | collective-permute-start | bytes 589832 | tf_op jit(solution)/shard_map/ppermute | solution.py:27
  117.2 54.5 %collective-permute-start.85 = (bf16[128,1536]{1,0:T(8,128)(2,1)S(1)}, bf16[128,1536]{1,0:T(8,128)(2,1)S(1)}, u32[]{:S(2)}, u32[]{:S(2)}) collective-permute-start(bf16[128,1536]{1,0:T(8,128)(2,1)S(1)} %bitcast.304), channel_id=1, source_target_pairs={{0,12},{1,13},{2,14},{3,15},{4,8},{5,9},{6,10},{7,11},{8,4},{9,5},... | collective-permute-start | bytes 1179656 | tf_op jit(solution)/shard_map/ppermute | solution.py:27
  118.6 53.3 %collective-permute-start.79 = (bf16[128,1536]{1,0:T(8,128)(2,1)S(1)}, bf16[128,1536]{1,0:T(8,128)(2,1)S(1)}, u32[]{:S(2)}, u32[]{:S(2)}) collective-permute-start(bf16[128,1536]{1,0:T(8,128)(2,1)S(1)} %bitcast.305), channel_id=1, source_target_pairs={{0,8},{1,9},{2,10},{3,11},{4,12},{5,13},{6,14},{7,15},{8,0},{9,1},... | collective-permute-start | bytes 1179656 | tf_op jit(solution)/shard_map/ppermute | solution.py:27
  120.6 52.7 %collective-permute-start.73 = (bf16[128,1536]{1,0:T(8,128)(2,1)S(1)}, bf16[128,1536]{1,0:T(8,128)(2,1)S(1)}, u32[]{:S(2)}, u32[]{:S(2)}) collective-permute-start(bf16[128,1536]{1,0:T(8,128)(2,1)S(1)} %bitcast.307), channel_id=1, source_target_pairs={{0,4},{1,5},{2,6},{3,7},{4,0},{5,1},{6,2},{7,3},{8,12},{9,13},{10,... | collective-permute-start | bytes 1179656 | tf_op jit(solution)/shard_map/ppermute | solution.py:27
  197.2 60.7 %collective-permute-start.48 = (bf16[16,48,1120]{2,1,0:T(8,128)(2,1)}, bf16[16,48,1120]{2,1,0:T(8,128)(2,1)}, u32[]{:S(2)}, u32[]{:S(2)}) collective-permute-start(bf16[16,48,1120]{2,1,0:T(8,128)(2,1)} %shard_map.180), channel_id=1, source_target_pairs={{0,16},{16,0},{1,17},{17,1},{2,18},{18,2},{3,19},{19,3},{4,20},{20... | collective-permute-start | bytes 5160968 | tf_op jit(solution)/shard_map/ppermute | solution.py:31
  206.4 34.8 %collective-permute-start.15 = (bf16[128,512]{1,0:T(8,128)(2,1)S(1)}, bf16[128,512]{1,0:T(8,128)(2,1)}, u32[]{:S(2)}, u32[]{:S(2)}) collective-permute-start(bf16[128,512]{1,0:T(8,128)(2,1)S(1)} %pad_maximum_fusion.38), channel_id=1, source_target_pairs={{0,16},{16,0},{1,17},{17,1},{2,18},{18,2},{3,19},{19,3},{4,20},{20... | collective-permute-start | bytes 393224 | tf_op jit(solution)/shard_map/ppermute | solution.py:31
  250.8 28.6 %collective-permute-start.63 = (bf16[128,1536]{1,0:T(8,128)(2,1)}, bf16[128,1536]{1,0:T(8,128)(2,1)S(1)}, u32[]{:S(2)}, u32[]{:S(2)}) collective-permute-start(bf16[128,1536]{1,0:T(8,128)(2,1)} %get-tuple-element.14), channel_id=1, source_target_pairs={{0,12},{1,13},{2,14},{3,15},{4,8},{5,9},{6,10},{7,11},{8,4},{9,5},... | collective-permute-start | bytes 1179656 | tf_op jit(solution)/shard_map/ppermute | solution.py:27
  253.6 35.1 %collective-permute-start.57 = (bf16[128,1536]{1,0:T(8,128)(2,1)}, bf16[128,1536]{1,0:T(8,128)(2,1)S(1)}, u32[]{:S(2)}, u32[]{:S(2)}) collective-permute-start(bf16[128,1536]{1,0:T(8,128)(2,1)} %get-tuple-element.14), channel_id=1, source_target_pairs={{0,8},{1,9},{2,10},{3,11},{4,12},{5,13},{6,14},{7,15},{8,0},{9,1},... | collective-permute-start | bytes 1179656 | tf_op jit(solution)/shard_map/ppermute | solution.py:27
  255.5 34.1 %collective-permute-start.51 = (bf16[128,1536]{1,0:T(8,128)(2,1)}, bf16[128,1536]{1,0:T(8,128)(2,1)}, u32[]{:S(2)}, u32[]{:S(2)}) collective-permute-start(bf16[128,1536]{1,0:T(8,128)(2,1)} %get-tuple-element.14), channel_id=1, source_target_pairs={{0,4},{1,5},{2,6},{3,7},{4,0},{5,1},{6,2},{7,3},{8,12},{9,13},{10,... | collective-permute-start | bytes 1179656 | tf_op jit(solution)/shard_map/ppermute | solution.py:27
  255.5 25.1 %collective-permute-start.31 = (bf16[128,1536]{1,0:T(8,128)(2,1)}, bf16[128,1536]{1,0:T(8,128)(2,1)}, u32[]{:S(2)}, u32[]{:S(2)}) collective-permute-start(bf16[128,1536]{1,0:T(8,128)(2,1)} %get-tuple-element.14), channel_id=1, source_target_pairs={{0,2},{1,3},{2,0},{3,1},{4,6},{5,7},{6,4},{7,5},{8,10},{9,11},{10,... | collective-permute-start | bytes 1179656 | tf_op jit(solution)/shard_map/ppermute | solution.py:27
  282.1 27.2 %collective-permute-start.32 = (bf16[256,1536]{1,0:T(8,128)(2,1)S(1)}, bf16[256,1536]{1,0:T(8,128)(2,1)S(1)}, u32[]{:S(2)}, u32[]{:S(2)}) collective-permute-start(bf16[256,1536]{1,0:T(8,128)(2,1)S(1)} %pad_maximum_fusion.6), channel_id=1, source_target_pairs={{0,1},{1,0},{2,3},{3,2},{4,5},{5,4},{6,7},{7,6},{8,9},{9,8},{10,11... | collective-permute-start | bytes 2359304 | tf_op jit(solution)/shard_map/ppermute | solution.py:27
  291.8 28.3 %collective-permute-start.65 = (bf16[256,1536]{1,0:T(8,128)(2,1)S(1)}, bf16[256,1536]{1,0:T(8,128)(2,1)S(1)}, u32[]{:S(2)}, u32[]{:S(2)}) collective-permute-start(bf16[256,1536]{1,0:T(8,128)(2,1)S(1)} %pad_maximum_fusion.9), channel_id=1, source_target_pairs={{0,1},{1,0},{2,3},{3,2},{4,5},{5,4},{6,7},{7,6},{8,9},{9,8},{10,11... | collective-permute-start | bytes 2359304 | tf_op jit(solution)/shard_map/ppermute | solution.py:27
  300.7 28.0 %collective-permute-start.59 = (bf16[256,1536]{1,0:T(8,128)(2,1)S(1)}, bf16[256,1536]{1,0:T(8,128)(2,1)S(1)}, u32[]{:S(2)}, u32[]{:S(2)}) collective-permute-start(bf16[256,1536]{1,0:T(8,128)(2,1)S(1)} %pad_maximum_fusion.8), channel_id=1, source_target_pairs={{0,1},{1,0},{2,3},{3,2},{4,5},{5,4},{6,7},{7,6},{8,9},{9,8},{10,11... | collective-permute-start | bytes 2359304 | tf_op jit(solution)/shard_map/ppermute | solution.py:27
  309.2 27.9 %collective-permute-start.53 = (bf16[256,1536]{1,0:T(8,128)(2,1)S(1)}, bf16[256,1536]{1,0:T(8,128)(2,1)S(1)}, u32[]{:S(2)}, u32[]{:S(2)}) collective-permute-start(bf16[256,1536]{1,0:T(8,128)(2,1)S(1)} %pad_maximum_fusion.7), channel_id=1, source_target_pairs={{0,1},{1,0},{2,3},{3,2},{4,5},{5,4},{6,7},{7,6},{8,9},{9,8},{10,11... | collective-permute-start | bytes 2359304 | tf_op jit(solution)/shard_map/ppermute | solution.py:27
  316.8 76.4 %collective-permute-start.71 = (bf16[256,1536]{1,0:T(8,128)(2,1)}, bf16[256,1536]{1,0:T(8,128)(2,1)}, u32[]{:S(2)}, u32[]{:S(2)}) collective-permute-start(bf16[256,1536]{1,0:T(8,128)(2,1)} %convolution_convert_fusion.9), channel_id=1, source_target_pairs={{0,1},{1,0},{2,3},{3,2},{4,5},{5,4},{6,7},{7,6},{8,9},{9,8},{10,11... | collective-permute-start | bytes 2359304 | tf_op jit(solution)/shard_map/ppermute | solution.py:27
  318.9 77.8 %collective-permute-start.49 = (bf16[256,1536]{1,0:T(8,128)(2,1)}, bf16[256,1536]{1,0:T(8,128)(2,1)}, u32[]{:S(2)}, u32[]{:S(2)}) collective-permute-start(bf16[256,1536]{1,0:T(8,128)(2,1)} %convolution_convert_fusion.5), channel_id=1, source_target_pairs={{0,1},{1,0},{2,3},{3,2},{4,5},{5,4},{6,7},{7,6},{8,9},{9,8},{10,11... | collective-permute-start | bytes 2359304 | tf_op jit(solution)/shard_map/ppermute | solution.py:27
  328.2 70.9 %collective-permute-start.88 = (bf16[256,1536]{1,0:T(8,128)(2,1)}, bf16[256,1536]{1,0:T(8,128)(2,1)}, u32[]{:S(2)}, u32[]{:S(2)}) collective-permute-start(bf16[256,1536]{1,0:T(8,128)(2,1)} %convolution_convert_fusion.6), channel_id=1, source_target_pairs={{0,1},{1,0},{2,3},{3,2},{4,5},{5,4},{6,7},{7,6},{8,9},{9,8},{10,11... | collective-permute-start | bytes 2359304 | tf_op jit(solution)/shard_map/ppermute | solution.py:27
  336.9 64.9 %collective-permute-start.82 = (bf16[256,1536]{1,0:T(8,128)(2,1)}, bf16[256,1536]{1,0:T(8,128)(2,1)}, u32[]{:S(2)}, u32[]{:S(2)}) collective-permute-start(bf16[256,1536]{1,0:T(8,128)(2,1)} %convolution_convert_fusion.7), channel_id=1, source_target_pairs={{0,1},{1,0},{2,3},{3,2},{4,5},{5,4},{6,7},{7,6},{8,9},{9,8},{10,11... | collective-permute-start | bytes 2359304 | tf_op jit(solution)/shard_map/ppermute | solution.py:27
  345.1 62.7 %collective-permute-start.76 = (bf16[256,1536]{1,0:T(8,128)(2,1)}, bf16[256,1536]{1,0:T(8,128)(2,1)}, u32[]{:S(2)}, u32[]{:S(2)}) collective-permute-start(bf16[256,1536]{1,0:T(8,128)(2,1)} %convolution_convert_fusion.8), channel_id=1, source_target_pairs={{0,1},{1,0},{2,3},{3,2},{4,5},{5,4},{6,7},{7,6},{8,9},{9,8},{10,11... | collective-permute-start | bytes 2359304 | tf_op jit(solution)/shard_map/ppermute | solution.py:27
  401.9 147.8 %collective-permute-start.111 = (bf16[16,48,1120]{2,1,0:T(8,128)(2,1)}, bf16[16,48,1120]{2,1,0:T(8,128)(2,1)}, u32[]{:S(2)}, u32[]{:S(2)}) collective-permute-start(bf16[16,48,1120]{2,1,0:T(8,128)(2,1)} %fusion.26), channel_id=1, source_target_pairs={{0,16},{16,0},{1,17},{17,1},{2,18},{18,2},{3,19},{19,3},{4,20},{20... | collective-permute-start | bytes 5160968 | tf_op jit(solution)/shard_map/ppermute | solution.py:31
  406.1 62.4 %collective-permute-start.72 = (bf16[128,1536]{1,0:T(8,128)(2,1)S(1)}, bf16[128,1536]{1,0:T(8,128)(2,1)S(1)}, u32[]{:S(2)}, u32[]{:S(2)}) collective-permute-start(bf16[128,1536]{1,0:T(8,128)(2,1)S(1)} %slice.631), channel_id=1, source_target_pairs={{0,2},{1,3},{2,0},{3,1},{4,6},{5,7},{6,4},{7,5},{8,10},{9,11},{10,... | collective-permute-start | bytes 1179656 | tf_op jit(solution)/shard_map/ppermute | solution.py:27
  411.5 23.5 %collective-permute-start.83 = (bf16[128,1536]{1,0:T(8,128)(2,1)S(1)}, bf16[128,1536]{1,0:T(8,128)(2,1)S(1)}, u32[]{:S(2)}, u32[]{:S(2)}) collective-permute-start(bf16[128,1536]{1,0:T(8,128)(2,1)S(1)} %slice.629), channel_id=1, source_target_pairs={{0,2},{1,3},{2,0},{3,1},{4,6},{5,7},{6,4},{7,5},{8,10},{9,11},{10,... | collective-permute-start | bytes 1179656 | tf_op jit(solution)/shard_map/ppermute | solution.py:27
  413.3 30.1 %collective-permute-start.77 = (bf16[128,1536]{1,0:T(8,128)(2,1)S(1)}, bf16[128,1536]{1,0:T(8,128)(2,1)S(1)}, u32[]{:S(2)}, u32[]{:S(2)}) collective-permute-start(bf16[128,1536]{1,0:T(8,128)(2,1)S(1)} %slice.630), channel_id=1, source_target_pairs={{0,2},{1,3},{2,0},{3,1},{4,6},{5,7},{6,4},{7,5},{8,10},{9,11},{10,... | collective-permute-start | bytes 1179656 | tf_op jit(solution)/shard_map/ppermute | solution.py:27
  426.5 25.3 %collective-permute-start.67 = (bf16[128,1536]{1,0:T(8,128)(2,1)S(1)}, bf16[128,1536]{1,0:T(8,128)(2,1)S(1)}, u32[]{:S(2)}, u32[]{:S(2)}) collective-permute-start(bf16[128,1536]{1,0:T(8,128)(2,1)S(1)} %slice.632), channel_id=1, source_target_pairs={{0,2},{1,3},{2,0},{3,1},{4,6},{5,7},{6,4},{7,5},{8,10},{9,11},{10,... | collective-permute-start | bytes 1179656 | tf_op jit(solution)/shard_map/ppermute | solution.py:27
  435.0 25.3 %collective-permute-start.61 = (bf16[128,1536]{1,0:T(8,128)(2,1)S(1)}, bf16[128,1536]{1,0:T(8,128)(2,1)S(1)}, u32[]{:S(2)}, u32[]{:S(2)}) collective-permute-start(bf16[128,1536]{1,0:T(8,128)(2,1)S(1)} %slice.633), channel_id=1, source_target_pairs={{0,2},{1,3},{2,0},{3,1},{4,6},{5,7},{6,4},{7,5},{8,10},{9,11},{10,... | collective-permute-start | bytes 1179656 | tf_op jit(solution)/shard_map/ppermute | solution.py:27
  443.4 24.3 %collective-permute-start.55 = (bf16[128,1536]{1,0:T(8,128)(2,1)S(1)}, bf16[128,1536]{1,0:T(8,128)(2,1)S(1)}, u32[]{:S(2)}, u32[]{:S(2)}) collective-permute-start(bf16[128,1536]{1,0:T(8,128)(2,1)S(1)} %slice.634), channel_id=1, source_target_pairs={{0,2},{1,3},{2,0},{3,1},{4,6},{5,7},{6,4},{7,5},{8,10},{9,11},{10,... | collective-permute-start | bytes 1179656 | tf_op jit(solution)/shard_map/ppermute | solution.py:27
  460.2 40.6 %collective-permute-start.84 = (bf16[128,1536]{1,0:T(8,128)(2,1)S(1)}, bf16[128,1536]{1,0:T(8,128)(2,1)S(1)}, u32[]{:S(2)}, u32[]{:S(2)}) collective-permute-start(bf16[128,1536]{1,0:T(8,128)(2,1)S(1)} %fusion.106), channel_id=1, source_target_pairs={{0,8},{1,9},{2,10},{3,11},{4,12},{5,13},{6,14},{7,15},{8,0},{9,1},... | collective-permute-start | bytes 1179656 | tf_op jit(solution)/shard_map/ppermute | solution.py:27
  467.7 33.2 %collective-permute-start.78 = (bf16[128,1536]{1,0:T(8,128)(2,1)S(1)}, bf16[128,1536]{1,0:T(8,128)(2,1)S(1)}, u32[]{:S(2)}, u32[]{:S(2)}) collective-permute-start(bf16[128,1536]{1,0:T(8,128)(2,1)S(1)} %fusion.107), channel_id=1, source_target_pairs={{0,4},{1,5},{2,6},{3,7},{4,0},{5,1},{6,2},{7,3},{8,12},{9,13},{10,... | collective-permute-start | bytes 1179656 | tf_op jit(solution)/shard_map/ppermute | solution.py:27
  468.5 34.7 %collective-permute-start.50 = (bf16[128,1536]{1,0:T(8,128)(2,1)S(1)}, bf16[128,1536]{1,0:T(8,128)(2,1)S(1)}, u32[]{:S(2)}, u32[]{:S(2)}) collective-permute-start(bf16[128,1536]{1,0:T(8,128)(2,1)S(1)} %slice.635), channel_id=1, source_target_pairs={{0,2},{1,3},{2,0},{3,1},{4,6},{5,7},{6,4},{7,5},{8,10},{9,11},{10,... | collective-permute-start | bytes 1179656 | tf_op jit(solution)/shard_map/ppermute | solution.py:27
  469.5 34.1 %collective-permute-start.68 = (bf16[128,1536]{1,0:T(8,128)(2,1)S(1)}, bf16[128,1536]{1,0:T(8,128)(2,1)S(1)}, u32[]{:S(2)}, u32[]{:S(2)}) collective-permute-start(bf16[128,1536]{1,0:T(8,128)(2,1)S(1)} %fusion.111), channel_id=1, source_target_pairs={{0,12},{1,13},{2,14},{3,15},{4,8},{5,9},{6,10},{7,11},{8,4},{9,5},... | collective-permute-start | bytes 1179656 | tf_op jit(solution)/shard_map/ppermute | solution.py:27
  500.8 19.2 %collective-permute-start.62 = (bf16[128,1536]{1,0:T(8,128)(2,1)S(1)}, bf16[128,1536]{1,0:T(8,128)(2,1)S(1)}, u32[]{:S(2)}, u32[]{:S(2)}) collective-permute-start(bf16[128,1536]{1,0:T(8,128)(2,1)S(1)} %fusion.112), channel_id=1, source_target_pairs={{0,8},{1,9},{2,10},{3,11},{4,12},{5,13},{6,14},{7,15},{8,0},{9,1},... | collective-permute-start | bytes 1179656 | tf_op jit(solution)/shard_map/ppermute | solution.py:27
  500.8 19.2 %collective-permute-start.56 = (bf16[128,1536]{1,0:T(8,128)(2,1)S(1)}, bf16[128,1536]{1,0:T(8,128)(2,1)S(1)}, u32[]{:S(2)}, u32[]{:S(2)}) collective-permute-start(bf16[128,1536]{1,0:T(8,128)(2,1)S(1)} %fusion.113), channel_id=1, source_target_pairs={{0,4},{1,5},{2,6},{3,7},{4,0},{5,1},{6,2},{7,3},{8,12},{9,13},{10,... | collective-permute-start | bytes 1179656 | tf_op jit(solution)/shard_map/ppermute | solution.py:27
  503.2 133.1 %collective-permute-start.128 = (bf16[560,1536]{1,0:T(8,128)(2,1)}, bf16[560,1536]{1,0:T(8,128)(2,1)}, u32[]{:S(2)}, u32[]{:S(2)}) collective-permute-start(bf16[560,1536]{1,0:T(8,128)(2,1)} %slice.623), channel_id=1, source_target_pairs={{0,16},{16,0},{1,17},{17,1},{2,18},{18,2},{3,19},{19,3},{4,20},{20... | collective-permute-start | bytes 5160968 | tf_op jit(solution)/shard_map/ppermute | solution.py:31
  531.9 100.8 %collective-permute-start.104 = (bf16[768,1536]{1,0:T(8,128)(2,1)}, bf16[768,1536]{1,0:T(8,128)(2,1)}, u32[]{:S(2)}, u32[]{:S(2)}) collective-permute-start(bf16[768,1536]{1,0:T(8,128)(2,1)} %convolution_convert_fusion), channel_id=1, source_target_pairs={{0,1},{1,0},{2,3},{3,2},{4,5},{5,4},{6,7},{7,6},{8,9},{9,8},{10,11... | collective-permute-start | bytes 7077896 | tf_op jit(solution)/shard_map/ppermute | solution.py:27
  549.2 92.4 %collective-permute-start.97 = (bf16[768,2048]{1,0:T(8,128)(2,1)}, bf16[768,2048]{1,0:T(8,128)(2,1)}, u32[]{:S(2)}, u32[]{:S(2)}) collective-permute-start(bf16[768,2048]{1,0:T(8,128)(2,1)} %convolution_convert_fusion.1), channel_id=1, source_target_pairs={{0,1},{1,0},{2,3},{3,2},{4,5},{5,4},{6,7},{7,6},{8,9},{9,8},{10,11... | collective-permute-start | bytes 9437192 | tf_op jit(solution)/shard_map/ppermute | solution.py:27
  620.6 19.7 %collective-permute-start.96 = (f32[5120]{0:T(1024)S(1)}, f32[5120]{0:T(1024)S(1)}, u32[]{:S(2)}, u32[]{:S(2)}) collective-permute-start(f32[5120]{0:T(1024)S(1)} %add.1091), channel_id=1, source_target_pairs={{0,16},{16,0},{1,17},{17,1},{2,18},{18,2},{3,19},{19,3},{4,20},{20... | collective-permute-start | bytes 61448 | tf_op jit(solution)/shard_map/ppermute | solution.py:31
  630.8 40.0 %collective-permute-start.127 = (bf16[48,17920]{1,0:T(8,128)(2,1)}, bf16[48,17920]{1,0:T(8,128)(2,1)S(1)}, u32[]{:S(2)}, u32[]{:S(2)}) collective-permute-start(bf16[48,17920]{1,0:T(8,128)(2,1)} %reshape.298), channel_id=1, source_target_pairs={{0,16},{16,0},{1,17},{17,1},{2,18},{18,2},{3,19},{19,3},{4,20},{20... | collective-permute-start | bytes 5160968 | tf_op jit(solution)/shard_map/ppermute | solution.py:31
  635.3 28.9 %collective-permute-start.105 = (bf16[384,1536]{1,0:T(8,128)(2,1)S(1)}, bf16[384,1536]{1,0:T(8,128)(2,1)S(1)}, u32[]{:S(2)}, u32[]{:S(2)}) collective-permute-start(bf16[384,1536]{1,0:T(8,128)(2,1)S(1)} %slice.625), channel_id=1, source_target_pairs={{0,2},{1,3},{2,0},{3,1},{4,6},{5,7},{6,4},{7,5},{8,10},{9,11},{10,... | collective-permute-start | bytes 3538952 | tf_op jit(solution)/shard_map/ppermute | solution.py:27
  644.7 52.1 %collective-permute-start.98 = (bf16[384,2048]{1,0:T(8,128)(2,1)S(1)}, bf16[384,2048]{1,0:T(8,128)(2,1)S(1)}, u32[]{:S(2)}, u32[]{:S(2)}) collective-permute-start(bf16[384,2048]{1,0:T(8,128)(2,1)S(1)} %slice.624), channel_id=1, source_target_pairs={{0,2},{1,3},{2,0},{3,1},{4,6},{5,7},{6,4},{7,5},{8,10},{9,11},{10,... | collective-permute-start | bytes 4718600 | tf_op jit(solution)/shard_map/ppermute | solution.py:27
  697.3 20.5 %collective-permute-start.99 = (bf16[192,2048]{1,0:T(8,128)(2,1)S(1)}, bf16[192,2048]{1,0:T(8,128)(2,1)S(1)}, u32[]{:S(2)}, u32[]{:S(2)}) collective-permute-start(bf16[192,2048]{1,0:T(8,128)(2,1)S(1)} %slice.626), channel_id=1, source_target_pairs={{0,16},{16,0},{1,17},{17,1},{2,18},{18,2},{3,19},{19,3},{4,20},{20... | collective-permute-start | bytes 2359304 | tf_op jit(solution)/shard_map/ppermute | solution.py:31
  702.0 20.6 %collective-permute-start.110 = (bf16[48,1536]{1,0:T(8,128)(2,1)S(1)}, bf16[48,1536]{1,0:T(8,128)(2,1)S(1)}, u32[]{:S(2)}, u32[]{:S(2)}) collective-permute-start(bf16[48,1536]{1,0:T(8,128)(2,1)S(1)} %fusion.188), channel_id=1, source_target_pairs={{0,16},{16,0},{1,17},{17,1},{2,18},{18,2},{3,19},{19,3},{4,20},{20... | collective-permute-start | bytes 442376 | tf_op jit(solution)/shard_map/ppermute | solution.py:31
  (198 other events, 2059.4 us)

commit v2 on v0

v2 whole, which is shorter than its diff:
```python
import functools

import jax
import jax.numpy as jnp
from jax import lax
from jax.experimental import pallas as pl
from jax.experimental.pallas import tpu as pltpu
from jax.sharding import PartitionSpec as P

D = 1536
FF = 8960
HQ = 12
KV = 2
HD = 128
GROUP = HQ // KV
QW = HQ * HD
KW = KV * HD

rope_base = 1000000.0
norm_eps = 1e-06
bf16 = jnp.bfloat16
f32 = jnp.float32


CORE, X, Z = 1, 2, 4
ROTATED = ((Z, X, "y"), (X, "y", Z), ("y", Z, X))
CROSSED = ((X, Z), (Z, X))
VMEM = 48 * 1024 * 1024


def far_bits():
    return [bit for bit in (8 << i for i in range(16)) if bit < lax.axis_size("fsdp")]


def after(value, *earlier):
    return lax.optimization_barrier((value,) + earlier)[0]


class Move:
    def __init__(self, steps):
        self.steps = steps
        self.result = self.arrived = None
        self.wanted = next(steps)

    def resume(self, beside=()):
        if self.arrived is None:
            return
        arrived, self.arrived = self.arrived, None
        if beside:
            arrived = [after(value, *beside) for value in arrived]
        try:
            self.wanted = self.steps.send(arrived)
        except StopIteration as stop:
            self.result = stop.value


class Lanes:
    def __init__(self):
        self.moves, self.flying, self.ended, self.before, self.kernels = [], [], [], [], []

    def round(self, *entries):
        for move in self.moves:
            move.resume(self.kernels)
        self.moves = []
        ended = [value for value, left in self.flying if left <= 1] + self.kernels
        self.before, self.ended = ended + self.ended, ended
        self.flying = [(value, left - 1) for value, left in self.flying if left > 1]
        self.kernels = []
        self.more(*entries)

    def more(self, *entries):
        size = lax.axis_size("fsdp")
        for entry in entries:
            move, lasts = entry if isinstance(entry, tuple) else (entry, 1)
            if not move.wanted:
                continue
            move.arrived = []
            for link, value in move.wanted:
                if self.before:
                    value = after(value, *self.before)
                if link == "y":
                    value = lax.ppermute(value, "seq", [(0, 1), (1, 0)])
                else:
                    value = lax.ppermute(value, "fsdp", [(i, i ^ link) for i in range(size)])
                move.arrived.append(value)
                self.flying.append((value, lasts))
            move.wanted = None
            self.moves.append(move)

    def hold(self, value):
        return after(value, *self.before) if self.before else value

    def beside(self, *values):
        self.kernels += values

    def drain(self, *moves):
        for move in moves:
            move.resume()
        while any(move.wanted for move in moves):
            self.round(*moves)
            for move in moves:
                move.resume()
        return [move.result for move in moves]


def add(left, right):
    return left.astype(f32) + right.astype(f32)


def dot(left, right):
    return jnp.dot(left, right, preferred_element_type=f32)


def dot_t(left, right):
    return lax.dot_general(left, right, (((1,), (1,)), ((), ())), preferred_element_type=f32)


def t_dot(left, right):
    return lax.dot_general(left, right, (((0,), (0,)), ((), ())), preferred_element_type=f32)


def join(*pieces, axis=0):
    return jnp.concatenate(pieces, axis=axis)


def pick(value, index, axis):
    return lax.index_in_dim(value, index, axis, keepdims=False)


def whole_call(kernel, out_shape, scalars, arrays, scratch=(), flops=0):
    outs = out_shape if isinstance(out_shape, (list, tuple)) else [out_shape]
    moved = sum(a.size * a.dtype.itemsize for a in list(arrays) + list(outs))
    spec = pl.BlockSpec(memory_space=pltpu.VMEM)
    return pl.pallas_call(
        kernel,
        out_shape=out_shape,
        in_specs=[pl.BlockSpec(memory_space=pltpu.SMEM)] + [spec] * len(arrays),
        out_specs=jax.tree.map(lambda _: spec, out_shape),
        scratch_shapes=list(scratch),
        compiler_params=pltpu.CompilerParams(vmem_limit_bytes=VMEM),
        cost_estimate=pl.CostEstimate(flops=flops, bytes_accessed=moved, transcendentals=0),
    )(jnp.stack(scalars).astype(jnp.int32), *arrays)


def gather_tokens(rows, blocks):
    state = rows[None]
    for bit in far_bits():
        (got,) = yield [(bit, state)]
        state = join(state, got)
    half, width = rows.shape[0] // 2, rows.shape[1]
    first, second = state[:, :half], state[:, half:]
    got = yield [(Z, first), (X, second)]
    first, second = join(first, got[0]), join(second, got[1])
    blocks.append([v.reshape(-1, width) for v in (first, second)])
    last = yield [(X, first), (Z, second)]
    blocks.append([v.reshape(-1, width) for v in last])


def scatter_tokens(early, last):
    width = last[0].shape[1]
    far = far_bits()
    count = 1 << len(far)
    half = last[0].shape[0] // count // 2
    got = yield [(X, last[0]), (Z, last[1])]
    first = add(early[0], got[0]).reshape(2, count, half, width)
    second = add(early[1], got[1]).reshape(2, count, half, width)
    got = yield [(Z, first[1].astype(bf16)), (X, second[1].astype(bf16))]
    state = join(add(first[0], got[0]), add(second[0], got[1]), axis=1)
    for bit in reversed(far):
        count //= 2
        (got,) = yield [(bit, state[count:].astype(bf16))]
        state = add(state[:count], got)
    return state[0]


def place_kernel(where, *refs):
    out = refs[-1]
    at = 0
    for ref in refs[:-1]:
        for i in range(ref.shape[0]):
            out[where[at]] = ref[i]
            at += 1


def cut_columns(width):
    third = width // 3 // 128 * 128
    return ((0, third), (third, 2 * third), (2 * third, width))


def gather_weight(shard, me, s):
    size = lax.axis_size("fsdp")
    half, width = shard.shape[0] // 2, shard.shape[1]
    state = lax.dynamic_index_in_dim(shard.reshape(2, half, width), s, 0)
    marks = [(0, 0)]
    for bit in far_bits():
        (got,) = yield [(bit, state)]
        state = join(state, got)
        marks = marks + [(f ^ bit, h) for f, h in marks]
    states = [state[:, :, low:high] for low, high in cut_columns(width)]
    for step in range(3):
        got = yield [(ROTATED[part][step], states[part]) for part in range(3)]
        states = [join(*pair) for pair in zip(states, got)]
    turns = []
    for order in ROTATED:
        index = [order.index(link) for link in reversed(ROTATED[0])]
        turns.append([2 - i for i in index])
    count = len(marks)
    split = [v.reshape(2, 2, 2, count, half, v.shape[-1]) for v in states]
    state = join(*[jnp.transpose(v, t + [3, 4, 5]) for v, t in zip(split, turns)], axis=-1)
    state = state.reshape(8 * count, half, width)
    for link in ROTATED[0]:
        marks = marks + [(f, 1 - h) if link == "y" else (f ^ link, h) for f, h in marks]
    (got,) = yield [(CORE, state)]
    where = []
    for core in range(2):
        where += [(me ^ f ^ core) * 2 + (s ^ h) for f, h in marks]
    whole = whole_call(
        place_kernel,
        jax.ShapeDtypeStruct((size * 2, half, width), bf16),
        where,
        [state, got],
    )
    return whole.reshape(size * 2 * half, width)


def gather_weight_plain(shard, me):
    size = lax.axis_size("fsdp")
    rows, width = shard.shape
    state = shard[None]
    marks = [0]
    for bit in far_bits():
        (got,) = yield [(bit, state)]
        state = join(state, got)
        marks = marks + [f ^ bit for f in marks]
    half = width // 2
    first, second = state[:, :, :half], state[:, :, half:]
    got = yield [(X, first), (Z, second)]
    first, second = join(first, got[0]), join(second, got[1])
    got = yield [(Z, first), (X, second)]
    count = len(marks)
    second = join(second[:count], got[1][:count], second[count:], got[1][count:])
    state = join(join(first, got[0]), second, axis=2)
    for link in (X, Z):
        marks = marks + [f ^ link for f in marks]
    (got,) = yield [(CORE, state)]
    where = [me ^ f for f in marks] + [me ^ f ^ CORE for f in marks]
    whole = whole_call(
        place_kernel, jax.ShapeDtypeStruct((size, rows, width), bf16), where, [state, got]
    )
    return whole.reshape(size * rows, width)


def order_kernel(where, source, out):
    for i in range(source.shape[0]):
        out[where[i]] = source[i]


def scatter_weight(left, right, me, s):
    size = lax.axis_size("fsdp")
    far = far_bits()
    count = 1 << len(far)
    rows, width = left.shape[1], right.shape[1]
    half = rows // size // 2
    turned = left.T.reshape(size * 2, half, left.shape[0])
    where = []
    for place in range(size):
        for h in range(2):
            k = me ^ place
            kept = ((k % 2) * 2 + (k // 2) % 2) * 2 + (k // 4) % 2
            where.append((kept * count + k // 8) * 2 + (s ^ h))
    turned = whole_call(
        order_kernel, jax.ShapeDtypeStruct(turned.shape, bf16), where, [turned]
    ).reshape(2, rows // 2, left.shape[0])
    (got,) = yield [(CORE, dot(turned[1], right).astype(bf16))]
    total = add(dot(turned[0], right), got).reshape(2, 2, count, 2, half, width)
    low, high = total[..., : width // 2], total[..., width // 2 :]
    got = yield [(X, low[1].astype(bf16)), (Z, high[:, 1].astype(bf16))]
    low, high = add(low[0], got[0]), add(high[:, 0], got[1])
    got = yield [(Z, low[1].astype(bf16)), (X, high[1].astype(bf16))]
    state = join(add(low[0], got[0]), add(high[0], got[1]), axis=-1)
    for bit in reversed(far):
        count //= 2
        (got,) = yield [(bit, state[count:].astype(bf16))]
        state = add(state[:count], got)
    (got,) = yield [("y", state[0, 1].astype(bf16))]
    mine = add(state[0, 0], got).astype(bf16)
    (other,) = yield [("y", mine)]
    low = jnp.where(s == 0, mine, other)
    high = jnp.where(s == 0, other, mine)
    return join(low, high).astype(f32)


def sum_everywhere(value):
    for link in [CORE, X, Z] + far_bits() + ["y"]:
        (got,) = yield [(link, value)]
        value = value + got
    return value


def swap(link, value):
    (got,) = yield [(link, value)]
    return got


def exchange_blocks(blocks, order):
    axes = list(reversed(far_bits())) + [Z, X]
    state = blocks.reshape((1,) + (2,) * len(axes) + blocks.shape[1:])
    marks = [0]
    for link in order:
        axis = 1 + axes.index(link)
        axes.remove(link)
        (got,) = yield [(link, pick(state, 1, axis))]
        state = join(pick(state, 0, axis), got)
        marks = marks + [f ^ link for f in marks]
    return state, marks


def split_kernel(unit, at, shard, gate, up):
    for chip in range(gate.shape[0]):
        low = chip * unit
        gate[at[0] ^ chip] = shard[at[1], :, low : low + unit]
        up[at[0] ^ chip] = shard[at[1], :, FF + low : FF + low + unit]


def weave_kernel(unit, where, *refs):
    out = refs[-1]
    half, padded = out.shape[1], out.shape[2] // 2
    at = 0
    for part in range(2):
        low = part * padded
        for ref in refs[3 * part : 3 * part + 3]:
            for i in range(ref.shape[0]):
                out[where[at], :, low : low + unit] = ref[i]
                if padded > unit:
                    out[where[at], :, low + unit : low + padded] = jnp.zeros(
                        (half, padded - unit), out.dtype
                    )
                at += 1


def split_gate_up(shard, me, s):
    size = lax.axis_size("fsdp")
    half = shard.shape[0] // 2
    unit = 2 * FF // size
    block = jax.ShapeDtypeStruct((size // 2, half, unit), bf16)
    return whole_call(
        functools.partial(split_kernel, unit),
        (block, block),
        [me // 2, s],
        [shard.reshape(2, half, 2 * FF)],
    )


def shuffle_part(blocks, order):
    mine, marks = yield from exchange_blocks(blocks, order)
    (other,) = yield [("y", mine)]
    (got,) = yield [(CORE, join(mine, other))]
    return [mine, other, got], marks


def weave_gate_up(parts, me, s):
    size = lax.axis_size("fsdp")
    half, unit = parts[0][0][0].shape[1:]
    padded = -(-unit // 384) * 384
    pieces, where = [], []
    for blocks, marks in parts:
        pieces += blocks
        for core in range(2):
            for h in range(2):
                where += [(me ^ f ^ core) * 2 + (s ^ h) for f in marks]
    whole = whole_call(
        functools.partial(weave_kernel, unit),
        jax.ShapeDtypeStruct((size * 2, half, 2 * padded), bf16),
        where,
        pieces,
    )
    return whole.reshape(size * 2 * half, 2 * padded)


def grad_kernel(count, unit, at, *refs):
    outs = refs[-2:]
    half = outs[0].shape[2]
    total = 0.0
    for j in range(count):
        total = total + t_dot(refs[j][...], refs[count + j][...])
    total = total.astype(bf16)[:, :unit]
    here = total.shape[0] // (2 * half)
    for i in range(here):
        k = at[0] ^ (pl.program_id(0) * here + i)
        for h in range(2):
            low = (2 * i + h) * half
            for core, out in enumerate(outs):

                @pl.when(k % 2 == core)
                def _():
                    out[at[1] ^ h, k // 2] = total[low : low + half]


def gate_up_grad(token_blocks, grad_blocks, me, s):
    size = lax.axis_size("fsdp")
    unit = 2 * FF // size
    padded = grad_blocks[0].shape[1]
    half = D // size // 2
    count = len(token_blocks)
    rows = token_blocks[0].shape[0]
    tile = 768
    return pl.pallas_call(
        functools.partial(grad_kernel, count, unit),
        out_shape=[jax.ShapeDtypeStruct((2, size // 2, half, unit), bf16)] * 2,
        grid=(D // tile,),
        in_specs=[pl.BlockSpec(memory_space=pltpu.SMEM)]
        + [pl.BlockSpec((rows, tile), lambda i: (0, i))] * count
        + [pl.BlockSpec((rows, padded), lambda i: (0, 0))] * count,
        out_specs=[pl.BlockSpec(memory_space=pltpu.VMEM)] * 2,
        compiler_params=pltpu.CompilerParams(vmem_limit_bytes=VMEM),
        cost_estimate=pl.CostEstimate(
            flops=2 * count * rows * D * padded,
            bytes_accessed=2 * count * rows * (D + padded) + 4 * D * unit,
            transcendentals=0,
        ),
    )(jnp.stack([me, s]).astype(jnp.int32), *token_blocks, *grad_blocks)


def spread_kernel(unit, where, blocks, out, held):
    for i in range(blocks.shape[0]):
        held[where[i]] = blocks[i]
    for chip in range(blocks.shape[0]):
        out[:, chip * unit : (chip + 1) * unit] = held[chip]


def widen_kernel(at, gate, up, other_gate, other_up, out):
    for ref, other, low in ((gate, other_gate, 0), (up, other_up, FF)):
        out[at[0], :, low : low + FF] = ref[...].astype(f32)
        out[1 - at[0], :, low : low + FF] = other[...].astype(f32)


def unshuffle_part(terms, order, me):
    half, unit = terms[0].shape[2:]
    (got,) = yield [(CORE, terms[1])]
    total = add(terms[0], got)
    (got,) = yield [("y", total[1].astype(bf16))]
    total = add(total[0], got).astype(bf16)
    blocks, marks = yield from exchange_blocks(total, order)
    mine = whole_call(
        functools.partial(spread_kernel, unit),
        jax.ShapeDtypeStruct((half, FF), bf16),
        [(me ^ f) // 2 for f in marks],
        [blocks],
        scratch=[pltpu.VMEM(blocks.shape, bf16)],
    )
    (other,) = yield [("y", mine)]
    return mine, other


def widen_gate_up(parts, s):
    mine, others = zip(*parts)
    half = mine[0].shape[0]
    whole = whole_call(
        widen_kernel,
        jax.ShapeDtypeStruct((2, half, 2 * FF), f32),
        [s],
        list(mine) + list(others),
    )
    return whole.reshape(2 * half, 2 * FF)


def sum_down(terms, core):
    give = lax.dynamic_index_in_dim(terms, 1 - core, 0, keepdims=False)
    (got,) = yield [(CORE, give)]
    part = add(lax.dynamic_index_in_dim(terms, core, 0, keepdims=False), got).astype(bf16)
    half = part.shape[0] // 2
    (low,) = yield [("y", part[:half])]
    (high,) = yield [("y", part[half:])]
    return add(part, join(low, high))


def rope_tables(positions):
    steps_half = jnp.arange(HD // 2, dtype=f32)
    inverse = rope_base ** (-2.0 * steps_half / HD)
    angles = positions.astype(f32)[:, None] * inverse
    cosines, sines = jnp.cos(angles), jnp.sin(angles)
    return join(cosines, cosines, axis=1), join(-sines, sines, axis=1)


def turn(head, cosines, sines):
    return head * cosines + pltpu.roll(head, HD // 2, 1) * sines


def rms_scale(values):
    return lax.rsqrt(jnp.mean(values * values, axis=-1, keepdims=True) + norm_eps)


def norm_backward(grad_normed, values, gain):
    scale_rows = rms_scale(values)
    scaled = grad_normed * gain
    gain_part = jnp.sum(grad_normed * values * scale_rows, axis=0, keepdims=True)
    grad_values = scale_rows * scaled - values * scale_rows**3 * jnp.mean(
        scaled * values, axis=-1, keepdims=True
    )
    return grad_values, gain_part


def head_at(index):
    return slice(index * HD, (index + 1) * HD)


def masks(second, ids_col, ids_row, other_row):
    shape = (ids_col.shape[0], ids_row.shape[1])
    rows = lax.broadcasted_iota(jnp.int32, shape, 0)
    cols = lax.broadcasted_iota(jnp.int32, shape, 1)
    near = (ids_col[...] == ids_row[...]) & (rows >= cols)
    far = (ids_col[...] == other_row[...]) & (rows + shape[0] * second >= shape[0])
    return near, far


def project_kernel(at, inputs, gain, weight, bias, cosines, sines, normed, queries, kv):
    values = inputs[...].astype(f32)
    rows = (values * rms_scale(values) * gain[...]).astype(bf16)
    normed[...] = rows
    projected = dot(rows, weight[...]) + bias[...]
    cos, sin = cosines[...], sines[...]
    for head in range(HQ):
        queries[:, head_at(head)] = turn(projected[:, head_at(head)], cos, sin).astype(bf16)
    for head in range(KV):
        kv[:, head_at(head)] = turn(projected[:, head_at(HQ + head)], cos, sin).astype(bf16)
    kv[:, KW:] = projected[:, QW + KW :].astype(bf16)


def attend_kernel(
    at, inputs, queries, kv, other, ids_col, ids_row, other_row, weight, gain,
    attended, logs, middle, normed,
):
    near, far = masks(at[0], ids_col, ids_row, other_row)
    factor = HD ** (-0.5)
    lanes = lax.broadcasted_iota(jnp.int32, logs.shape, 1)
    kept = jnp.zeros(logs.shape, f32)
    for head in range(HQ):
        k, v = head_at(head // GROUP), head_at(KV + head // GROUP)
        q = queries[:, head_at(head)]
        first = jnp.where(near, dot_t(q, kv[:, k]) * factor, -1e30)
        second = jnp.where(far, dot_t(q, other[:, k]) * factor, -1e30)
        peak = jnp.maximum(
            jnp.max(first, axis=-1, keepdims=True), jnp.max(second, axis=-1, keepdims=True)
        )
        total = jnp.sum(jnp.exp(first - peak), axis=-1, keepdims=True)
        total = total + jnp.sum(jnp.exp(second - peak), axis=-1, keepdims=True)
        log_total = peak + jnp.log(total)
        kept = jnp.where(lanes == head, log_total, kept)
        out = dot(jnp.exp(first - log_total).astype(bf16), kv[:, v])
        out = out + dot(jnp.exp(second - log_total).astype(bf16), other[:, v])
        attended[:, head_at(head)] = out.astype(bf16)
    logs[...] = kept
    rows = inputs[...].astype(f32) + dot(attended[...], weight[...])
    middle[...] = rows
    normed[...] = (rows * rms_scale(rows) * gain[...]).astype(bf16)


def attend_back_kernel(
    at, grad_normed, middle, gain, cotangent, weight, queries, kv, other,
    ids_col, ids_row, other_row, logs, cosines, sines,
    grad_middle, grad_branch, gain_part, grad_queries, keep, give,
):
    grad_values, part = norm_backward(grad_normed[...], middle[...], gain[...])
    gain_part[...] = part
    grad_rows = cotangent[...].astype(f32) + grad_values
    grad_middle[...] = grad_rows
    branch = grad_rows.astype(bf16)
    grad_branch[...] = branch
    grad_out = dot_t(branch, weight[...]).astype(bf16)
    near, far = masks(at[0], ids_col, ids_row, other_row)
    factor = HD ** (-0.5)
    lanes = lax.broadcasted_iota(jnp.int32, logs.shape, 1)
    cos, sin = cosines[...], -sines[...]
    for group in range(KV):
        k, v = head_at(group), head_at(KV + group)
        sums = [jnp.zeros((kv.shape[0], HD), f32) for _ in range(4)]
        for head in range(group * GROUP, (group + 1) * GROUP):
            q, g = queries[:, head_at(head)], grad_out[:, head_at(head)]
            log_total = jnp.sum(
                jnp.where(lanes == head, logs[...], 0.0), axis=-1, keepdims=True
            )
            first = jnp.where(near, dot_t(q, kv[:, k]) * factor, -1e30)
            second = jnp.where(far, dot_t(q, other[:, k]) * factor, -1e30)
            first, second = jnp.exp(first - log_total), jnp.exp(second - log_total)
            grad_first, grad_second = dot_t(g, kv[:, v]), dot_t(g, other[:, v])
            balance = jnp.sum(first * grad_first, axis=-1, keepdims=True)
            balance = balance + jnp.sum(second * grad_second, axis=-1, keepdims=True)
            grad_first = (first * (grad_first - balance)).astype(bf16)
            grad_second = (second * (grad_second - balance)).astype(bf16)
            grad_q = (dot(grad_first, kv[:, k]) + dot(grad_second, other[:, k])) * factor
            grad_q = turn(grad_q.astype(bf16).astype(f32), cos, sin)
            grad_queries[:, head_at(head)] = grad_q.astype(bf16)
            sums[0] = sums[0] + t_dot(grad_first, q)
            sums[1] = sums[1] + t_dot(first.astype(bf16), g)
            sums[2] = sums[2] + t_dot(grad_second, q)
            sums[3] = sums[3] + t_dot(second.astype(bf16), g)
        keep[:, k] = sums[0] * factor
        keep[:, v] = sums[1]
        give[:, k] = (sums[2] * factor).astype(bf16)
        give[:, v] = sums[3].astype(bf16)


def project_back_kernel(
    at, grad_queries, keep, got, cosines, sines, weight, inputs, gain, grad_middle,
    grad_projected, input_grad, gain_part, bias_part,
):
    grad_kv = (keep[...] + got[...].astype(f32)).astype(bf16)
    cos, sin = cosines[...], -sines[...]
    grad_projected[:, :QW] = grad_queries[...]
    for head in range(KV):
        grad_k = turn(grad_kv[:, head_at(head)].astype(f32), cos, sin)
        grad_projected[:, head_at(HQ + head)] = grad_k.astype(bf16)
    grad_projected[:, QW + KW :] = grad_kv[:, KW:]
    rows = grad_projected[...]
    bias_part[...] = jnp.sum(rows.astype(f32), axis=0, keepdims=True)
    grad_normed = dot_t(rows, weight[...])
    grad_values, part = norm_backward(grad_normed, inputs[...].astype(f32), gain[...])
    gain_part[...] = part
    input_grad[...] = grad_middle[...] + grad_values


def feed_kernel(
    tokens_a, tokens_b, cot_a, cot_b, gate_weight, up_weight, down_weight,
    hidden, grad_gate, grad_up, tokens, cotangent, back_a, back_b, total,
):
    step, steps = pl.program_id(0), pl.num_programs(0)
    half = tokens_a.shape[0]

    @pl.when(step == 0)
    def _():
        tokens[:half], tokens[half:] = tokens_a[...], tokens_b[...]
        cotangent[:half], cotangent[half:] = cot_a[...], cot_b[...]
        total[...] = jnp.zeros_like(total)

    gate = dot(tokens[...], gate_weight[...])
    up = dot(tokens[...], up_weight[...])
    grad_hidden = dot_t(cotangent[...], down_weight[...])
    sigmoid = jax.nn.sigmoid(gate)
    silu = gate * sigmoid
    hidden[...] = (silu * up).astype(bf16)
    gate_rows = (grad_hidden * up * sigmoid * (1.0 + gate * (1.0 - sigmoid))).astype(bf16)
    up_rows = (grad_hidden * silu).astype(bf16)
    grad_gate[...] = gate_rows
    grad_up[...] = up_rows
    total[...] += dot_t(
        join(gate_rows, up_rows, axis=1), join(gate_weight[...], up_weight[...], axis=1)
    )

    @pl.when(step == steps - 1)
    def _():
        back_a[...] = total[:half].astype(back_a.dtype)
        back_b[...] = total[half:].astype(back_b.dtype)


def feed_forward(tokens, cotangent, gate_up_weight, down_weight, back_type):
    half = tokens[0].shape[0]
    if half > 256 and half % 256 == 0:
        parts = [
            feed_forward(
                [v[low : low + 256] for v in tokens],
                [v[low : low + 256] for v in cotangent],
                gate_up_weight,
                down_weight,
                back_type,
            )
            for low in range(0, half, 256)
        ]
        halves = [
            join(*[part[i][low : low + 256] for low in (0, 256) for part in parts])
            for i in range(5)
        ]
        return (*halves, *[join(*[part[i] for part in parts]) for i in (5, 6)])
    rows = 2 * half
    padded = down_weight.shape[0]
    tile = 384
    steps = padded // tile
    whole = pl.BlockSpec((rows, D), lambda j: (0, 0))
    piece = pl.BlockSpec((half, D), lambda j: (0, 0))
    part = pl.BlockSpec((rows, tile), lambda j: (0, j))
    units = jax.ShapeDtypeStruct((rows, padded), bf16)
    lines = jax.ShapeDtypeStruct((rows, D), bf16)
    back = jax.ShapeDtypeStruct((half, D), back_type)
    return pl.pallas_call(
        feed_kernel,
        grid=(steps,),
        out_shape=(units, units, units, lines, lines, back, back),
        in_specs=[piece] * 4
        + [
            pl.BlockSpec((D, tile), lambda j: (0, j)),
            pl.BlockSpec((D, tile), lambda j: (0, j + steps)),
            pl.BlockSpec((tile, D), lambda j: (j, 0)),
        ],
        out_specs=(part, part, part, whole, whole, piece, piece),
        scratch_shapes=[pltpu.VMEM((rows, D), f32)],
        compiler_params=pltpu.CompilerParams(vmem_limit_bytes=VMEM),
        cost_estimate=pl.CostEstimate(
            flops=10 * rows * D * padded,
            bytes_accessed=6 * D * padded + 8 * rows * D + 6 * rows * padded,
            transcendentals=rows * padded,
        ),
    )(*tokens, *cotangent, gate_up_weight, gate_up_weight, down_weight)


def pair_kernel(at, own, other, out):
    rows = own.shape[0]
    for core, first, second in ((0, own, other), (1, other, own)):

        @pl.when(at[0] == core)
        def _():
            out[:rows], out[rows : 2 * rows] = first[...], second[...]

    if out.shape[0] > 2 * rows:
        out[2 * rows :] = jnp.zeros((out.shape[0] - 2 * rows, out.shape[1]), out.dtype)


def body(
    inputs,
    positions,
    segments,
    gain_one,
    qkv_weight,
    qkv_bias,
    out_weight,
    gain_two,
    gate_up_weight,
    down_weight,
    cotangent,
):
    tokens = inputs.shape[0] * inputs.shape[1]
    size = lax.axis_size("fsdp")
    me = lax.axis_index("fsdp")
    s = lax.axis_index("seq")
    unit = 2 * FF // size
    padded = -(-unit // 384) * 384

    lanes = Lanes()
    far = far_bits()
    core = me % 2
    input_rows = inputs.reshape(tokens, D)
    grad_rows = cotangent.reshape(tokens, D)
    gate_blocks, up_blocks = split_gate_up(gate_up_weight, me, s)
    cot_blocks, token_blocks = [], []
    qkv = Move(gather_weight(qkv_weight, me, s))
    out = Move(gather_weight_plain(out_weight, me))
    gate = Move(shuffle_part(gate_blocks, [X] + far + [Z]))
    up = Move(shuffle_part(up_blocks, [X] + far + [Z]))
    cot = Move(gather_tokens(grad_rows, cot_blocks))
    down = Move(swap(CORE, down_weight))
    lanes.round(qkv, up)
    lanes.round(qkv, (out, 2), gate)
    lanes.round(qkv)
    lanes.round(qkv, out, (gate, 2))
    lanes.round(qkv, out)
    (qkv_full,) = lanes.drain(qkv)

    rows_bf16 = jax.ShapeDtypeStruct((tokens, D), bf16)
    rows_f32 = jax.ShapeDtypeStruct((tokens, D), f32)
    cosines, sines = rope_tables(positions.reshape(tokens))
    ids = segments.reshape(2, tokens)
    ids_row = lax.dynamic_index_in_dim(ids, s, 0)
    other_row = lax.dynamic_index_in_dim(ids, 1 - s, 0)
    ids_col = ids_row.reshape(tokens, 1)
    gain_one, gain_two = gain_one[None], gain_two[None]
    normed, queries, kv = whole_call(
        project_kernel,
        (rows_bf16, rows_bf16, jax.ShapeDtypeStruct((tokens, 2 * KW), bf16)),
        [s],
        [input_rows, gain_one, qkv_full, qkv_bias[None], cosines, sines],
        flops=2 * tokens * D * (QW + 2 * KW),
    )
    lanes.beside(kv)
    other = Move(swap("y", kv))
    lanes.round(other, out, (up, 2), gate)
    other_kv, out_full = lanes.drain(other, out)
    attended, logs, middle, normed_two = whole_call(
        attend_kernel,
        (rows_bf16, jax.ShapeDtypeStruct((tokens, HD), f32), rows_f32, rows_bf16),
        [s],
        [input_rows, queries, kv, other_kv, ids_col, ids_row, other_row, out_full, gain_two],
        flops=2 * tokens * D * (D + 8 * tokens),
    )

    lanes.beside(normed_two)
    token = Move(gather_tokens(normed_two, token_blocks))
    lanes.round(token, gate, up)
    lanes.round(token, (cot, 2), (up, 2), down)
    lanes.round(token, gate)
    lanes.round(cot, up)
    parts = lanes.drain(gate, up)
    gate_up_full = weave_gate_up(parts, me, s)
    (other_down,) = lanes.drain(down)
    down_full = whole_call(
        pair_kernel,
        jax.ShapeDtypeStruct((padded, D), bf16),
        [core],
        [down_weight, other_down],
    )
    lanes.drain(token, cot)
    early = feed_forward(token_blocks[0], cot_blocks[0], gate_up_full, down_full, f32)
    last = feed_forward(
        [after(token_blocks[1][0], early[5]), token_blocks[1][1]],
        cot_blocks[1],
        gate_up_full,
        down_full,
        bf16,
    )
    back = Move(scatter_tokens(early[5:], last[5:]))
    lanes.round(back)

    half = last[5].shape[0]
    gate_terms = gate_up_grad([early[3], last[3]], [early[1], last[1]], me, s)
    out_terms = [[dot(v[0][:half], down_full), dot(v[0][half:], down_full)] for v in (early, last)]
    gate = Move(unshuffle_part(gate_terms, far + [Z, X], me))
    result = Move(scatter_tokens(out_terms[0], [term.astype(bf16) for term in out_terms[1]]))
    lanes.round(back, gate)
    up_terms = gate_up_grad(
        [early[3], last[3]], [lanes.hold(early[2]), lanes.hold(last[2])], me, s
    )
    up = Move(unshuffle_part(up_terms, [X, Z] + far, me))
    lanes.round(back, gate, result, up)
    down_terms = t_dot(lanes.hold(early[0]), early[4]) + t_dot(lanes.hold(last[0]), last[4])
    down_terms = down_terms[:unit].astype(bf16).reshape(2, unit // 2, D)
    down = Move(sum_down(down_terms, core))
    (grad_normed_two,) = lanes.drain(back)
    lanes.round(result, (gate, 2), (up, 2))

    grad_middle, grad_branch, gain_two_part, grad_queries, keep, give = whole_call(
        attend_back_kernel,
        (
            rows_f32,
            rows_bf16,
            jax.ShapeDtypeStruct((1, D), f32),
            rows_bf16,
            jax.ShapeDtypeStruct((tokens, 2 * KW), f32),
            jax.ShapeDtypeStruct((tokens, 2 * KW), bf16),
        ),
        [s],
        [grad_normed_two, middle, gain_two, grad_rows, out_full, queries, kv, other_kv]
        + [ids_col, ids_row, other_row, logs, cosines, sines],
        flops=2 * tokens * D * (D + 20 * tokens),
    )
    other = Move(swap("y", give))
    lanes.more(other)
    (got,) = lanes.drain(other)
    out = Move(scatter_weight(attended, grad_branch, me, s))
    grad_projected, input_grad, gain_one_part, bias_part = whole_call(
        project_back_kernel,
        (
            jax.ShapeDtypeStruct((tokens, QW + 2 * KW), bf16),
            rows_f32,
            jax.ShapeDtypeStruct((1, D), f32),
            jax.ShapeDtypeStruct((1, QW + 2 * KW), f32),
        ),
        [s],
        [grad_queries, keep, got, cosines, sines, qkv_full, input_rows, gain_one, grad_middle],
        flops=2 * tokens * D * (QW + 2 * KW),
    )
    lanes.beside(grad_projected)
    qkv = Move(scatter_weight(normed, grad_projected, me, s))
    sums = Move(sum_everywhere(join(gain_one_part[0], bias_part[0], gain_two_part[0])))
    lanes.round(qkv, down)
    lanes.round(qkv, (result, 2), out, down)
    lanes.round(qkv, gate, up, sums)
    lanes.round(qkv, gate, up, down, sums)
    lanes.round(qkv, out, (up, 2), (gate, 2), sums)
    lanes.round(qkv, out, sums)
    lanes.round(out, up, sums)
    qkv_weight_total, out_weight_total, down_total, out_sum, sums, *parts = lanes.drain(
        qkv, out, down, result, sums, gate, up
    )
    gate_up_total = widen_gate_up(parts, s)
    output = (middle + out_sum).astype(bf16).reshape(inputs.shape)
    width = bias_part.shape[1]
    return (
        output,
        input_grad.reshape(inputs.shape),
        sums[:D],
        qkv_weight_total,
        sums[D : D + width],
        out_weight_total,
        sums[D + width :],
        gate_up_total,
        down_total,
    )


def solution(mesh):
    placed = (
        P("fsdp", "seq", None),
        P("fsdp", "seq"),
        P("fsdp", None),
        P(),
        P("fsdp", None),
        P(),
        P("fsdp", None),
        P(),
        P("fsdp", None),
        P("fsdp", None),
        P("fsdp", "seq", None),
    )
    return jax.shard_map(
        body,
        mesh=mesh,
        in_specs=placed,
        out_specs=(
            P("fsdp", "seq", None),
            P("fsdp", "seq", None),
            P(),
            P("fsdp", None),
            P(),
            P("fsdp", None),
            P(),
            P("fsdp", None),
            P("fsdp", None),
        ),
        check_vma=False,
    )
```

time: 2640 us -> 529 us (0.20)
  waiting for transfers between devices: 2320 us -> 224 us
  matrix products: 183 us -> 26.3 us
  Pallas kernels: 0 us -> 103 us
  starting transfers between devices: 21.4 us -> 85.6 us
  blocking collectives: 58.2 us -> 0 us
  other arithmetic: 11.9 us -> 43.9 us
    reduce_scatter x4 -> x0, waiting for transfers between devices: 1620 us -> none  [weight_grad(): lax.psum_scatter(lax.dot_general(left, grad, (((0,), (0,)), ((), ())), pr...]
    all_gather x4 -> x0, waiting for transfers between devices: 459 us -> none  [contract_rows(): lax.all_gather(weight, 'fsdp', axis=0, tiled=True)]
    ppermute x0 -> x86, waiting for transfers between devices: none -> 224 us  [the longest x68 191 us: more(): value = lax.ppermute(value, 'fsdp', [(i, i ^ link) for i in range(size)])]
    psum x1 -> x0, waiting for transfers between devices: 215 us -> none  [body(): lax.psum((qkv_part, out_part, gate_up_part, down_part), 'seq')]
    dot_general x18 -> x10, matrix products: 183 us -> 26.3 us  [the longest x8 16.5 us: dot(): return jnp.dot(left, right, preferred_element_type=f32)]
    pallas_call x0 -> x18, Pallas kernels: none -> 103 us  [the longest x14 51.1 us: whole_call(): pl.pallas_call(kernel, out_shape=out_shape, in_specs=[pl.BlockSpec(memory...]
    ppermute x0 -> x86, starting transfers between devices: none -> 85.6 us  [the longest x68 67.2 us: more(): value = lax.ppermute(value, 'fsdp', [(i, i ^ link) for i in range(size)])]
    psum x1 -> x0, blocking collectives: 39.5 us -> none  [body(): lax.psum((gain_one_part, bias_part, gain_two_part), ('seq', 'fsdp'))]
  transfers between devices with their start and end apart: 15 -> 86, of which waited for: 13 -> 45; matrix products, arithmetic and copies ran while one was open for 6% -> 18% of each run, Pallas kernels for 0% -> 16%
where the time goes in v2:
time: 529 us; the launch traced here: 525 us
  waiting for transfers between devices  224 us (42%)
  Pallas kernels  103 us (19%)
  starting transfers between devices  85.6 us (16%)
  other arithmetic  43.9 us (8%)
  local copies, waits for them, and re-layouts  39.1 us (7%)
  matrix products  26.3 us (5%)
    ppermute x68, waiting for transfers between devices, more(): value = lax.ppermute(value, 'fsdp', [(i, i ^ link) for i in range(size)])  191 us
    ppermute x68, starting transfers between devices, more(): value = lax.ppermute(value, 'fsdp', [(i, i ^ link) for i in range(size)])  67.2 us
    pallas_call x14, Pallas kernels, whole_call(): pl.pallas_call(kernel, out_shape=out_shape, in_specs=[pl.BlockSpec(memory...  51.1 us
    pallas_call x2, Pallas kernels, feed_forward(): pl.pallas_call(feed_kernel, grid=(steps,), out_shape=(units, units, units...  36.5 us
    ppermute x18, waiting for transfers between devices, more(): value = lax.ppermute(value, 'seq', [(0, 1), (1, 0)])  32.9 us
    ppermute x18, starting transfers between devices, more(): value = lax.ppermute(value, 'seq', [(0, 1), (1, 0)])  18.4 us
    unnamed x179, local copies, waits for them, and re-layouts  17.1 us
    dot_general x8, matrix products, dot(): return jnp.dot(left, right, preferred_element_type=f32)  16.5 us
  transfers between devices with their start and end apart: 86, of which 45 were waited for; matrix products, arithmetic and copies ran while one was open for 18% of the time, Pallas kernels for 16%

profile of v2, /device:TPU:0, one launch (start us, length us, event | category | flops | bytes accessed | tf_op | source)
XLA Modules:
  0.0 525.5 jit_solution(14650258572638221127)
XLA Ops:
  1.7 4.1 collective-permute-start
  12.0 2.9 collective-permute-done
  14.9 6.4 %collective-permute-done.1 = bf16[1,2,2,48,1120]{4,3,0,2,1:T(8,128)(2,1)S(1)} collective-permute-done((bf16[1,2,2,48,1120]{4,3,0,2,1:T(8,128)(2,1)S(1)}, bf16[1,2,2,48,1120]{4,3,0,2,1:T(8,128)(2,1)S(1)}, u32[]{:S(2)}, u32[]{:S(2)}) %collective-permute-start.1) | collective-permute-done | bytes 430112 | tf_op jit(solution)/shard_map/ppermute | solution.py:84
  26.9 7.7 %collective-permute-done.3 = bf16[2,48,640]{2,1,0:T(8,128)(2,1)S(1)} collective-permute-done((bf16[2,48,640]{2,1,0:T(8,128)(2,1)S(1)}, bf16[2,48,640]{2,1,0:T(8,128)(2,1)S(1)}, u32[]{:S(2)}, u32[]{:S(2)}) %collective-permute-start.3) | collective-permute-done | bytes 122912 | tf_op jit(solution)/shard_map/ppermute | solution.py:84
  41.1 3.2 collective-permute-done.6
  51.4 9.1 %collective-permute-done.11 = bf16[8,48,640]{2,1,0:T(8,128)(2,1)S(1)} collective-permute-done((bf16[8,48,640]{2,1,0:T(8,128)(2,1)S(1)}, bf16[8,48,640]{2,1,0:T(8,128)(2,1)S(1)}, u32[]{:S(2)}, u32[]{:S(2)}) %collective-permute-start.11) | collective-permute-done | bytes 491552 | tf_op jit(solution)/shard_map/ppermute | solution.py:84
  63.7 4.5 collective-permute-done.13
  76.6 5.1 shard_map.179
  81.7 4.1 shard_map.180
  85.9 3.4 collective-permute-done.18
  89.2 5.7 %collective-permute-done.17 = bf16[4,96,768]{2,1,0:T(8,128)(2,1)S(1)} collective-permute-done((bf16[4,96,768]{2,1,0:T(8,128)(2,1)S(1)}, bf16[4,96,768]{2,1,0:T(8,128)(2,1)S(1)}, u32[]{:S(2)}, u32[]{:S(2)}) %collective-permute-start.17) | collective-permute-done | bytes 589856 | tf_op jit(solution)/shard_map/ppermute | solution.py:84
  95.3 3.8 collective-permute-done.16
  105.2 4.1 shard_map.181
  109.4 7.7 %shard_map.182 = (bf16[128,1536]{1,0:T(8,128)(2,1)S(1)}, f32[128,128]{1,0:T(8,128)S(1)}, f32[128,1536]{1,0:T(8,128)S(1)}, bf16[128,1536]{1,0:T(8,128)(2,1)S(1)}) custom-call(s32[1]{0:T(128)} %bitcast.at, bf16[128,1536]{1,0:T(8,128)(2,1)S(1)} %bitcast.321, bf16[128,1536]{1,0:T(8,128)(2,1)S(1)} %get-tuple-element.159.queries, ...), custom_call_target="tpu_custom_call" | custom-call | flops 1006632960 | bytes 7413248 | tf_op jit(solution)/shard_map/pallas_call | solution.py:134
  117.2 5.0 collective-permute-done.21
  123.4 3.7 collective-permute-done.23
  129.9 15.1 %collective-permute-done.22 = bf16[1,128,1536]{2,1,0:T(8,128)(2,1)S(1)} collective-permute-done((bf16[1,128,1536]{2,1,0:T(8,128)(2,1)S(1)}, bf16[1,128,1536]{2,1,0:T(8,128)(2,1)S(1)}, u32[]{:S(2)}, u32[]{:S(2)}) %collective-permute-start.22) | collective-permute-done | bytes 393248 | tf_op jit(solution)/shard_map/ppermute | solution.py:84
  151.9 7.0 %collective-permute-done.26 = bf16[2,64,1536]{2,1,0:T(8,128)(2,1)S(1)} collective-permute-done((bf16[2,64,1536]{2,1,0:T(8,128)(2,1)S(1)}, bf16[2,64,1536]{2,1,0:T(8,128)(2,1)S(1)}, u32[]{:S(2)}, u32[]{:S(2)}) %collective-permute-start.26) | collective-permute-done | bytes 393248 | tf_op jit(solution)/shard_map/ppermute | solution.py:84
  168.9 13.7 %collective-permute-done.29.refs_4_ = bf16[8,48,1120]{2,1,0:T(8,128)(2,1)S(1)} collective-permute-done((bf16[8,48,1120]{2,1,0:T(8,128)(2,1)}, bf16[8,48,1120]{2,1,0:T(8,128)(2,1)S(1)}, u32[]{:S(2)}, u32[]{:S(2)}) %collective-permute-start.29) | collective-permute-done | bytes 860192 | tf_op jit(solution)/shard_map/ppermute | solution.py:82
  185.2 6.1 %collective-permute-done.28 = bf16[1,128,1536]{2,1,0:T(8,128)(2,1)} collective-permute-done((bf16[1,128,1536]{2,1,0:T(8,128)(2,1)S(1)}, bf16[1,128,1536]{2,1,0:T(8,128)(2,1)}, u32[]{:S(2)}, u32[]{:S(2)}) %collective-permute-start.28) | collective-permute-done | bytes 393248 | tf_op jit(solution)/shard_map/ppermute | solution.py:84
  215.8 2.9 collective-permute-done.35
  219.7 5.8 %shard_map.183 = bf16[32,48,2304]{2,1,0:T(8,128)(2,1)} custom-call(s32[64]{0:T(128)S(1)} %stack.463.where, bf16[8,48,1120]{2,1,0:T(8,128)(2,1)S(1)} %pad_maximum_fusion.5.refs_0_, bf16[8,48,1120]{2,1,0:T(8,128)(2,1)S(1)} %collective-permute-done.24.refs_1_, bf16[16,48,1120]{2,1,0:T(8,128)(2,1)} %collective-permute-done.33.refs_2_, ...), custom_call_target="tpu_custom_call" | custom-call | bytes 13959168 | tf_op jit(solution)/shard_map/pallas_call | solution.py:134
  225.5 18.5 %shard_map.185 = (bf16[512,1152]{1,0:T(8,128)(2,1)S(1)}, bf16[512,1152]{1,0:T(8,128)(2,1)S(1)}, bf16[512,1152]{1,0:T(8,128)(2,1)}, bf16[512,1536]{1,0:T(8,128)(2...) custom-call(bf16[256,1536]{1,0:T(8,128)(2,1)} %bitcast.80.tokens_a, ...), custom_call_target="tpu_custom_call" | custom-call | flops 9059696640 | bytes 20447232 | tf_op jit(solution)/shard_map/pallas_call | solution.py:683
  244.0 18.0 %shard_map.186 = (bf16[512,1152]{1,0:T(8,128)(2,1)S(1)}, bf16[512,1152]{1,0:T(8,128)(2,1)}, bf16[512,1152]{1,0:T(8,128)(2,1)}, bf16[512,1536]{1,0:T(8,128)(2,1)}...) custom-call(bf16[256,1536]{1,0:T(8,128)(2,1)} %bitcast.87.tokens_a, ...), custom_call_target="tpu_custom_call" | custom-call | flops 9059696640 | bytes 20447232 | tf_op jit(solution)/shard_map/pallas_call | solution.py:683
  269.5 7.8 %shard_map.187 = (bf16[2,8,48,1120]{3,2,1,0:T(8,128)(2,1)}, bf16[2,8,48,1120]{3,2,1,0:T(8,128)(2,1)}) custom-call(s32[2]{0:T(128)S(1)} %get-tuple-element.333.at, bf16[512,1536]{1,0:T(8,128)(2,1)S(1)} %copy-done.36, bf16[512,1536]{1,0:T(8,128)(2,1)S(1)} %copy-done.37, bf16[512,1152]{1,0:T(8,128)(2,1)S(1)} %get-tuple-element.203.refs_2_, ...), custom_call_target="tpu_custom_call" | custom-call | flops 3623878656 | bytes 12386304 | tf_op jit(solution)/shard_map/pallas_call | solution.py:407
  277.3 2.7 collective-permute-done.39
  280.3 3.1 collective-permute-done.40
  287.6 7.8 %shard_map.188 = (bf16[2,8,48,1120]{3,2,1,0:T(8,128)(2,1)}, bf16[2,8,48,1120]{3,2,1,0:T(8,128)(2,1)}) custom-call(s32[2]{0:T(128)S(1)} %get-tuple-element.333.at, bf16[512,1536]{1,0:T(8,128)(2,1)S(1)} %copy-done.36, bf16[512,1536]{1,0:T(8,128)(2,1)S(1)} %copy-done.37, bf16[512,1152]{1,0:T(8,128)(2,1)S(1)} %copy-done.38, bf16[512,1152]{1,0:T(8,128)(2,1)S(1)} %copy-done.39), custom_call_target="tpu_custom_call" | custom-call | flops 3623878656 | bytes 12386304 | tf_op jit(solution)/shard_map/pallas_call | solution.py:407
  304.2 5.0 fusion.82
  309.2 4.9 fusion.81
  314.1 6.0 %fusion = bf16[1120,1536]{1,0:T(8,128)(2,1)S(1)} fusion(f32[1152,1536]{1,0:T(8,128)} %fusion.82, f32[1152,1536]{1,0:T(8,128)} %fusion.81), kind=kLoop, calls=%fused_computation.1 | loop fusion | flops 3440640 | bytes 17203200 | tf_op jit(solution)/shard_map/convert.13
  322.7 8.5 %shard_map.189 = (f32[128,1536]{1,0:T(8,128)S(1)}, bf16[128,1536]{1,0:T(8,128)(2,1)S(1)}, f32[1,1536]{1,0:T(1,128)S(1)}, bf16[128,1536]{1,0:T(8,128)(2,1)S(1)}, ...) custom-call(s32[1]{0:T(128)} %bitcast.at, f32[128,1536]{1,0:T(8,128)S(1)} %fusion.26.grad_normed, ...), custom_call_target="tpu_custom_call" | custom-call | flops 1610612736 | bytes 9516544 | tf_op jit(solution)/shard_map/pallas_call | solution.py:134
  335.0 3.7 convolution_add_fusion.1
  340.5 2.7 convolution_add_fusion
  355.5 6.1 %shard_map.190 = (bf16[128,2048]{1,0:T(8,128)(2,1)S(1)}, f32[128,1536]{1,0:T(8,128)}, f32[1,1536]{1,0:T(1,128)S(1)}, f32[1,2048]{1,0:T(1,128)S(1)}) custom-call(s32[1]{0:T(128)} %bitcast.at, bf16[128,1536]{1,0:T(8,128)(2,1)S(1)} %copy-done.26, f32[128,512]{1,0:T(8,128)S(1)} %copy-done.30, bf16[128,512]{1,0:T(8,128)(2,1)S(1)} %collective-permute-done.50.got, ...), custom_call_target="tpu_custom_call" | custom-call | flops 805306368 | bytes 9719808 | tf_op jit(solution)/shard_map/pallas_call | solution.py:134
  363.6 2.7 collective-permute-done.49
  369.4 2.6 collective-permute-done.52
  373.2 3.1 collective-permute-done.53
  386.1 12.6 %collective-permute-done.56 = bf16[1,128,1536]{2,1,0:T(8,128)(2,1)S(1)} collective-permute-done((bf16[1,128,1536]{2,1,0:T(8,128)(2,1)S(1)}, bf16[1,128,1536]{2,1,0:T(8,128)(2,1)S(1)}, u32[]{:S(2)}, u32[]{:S(2)}) %collective-permute-start.56) | collective-permute-done | bytes 393248 | tf_op jit(solution)/shard_map/ppermute | solution.py:84
  401.9 8.9 %collective-permute-done.58 = bf16[2,2,2,48,1024]{4,3,2,1,0:T(8,128)(2,1)S(1)} collective-permute-done((bf16[2,2,2,48,1024]{4,3,2,1,0:T(8,128)(2,1)S(1)}, bf16[2,2,2,48,1024]{4,3,2,1,0:T(8,128)(2,1)S(1)}, u32[]{:S(2)}, u32[]{:S(2)}) %collective-permute-start.58) | collective-permute-done | bytes 786464 | tf_op jit(solution)/shard_map/ppermute | solution.py:84
  416.7 7.7 %collective-permute-done.62 = bf16[2,2,48,1024]{3,2,1,0:T(8,128)(2,1)S(1)} collective-permute-done((bf16[2,2,48,1024]{3,2,1,0:T(8,128)(2,1)S(1)}, bf16[2,2,48,1024]{3,2,1,0:T(8,128)(2,1)S(1)}, u32[]{:S(2)}, u32[]{:S(2)}) %collective-permute-start.62) | collective-permute-done | bytes 393248 | tf_op jit(solution)/shard_map/ppermute | solution.py:84
  424.7 8.7 %collective-permute-done.64 = bf16[2,2,48,1120]{3,2,0,1:T(8,128)(2,1)S(1)} collective-permute-done((bf16[2,2,48,1120]{3,2,0,1:T(8,128)(2,1)S(1)}, bf16[2,2,48,1120]{3,2,0,1:T(8,128)(2,1)S(1)}, u32[]{:S(2)}, u32[]{:S(2)}) %collective-permute-start.64) | collective-permute-done | bytes 430112 | tf_op jit(solution)/shard_map/ppermute | solution.py:84
  438.4 16.1 %collective-permute-done.67 = bf16[1,2,48,2048]{3,2,1,0:T(8,128)(2,1)S(1)} collective-permute-done((bf16[1,2,48,2048]{3,2,1,0:T(8,128)(2,1)S(1)}, bf16[1,2,48,2048]{3,2,1,0:T(8,128)(2,1)S(1)}, u32[]{:S(2)}, u32[]{:S(2)}) %collective-permute-start.67) | collective-permute-done | bytes 393248 | tf_op jit(solution)/shard_map/ppermute | solution.py:84
  467.5 4.7 collective-permute-done.73
  472.3 10.7 %collective-permute-done.74 = bf16[2,2,2,48,768]{4,3,2,1,0:T(8,128)(2,1)S(1)} collective-permute-done((bf16[2,2,2,48,768]{4,3,2,1,0:T(8,128)(2,1)S(1)}, bf16[2,2,2,48,768]{4,3,2,1,0:T(8,128)(2,1)S(1)}, u32[]{:S(2)}, u32[]{:S(2)}) %collective-permute-start.74) | collective-permute-done | bytes 589856 | tf_op jit(solution)/shard_map/ppermute | solution.py:84
  496.8 8.0 %collective-permute-done.82 = bf16[1,2,48,1536]{3,2,1,0:T(8,128)(2,1)S(1)} collective-permute-done((bf16[1,2,48,1536]{3,2,1,0:T(8,128)(2,1)S(1)}, bf16[1,2,48,1536]{3,2,1,0:T(8,128)(2,1)S(1)}, u32[]{:S(2)}, u32[]{:S(2)}) %collective-permute-start.82) | collective-permute-done | bytes 294944 | tf_op jit(solution)/shard_map/ppermute | solution.py:84
  504.9 8.8 %collective-permute-done.83.other_up = bf16[48,8960]{1,0:T(8,128)(2,1)S(1)} collective-permute-done((bf16[48,8960]{1,0:T(8,128)(2,1)S(1)}, bf16[48,8960]{1,0:T(8,128)(2,1)S(1)}, u32[]{:S(2)}, u32[]{:S(2)}) %collective-permute-start.83) | collective-permute-done | bytes 860192 | tf_op jit(solution)/shard_map/ppermute | solution.py:82
  521.0 3.3 shard_map.195
  (462 shorter events, 198.3 us)
Async XLA Ops:
  26.6 14.5 %collective-permute-start.7 = (bf16[1,96,1536]{2,1,0:T(8,128)(2,1)S(1)}, bf16[1,96,1536]{2,1,0:T(8,128)(2,1)S(1)}, u32[]{:S(2)}, u32[]{:S(2)}) collective-permute-start(bf16[1,96,1536]{2,1,0:T(8,128)(2,1)S(1)} %bitcast.376), channel_id=1, source_target_pairs={{0,8},{1,9},{2,10},{3,11},{4,12},{5,13},{6,14},{7,15},{8,0},{9,1},... | collective-permute-start | bytes 884744 | tf_op jit(solution)/shard_map/ppermute | solution.py:84
  46.5 14.1 %collective-permute-start.11 = (bf16[8,48,640]{2,1,0:T(8,128)(2,1)S(1)}, bf16[8,48,640]{2,1,0:T(8,128)(2,1)S(1)}, u32[]{:S(2)}, u32[]{:S(2)}) collective-permute-start(bf16[8,48,640]{2,1,0:T(8,128)(2,1)S(1)} %pad_maximum_fusion.21), channel_id=1, source_target_pairs={{0,4},{1,5},{2,6},{3,7},{4,0},{5,1},{6,2},{7,3},{8,12},{9,13},{10,... | collective-permute-start | bytes 1474568 | tf_op jit(solution)/shard_map/ppermute | solution.py:84
  46.5 16.3 %collective-permute-start.12 = (bf16[8,48,768]{2,1,0:T(8,128)(2,1)S(1)}, bf16[8,48,768]{2,1,0:T(8,128)(2,1)S(1)}, u32[]{:S(2)}, u32[]{:S(2)}) collective-permute-start(bf16[8,48,768]{2,1,0:T(8,128)(2,1)S(1)} %pad_maximum_fusion.17), channel_id=1, source_target_pairs={{0,2},{1,3},{2,0},{3,1},{4,6},{5,7},{6,4},{7,5},{8,10},{9,11},{10,... | collective-permute-start | bytes 1769480 | tf_op jit(solution)/shard_map/ppermute | solution.py:84
  48.2 14.9 %collective-permute-start.10 = (bf16[8,48,640]{2,1,0:T(8,128)(2,1)S(1)}, bf16[8,48,640]{2,1,0:T(8,128)(2,1)S(1)}, u32[]{:S(2)}, u32[]{:S(2)}) collective-permute-start(bf16[8,48,640]{2,1,0:T(8,128)(2,1)S(1)} %pad_maximum_fusion.20), channel_id=1, source_target_pairs={{0,16},{16,0},{1,17},{17,1},{2,18},{18,2},{3,19},{19,3},{4,20},{20... | collective-permute-start | bytes 1474568 | tf_op jit(solution)/shard_map/ppermute | solution.py:82
  48.8 19.4 %collective-permute-start.13 = (bf16[2,96,768]{2,1,0:T(8,128)(2,1)S(1)}, bf16[2,96,768]{2,1,0:T(8,128)(2,1)S(1)}, u32[]{:S(2)}, u32[]{:S(2)}) collective-permute-start(bf16[2,96,768]{2,1,0:T(8,128)(2,1)S(1)} %get-tuple-element.156), channel_id=1, source_target_pairs={{0,2},{1,3},{2,0},{3,1},{4,6},{5,7},{6,4},{7,5},{8,10},{9,11},{10,... | collective-permute-start | bytes 884744 | tf_op jit(solution)/shard_map/ppermute | solution.py:84
  49.4 18.8 %collective-permute-start.14 = (bf16[2,96,768]{2,1,0:T(8,128)(2,1)S(1)}, bf16[2,96,768]{2,1,0:T(8,128)(2,1)S(1)}, u32[]{:S(2)}, u32[]{:S(2)}) collective-permute-start(bf16[2,96,768]{2,1,0:T(8,128)(2,1)S(1)} %get-tuple-element.157), channel_id=1, source_target_pairs={{0,4},{1,5},{2,6},{3,7},{4,0},{5,1},{6,2},{7,3},{8,12},{9,13},{10,... | collective-permute-start | bytes 884744 | tf_op jit(solution)/shard_map/ppermute | solution.py:84
  72.0 22.9 %collective-permute-start.17 = (bf16[4,96,768]{2,1,0:T(8,128)(2,1)S(1)}, bf16[4,96,768]{2,1,0:T(8,128)(2,1)S(1)}, u32[]{:S(2)}, u32[]{:S(2)}) collective-permute-start(bf16[4,96,768]{2,1,0:T(8,128)(2,1)S(1)} %pad_maximum_fusion.18), channel_id=1, source_target_pairs={{0,4},{1,5},{2,6},{3,7},{4,0},{5,1},{6,2},{7,3},{8,12},{9,13},{10,... | collective-permute-start | bytes 1769480 | tf_op jit(solution)/shard_map/ppermute | solution.py:84
  73.8 15.5 %collective-permute-start.18 = (bf16[4,96,768]{2,1,0:T(8,128)(2,1)S(1)}, bf16[4,96,768]{2,1,0:T(8,128)(2,1)S(1)}, u32[]{:S(2)}, u32[]{:S(2)}) collective-permute-start(bf16[4,96,768]{2,1,0:T(8,128)(2,1)S(1)} %pad_maximum_fusion.19), channel_id=1, source_target_pairs={{0,2},{1,3},{2,0},{3,1},{4,6},{5,7},{6,4},{7,5},{8,10},{9,11},{10,... | collective-permute-start | bytes 1769480 | tf_op jit(solution)/shard_map/ppermute | solution.py:84
  76.6 22.4 %collective-permute-start.16 = (bf16[2,2,48,1120]{3,2,0,1:T(8,128)(2,1)S(1)}, bf16[2,2,48,1120]{3,2,0,1:T(8,128)(2,1)S(1)}, u32[]{:S(2)}, u32[]{:S(2)}) collective-permute-start(bf16[2,2,48,1120]{3,2,0,1:T(8,128)(2,1)S(1)} %get-tuple-element.161), channel_id=1, source_target_pairs={{0,8},{1,9},{2,10},{3,11},{4,12},{5,13},{6,14},{7,15},{8,0},{9,1},... | collective-permute-start | bytes 1290248 | tf_op jit(solution)/shard_map/ppermute | solution.py:84
  102.1 20.1 %collective-permute-start.21 = (bf16[4,48,1120]{2,1,0:T(8,128)(2,1)}, bf16[4,48,1120]{2,1,0:T(8,128)(2,1)}, u32[]{:S(2)}, u32[]{:S(2)}) collective-permute-start(bf16[4,48,1120]{2,1,0:T(8,128)(2,1)} %get-tuple-element.170), channel_id=1, source_target_pairs={{0,4},{1,5},{2,6},{3,7},{4,0},{5,1},{6,2},{7,3},{8,12},{9,13},{10,... | collective-permute-start | bytes 1290248 | tf_op jit(solution)/shard_map/ppermute | solution.py:84
  104.3 22.8 %collective-permute-start.23 = (bf16[2,2,48,1120]{3,2,0,1:T(8,128)(2,1)S(1)}, bf16[2,2,48,1120]{3,2,0,1:T(8,128)(2,1)S(1)}, u32[]{:S(2)}, u32[]{:S(2)}) collective-permute-start(bf16[2,2,48,1120]{3,2,0,1:T(8,128)(2,1)S(1)} %get-tuple-element.172), channel_id=1, source_target_pairs={{0,8},{1,9},{2,10},{3,11},{4,12},{5,13},{6,14},{7,15},{8,0},{9,1},... | collective-permute-start | bytes 1290248 | tf_op jit(solution)/shard_map/ppermute | solution.py:84
  123.3 23.9 %collective-permute-start.24 = (bf16[8,48,1120]{2,1,0:T(8,128)(2,1)S(1)}, bf16[8,48,1120]{2,1,0:T(8,128)(2,1)S(1)}, u32[]{:S(2)}, u32[]{:S(2)}) collective-permute-start(bf16[8,48,1120]{2,1,0:T(8,128)(2,1)S(1)} %pad_maximum_fusion.5.refs_0_), channel_id=1, source_target_pairs={{0,16},{16,0},{1,17},{17,1},{2,18},{18,2},{3,19},{19,3},{4,20},{20... | collective-permute-start | bytes 2580488 | tf_op jit(solution)/shard_map/ppermute | solution.py:82
  127.2 20.0 %collective-permute-start.25 = (bf16[4,48,1120]{2,1,0:T(8,128)(2,1)S(1)}, bf16[4,48,1120]{2,1,0:T(8,128)(2,1)S(1)}, u32[]{:S(2)}, u32[]{:S(2)}) collective-permute-start(bf16[4,48,1120]{2,1,0:T(8,128)(2,1)S(1)} %get-tuple-element.176), channel_id=1, source_target_pairs={{0,4},{1,5},{2,6},{3,7},{4,0},{5,1},{6,2},{7,3},{8,12},{9,13},{10,... | collective-permute-start | bytes 1290248 | tf_op jit(solution)/shard_map/ppermute | solution.py:84
  127.3 17.7 %collective-permute-start.22 = (bf16[1,128,1536]{2,1,0:T(8,128)(2,1)S(1)}, bf16[1,128,1536]{2,1,0:T(8,128)(2,1)S(1)}, u32[]{:S(2)}, u32[]{:S(2)}) collective-permute-start(bf16[1,128,1536]{2,1,0:T(8,128)(2,1)S(1)} %bitcast.333), channel_id=1, source_target_pairs={{0,8},{1,9},{2,10},{3,11},{4,12},{5,13},{6,14},{7,15},{8,0},{9,1},... | collective-permute-start | bytes 1179656 | tf_op jit(solution)/shard_map/ppermute | solution.py:84
  159.2 34.1 %collective-permute-start.33 = (bf16[16,48,1120]{2,1,0:T(8,128)(2,1)}, bf16[16,48,1120]{2,1,0:T(8,128)(2,1)}, u32[]{:S(2)}, u32[]{:S(2)}) collective-permute-start(bf16[16,48,1120]{2,1,0:T(8,128)(2,1)} %pad_maximum_fusion.1), channel_id=1, source_target_pairs={{0,1},{1,0},{2,3},{3,2},{4,5},{5,4},{6,7},{7,6},{8,9},{9,8},{10,11... | collective-permute-start | bytes 5160968 | tf_op jit(solution)/shard_map/ppermute | solution.py:84
  160.3 22.2 %collective-permute-start.29 = (bf16[8,48,1120]{2,1,0:T(8,128)(2,1)}, bf16[8,48,1120]{2,1,0:T(8,128)(2,1)S(1)}, u32[]{:S(2)}, u32[]{:S(2)}) collective-permute-start(bf16[8,48,1120]{2,1,0:T(8,128)(2,1)} %pad_maximum_fusion.6.refs_3_), channel_id=1, source_target_pairs={{0,16},{16,0},{1,17},{17,1},{2,18},{18,2},{3,19},{19,3},{4,20},{20... | collective-permute-start | bytes 2580488 | tf_op jit(solution)/shard_map/ppermute | solution.py:82
  163.8 27.5 %collective-permute-start.31 = (bf16[4,64,1536]{2,1,0:T(8,128)(2,1)}, bf16[4,64,1536]{2,1,0:T(8,128)(2,1)}, u32[]{:S(2)}, u32[]{:S(2)}) collective-permute-start(bf16[4,64,1536]{2,1,0:T(8,128)(2,1)} %pad_maximum_fusion.12), channel_id=1, source_target_pairs={{0,2},{1,3},{2,0},{3,1},{4,6},{5,7},{6,4},{7,5},{8,10},{9,11},{10,... | collective-permute-start | bytes 2359304 | tf_op jit(solution)/shard_map/ppermute | solution.py:84
  165.2 28.1 %collective-permute-start.32 = (bf16[4,64,1536]{2,1,0:T(8,128)(2,1)}, bf16[4,64,1536]{2,1,0:T(8,128)(2,1)}, u32[]{:S(2)}, u32[]{:S(2)}) collective-permute-start(bf16[4,64,1536]{2,1,0:T(8,128)(2,1)} %pad_maximum_fusion.13), channel_id=1, source_target_pairs={{0,4},{1,5},{2,6},{3,7},{4,0},{5,1},{6,2},{7,3},{8,12},{9,13},{10,... | collective-permute-start | bytes 2359304 | tf_op jit(solution)/shard_map/ppermute | solution.py:84
  165.7 25.5 %collective-permute-start.28 = (bf16[1,128,1536]{2,1,0:T(8,128)(2,1)S(1)}, bf16[1,128,1536]{2,1,0:T(8,128)(2,1)}, u32[]{:S(2)}, u32[]{:S(2)}) collective-permute-start(bf16[1,128,1536]{2,1,0:T(8,128)(2,1)S(1)} %copy-done.10), channel_id=1, source_target_pairs={{0,8},{1,9},{2,10},{3,11},{4,12},{5,13},{6,14},{7,15},{8,0},{9,1},... | collective-permute-start | bytes 1179656 | tf_op jit(solution)/shard_map/ppermute | solution.py:84
  193.4 25.4 %collective-permute-start.36 = (bf16[16,48,1120]{2,1,0:T(8,128)(2,1)}, bf16[16,48,1120]{2,1,0:T(8,128)(2,1)}, u32[]{:S(2)}, u32[]{:S(2)}) collective-permute-start(bf16[16,48,1120]{2,1,0:T(8,128)(2,1)} %pad_maximum_fusion.2), channel_id=1, source_target_pairs={{0,1},{1,0},{2,3},{3,2},{4,5},{5,4},{6,7},{7,6},{8,9},{9,8},{10,11... | collective-permute-start | bytes 5160968 | tf_op jit(solution)/shard_map/ppermute | solution.py:84
  218.8 25.2 %collective-permute-start.37 = (bf16[4,64,1536]{2,1,0:T(8,128)(2,1)S(1)}, bf16[4,64,1536]{2,1,0:T(8,128)(2,1)S(1)}, u32[]{:S(2)}, u32[]{:S(2)}) collective-permute-start(bf16[4,64,1536]{2,1,0:T(8,128)(2,1)S(1)} %pad_maximum_fusion.14), channel_id=1, source_target_pairs={{0,2},{1,3},{2,0},{3,1},{4,6},{5,7},{6,4},{7,5},{8,10},{9,11},{10,... | collective-permute-start | bytes 2359304 | tf_op jit(solution)/shard_map/ppermute | solution.py:84
  219.4 24.6 %collective-permute-start.38 = (bf16[4,64,1536]{2,1,0:T(8,128)(2,1)S(1)}, bf16[4,64,1536]{2,1,0:T(8,128)(2,1)S(1)}, u32[]{:S(2)}, u32[]{:S(2)}) collective-permute-start(bf16[4,64,1536]{2,1,0:T(8,128)(2,1)S(1)} %pad_maximum_fusion.15), channel_id=1, source_target_pairs={{0,4},{1,5},{2,6},{3,7},{4,0},{5,1},{6,2},{7,3},{8,12},{9,13},{10,... | collective-permute-start | bytes 2359304 | tf_op jit(solution)/shard_map/ppermute | solution.py:84
  262.1 17.9 %collective-permute-start.39 = (bf16[256,1536]{1,0:T(8,128)(2,1)S(1)}, bf16[256,1536]{1,0:T(8,128)(2,1)S(1)}, u32[]{:S(2)}, u32[]{:S(2)}) collective-permute-start(bf16[256,1536]{1,0:T(8,128)(2,1)S(1)} %get-tuple-element.195), channel_id=1, source_target_pairs={{0,2},{1,3},{2,0},{3,1},{4,6},{5,7},{6,4},{7,5},{8,10},{9,11},{10,... | collective-permute-start | bytes 2359304 | tf_op jit(solution)/shard_map/ppermute | solution.py:84
  265.7 17.7 %collective-permute-start.40 = (bf16[256,1536]{1,0:T(8,128)(2,1)S(1)}, bf16[256,1536]{1,0:T(8,128)(2,1)S(1)}, u32[]{:S(2)}, u32[]{:S(2)}) collective-permute-start(bf16[256,1536]{1,0:T(8,128)(2,1)S(1)} %get-tuple-element.197), channel_id=1, source_target_pairs={{0,4},{1,5},{2,6},{3,7},{4,0},{5,1},{6,2},{7,3},{8,12},{9,13},{10,... | collective-permute-start | bytes 2359304 | tf_op jit(solution)/shard_map/ppermute | solution.py:84
  297.2 24.3 %collective-permute-start.45 = (bf16[1,128,1536]{2,1,0:T(8,128)(2,1)S(1)}, bf16[1,128,1536]{2,1,0:T(8,128)(2,1)S(1)}, u32[]{:S(2)}, u32[]{:S(2)}) collective-permute-start(bf16[1,128,1536]{2,1,0:T(8,128)(2,1)S(1)} %fusion.20), channel_id=1, source_target_pairs={{0,8},{1,9},{2,10},{3,11},{4,12},{5,13},{6,14},{7,15},{8,0},{9,1},... | collective-permute-start | bytes 1179656 | tf_op jit(solution)/shard_map/ppermute | solution.py:84
  297.9 37.1 %collective-permute-start.44 = (bf16[256,1536]{1,0:T(8,128)(2,1)}, bf16[256,1536]{1,0:T(8,128)(2,1)}, u32[]{:S(2)}, u32[]{:S(2)}) collective-permute-start(bf16[256,1536]{1,0:T(8,128)(2,1)} %convolution_convert_fusion.3), channel_id=1, source_target_pairs={{0,2},{1,3},{2,0},{3,1},{4,6},{5,7},{6,4},{7,5},{8,10},{9,11},{10,... | collective-permute-start | bytes 2359304 | tf_op jit(solution)/shard_map/ppermute | solution.py:84
  298.7 41.7 %collective-permute-start.47 = (bf16[256,1536]{1,0:T(8,128)(2,1)}, bf16[256,1536]{1,0:T(8,128)(2,1)}, u32[]{:S(2)}, u32[]{:S(2)}) collective-permute-start(bf16[256,1536]{1,0:T(8,128)(2,1)} %convolution_convert_fusion.2), channel_id=1, source_target_pairs={{0,4},{1,5},{2,6},{3,7},{4,0},{5,1},{6,2},{7,3},{8,12},{9,13},{10,... | collective-permute-start | bytes 2359304 | tf_op jit(solution)/shard_map/ppermute | solution.py:84
  303.7 40.3 %collective-permute-start.46 = (bf16[8,48,1120]{2,1,0:T(8,128)(2,1)}, bf16[8,48,1120]{2,1,0:T(8,128)(2,1)}, u32[]{:S(2)}, u32[]{:S(2)}) collective-permute-start(bf16[8,48,1120]{2,1,0:T(8,128)(2,1)} %fusion.10), channel_id=1, source_target_pairs={{0,16},{16,0},{1,17},{17,1},{2,18},{18,2},{3,19},{19,3},{4,20},{20... | collective-permute-start | bytes 2580488 | tf_op jit(solution)/shard_map/ppermute | solution.py:82
  304.2 42.3 %collective-permute-start.48 = (bf16[2,8,48,1120]{3,2,1,0:T(8,128)(2,1)}, bf16[2,8,48,1120]{3,2,1,0:T(8,128)(2,1)}, u32[]{:S(2)}, u32[]{:S(2)}) collective-permute-start(bf16[2,8,48,1120]{3,2,1,0:T(8,128)(2,1)} %get-tuple-element.217), channel_id=1, source_target_pairs={{0,1},{1,0},{2,3},{3,2},{4,5},{5,4},{6,7},{7,6},{8,9},{9,8},{10,11... | collective-permute-start | bytes 5160968 | tf_op jit(solution)/shard_map/ppermute | solution.py:84
  348.1 18.2 %collective-permute-start.49 = (bf16[2,64,1536]{2,1,0:T(8,128)(2,1)}, bf16[2,64,1536]{2,1,0:T(8,128)(2,1)}, u32[]{:S(2)}, u32[]{:S(2)}) collective-permute-start(bf16[2,64,1536]{2,1,0:T(8,128)(2,1)} %bitcast.94), channel_id=1, source_target_pairs={{0,4},{1,5},{2,6},{3,7},{4,0},{5,1},{6,2},{7,3},{8,12},{9,13},{10,... | collective-permute-start | bytes 1179656 | tf_op jit(solution)/shard_map/ppermute | solution.py:84
  348.3 18.0 %collective-permute-start.51 = (bf16[2,64,1536]{2,1,0:T(8,128)(2,1)}, bf16[2,64,1536]{2,1,0:T(8,128)(2,1)}, u32[]{:S(2)}, u32[]{:S(2)}) collective-permute-start(bf16[2,64,1536]{2,1,0:T(8,128)(2,1)} %bitcast.101), channel_id=1, source_target_pairs={{0,2},{1,3},{2,0},{3,1},{4,6},{5,7},{6,4},{7,5},{8,10},{9,11},{10,... | collective-permute-start | bytes 1179656 | tf_op jit(solution)/shard_map/ppermute | solution.py:84
  349.5 22.5 %collective-permute-start.52 = (bf16[1,2,2,48,1120]{4,3,0,2,1:T(8,128)(2,1)}, bf16[1,2,2,48,1120]{4,3,0,2,1:T(8,128)(2,1)}, u32[]{:S(2)}, u32[]{:S(2)}) collective-permute-start(bf16[1,2,2,48,1120]{4,3,0,2,1:T(8,128)(2,1)} %get-tuple-element.229), channel_id=1, source_target_pairs={{0,8},{1,9},{2,10},{3,11},{4,12},{5,13},{6,14},{7,15},{8,0},{9,1},... | collective-permute-start | bytes 1290248 | tf_op jit(solution)/shard_map/ppermute | solution.py:84
  355.0 21.3 %collective-permute-start.53 = (bf16[8,48,1120]{2,1,0:T(8,128)(2,1)}, bf16[8,48,1120]{2,1,0:T(8,128)(2,1)}, u32[]{:S(2)}, u32[]{:S(2)}) collective-permute-start(bf16[8,48,1120]{2,1,0:T(8,128)(2,1)} %fusion.11), channel_id=1, source_target_pairs={{0,16},{16,0},{1,17},{17,1},{2,18},{18,2},{3,19},{19,3},{4,20},{20... | collective-permute-start | bytes 2580488 | tf_op jit(solution)/shard_map/ppermute | solution.py:82
  380.0 18.7 %collective-permute-start.56 = (bf16[1,128,1536]{2,1,0:T(8,128)(2,1)S(1)}, bf16[1,128,1536]{2,1,0:T(8,128)(2,1)S(1)}, u32[]{:S(2)}, u32[]{:S(2)}) collective-permute-start(bf16[1,128,1536]{2,1,0:T(8,128)(2,1)S(1)} %fusion.24), channel_id=1, source_target_pairs={{0,8},{1,9},{2,10},{3,11},{4,12},{5,13},{6,14},{7,15},{8,0},{9,1},... | collective-permute-start | bytes 1179656 | tf_op jit(solution)/shard_map/ppermute | solution.py:84
  380.7 30.7 %collective-permute-start.59 = (bf16[768,1536]{1,0:T(8,128)(2,1)S(1)}, bf16[768,1536]{1,0:T(8,128)(2,1)S(1)}, u32[]{:S(2)}, u32[]{:S(2)}) collective-permute-start(bf16[768,1536]{1,0:T(8,128)(2,1)S(1)} %copy-done.58), channel_id=1, source_target_pairs={{0,1},{1,0},{2,3},{3,2},{4,5},{5,4},{6,7},{7,6},{8,9},{9,8},{10,11... | collective-permute-start | bytes 7077896 | tf_op jit(solution)/shard_map/ppermute | solution.py:84
  381.9 20.0 %collective-permute-start.57 = (bf16[2,2,2,48,1024]{4,3,2,1,0:T(8,128)(2,1)S(1)}, bf16[2,2,2,48,1024]{4,3,2,1,0:T(8,128)(2,1)S(1)}, u32[]{:S(2)}, u32[]{:S(2)}) collective-permute-start(bf16[2,2,2,48,1024]{4,3,2,1,0:T(8,128)(2,1)S(1)} %slice_bitcast_fusion.9), channel_id=1, source_target_pairs={{0,2},{1,3},{2,0},{3,1},{4,6},{5,7},{6,4},{7,5},{8,10},{9,11},{10,... | collective-permute-start | bytes 2359304 | tf_op jit(solution)/shard_map/ppermute | solution.py:84
  382.8 28.0 %collective-permute-start.58 = (bf16[2,2,2,48,1024]{4,3,2,1,0:T(8,128)(2,1)S(1)}, bf16[2,2,2,48,1024]{4,3,2,1,0:T(8,128)(2,1)S(1)}, u32[]{:S(2)}, u32[]{:S(2)}) collective-permute-start(bf16[2,2,2,48,1024]{4,3,2,1,0:T(8,128)(2,1)S(1)} %slice_bitcast_fusion.8), channel_id=1, source_target_pairs={{0,4},{1,5},{2,6},{3,7},{4,0},{5,1},{6,2},{7,3},{8,12},{9,13},{10,... | collective-permute-start | bytes 2359304 | tf_op jit(solution)/shard_map/ppermute | solution.py:84
  385.6 26.7 %collective-permute-start.60 = (bf16[280,1536]{1,0:T(8,128)(2,1)S(1)}, bf16[280,1536]{1,0:T(8,128)(2,1)S(1)}, u32[]{:S(2)}, u32[]{:S(2)}) collective-permute-start(bf16[280,1536]{1,0:T(8,128)(2,1)S(1)} %get-tuple-element.249), channel_id=1, source_target_pairs={{0,16},{16,0},{1,17},{17,1},{2,18},{18,2},{3,19},{19,3},{4,20},{20... | collective-permute-start | bytes 2580488 | tf_op jit(solution)/shard_map/ppermute | solution.py:82
  413.8 19.6 %collective-permute-start.64 = (bf16[2,2,48,1120]{3,2,0,1:T(8,128)(2,1)S(1)}, bf16[2,2,48,1120]{3,2,0,1:T(8,128)(2,1)S(1)}, u32[]{:S(2)}, u32[]{:S(2)}) collective-permute-start(bf16[2,2,48,1120]{3,2,0,1:T(8,128)(2,1)S(1)} %get-tuple-element.254), channel_id=1, source_target_pairs={{0,4},{1,5},{2,6},{3,7},{4,0},{5,1},{6,2},{7,3},{8,12},{9,13},{10,... | collective-permute-start | bytes 1290248 | tf_op jit(solution)/shard_map/ppermute | solution.py:84
  415.8 17.7 %collective-permute-start.65 = (bf16[1,2,2,48,1120]{4,3,0,1,2:T(8,128)(2,1)S(1)}, bf16[1,2,2,48,1120]{4,3,0,1,2:T(8,128)(2,1)S(1)}, u32[]{:S(2)}, u32[]{:S(2)}) collective-permute-start(bf16[1,2,2,48,1120]{4,3,0,1,2:T(8,128)(2,1)S(1)} %bitcast.373), channel_id=1, source_target_pairs={{0,2},{1,3},{2,0},{3,1},{4,6},{5,7},{6,4},{7,5},{8,10},{9,11},{10,... | collective-permute-start | bytes 1290248 | tf_op jit(solution)/shard_map/ppermute | solution.py:84
  434.7 19.8 %collective-permute-start.67 = (bf16[1,2,48,2048]{3,2,1,0:T(8,128)(2,1)S(1)}, bf16[1,2,48,2048]{3,2,1,0:T(8,128)(2,1)S(1)}, u32[]{:S(2)}, u32[]{:S(2)}) collective-permute-start(bf16[1,2,48,2048]{3,2,1,0:T(8,128)(2,1)S(1)} %fusion.13), channel_id=1, source_target_pairs={{0,8},{1,9},{2,10},{3,11},{4,12},{5,13},{6,14},{7,15},{8,0},{9,1},... | collective-permute-start | bytes 1179656 | tf_op jit(solution)/shard_map/ppermute | solution.py:84
  437.3 18.4 %collective-permute-start.69 = (bf16[2,2,48,1120]{3,2,0,1:T(8,128)(2,1)S(1)}, bf16[2,2,48,1120]{3,2,0,1:T(8,128)(2,1)S(1)}, u32[]{:S(2)}, u32[]{:S(2)}) collective-permute-start(bf16[2,2,48,1120]{3,2,0,1:T(8,128)(2,1)S(1)} %get-tuple-element.260), channel_id=1, source_target_pairs={{0,4},{1,5},{2,6},{3,7},{4,0},{5,1},{6,2},{7,3},{8,12},{9,13},{10,... | collective-permute-start | bytes 1290248 | tf_op jit(solution)/shard_map/ppermute | solution.py:84
  437.6 17.0 %collective-permute-start.68 = (bf16[4,48,1120]{2,1,0:T(8,128)(2,1)S(1)}, bf16[4,48,1120]{2,1,0:T(8,128)(2,1)S(1)}, u32[]{:S(2)}, u32[]{:S(2)}) collective-permute-start(bf16[4,48,1120]{2,1,0:T(8,128)(2,1)S(1)} %get-tuple-element.259), channel_id=1, source_target_pairs={{0,2},{1,3},{2,0},{3,1},{4,6},{5,7},{6,4},{7,5},{8,10},{9,11},{10,... | collective-permute-start | bytes 1290248 | tf_op jit(solution)/shard_map/ppermute | solution.py:84
  437.9 20.0 %collective-permute-start.70 = (bf16[280,1536]{1,0:T(8,128)(2,1)}, bf16[280,1536]{1,0:T(8,128)(2,1)S(1)}, u32[]{:S(2)}, u32[]{:S(2)}) collective-permute-start(bf16[280,1536]{1,0:T(8,128)(2,1)} %get-tuple-element.261), channel_id=1, source_target_pairs={{0,16},{16,0},{1,17},{17,1},{2,18},{18,2},{3,19},{19,3},{4,20},{20... | collective-permute-start | bytes 2580488 | tf_op jit(solution)/shard_map/ppermute | solution.py:82
  461.4 21.6 %collective-permute-start.74 = (bf16[2,2,2,48,768]{4,3,2,1,0:T(8,128)(2,1)S(1)}, bf16[2,2,2,48,768]{4,3,2,1,0:T(8,128)(2,1)S(1)}, u32[]{:S(2)}, u32[]{:S(2)}) collective-permute-start(bf16[2,2,2,48,768]{4,3,2,1,0:T(8,128)(2,1)S(1)} %slice_bitcast_fusion.12), channel_id=1, source_target_pairs={{0,4},{1,5},{2,6},{3,7},{4,0},{5,1},{6,2},{7,3},{8,12},{9,13},{10,... | collective-permute-start | bytes 1769480 | tf_op jit(solution)/shard_map/ppermute | solution.py:84
  464.2 22.3 %collective-permute-start.76 = (bf16[4,48,1120]{2,1,0:T(8,128)(2,1)S(1)}, bf16[4,48,1120]{2,1,0:T(8,128)(2,1)S(1)}, u32[]{:S(2)}, u32[]{:S(2)}) collective-permute-start(bf16[4,48,1120]{2,1,0:T(8,128)(2,1)S(1)} %get-tuple-element.267), channel_id=1, source_target_pairs={{0,8},{1,9},{2,10},{3,11},{4,12},{5,13},{6,14},{7,15},{8,0},{9,1},... | collective-permute-start | bytes 1290248 | tf_op jit(solution)/shard_map/ppermute | solution.py:84
  466.0 28.3 %collective-permute-start.77 = (bf16[48,8960]{1,0:T(8,128)(2,1)S(1)}, bf16[48,8960]{1,0:T(8,128)(2,1)S(1)}, u32[]{:S(2)}, u32[]{:S(2)}) collective-permute-start(bf16[48,8960]{1,0:T(8,128)(2,1)S(1)} %shard_map.193.gate), channel_id=1, source_target_pairs={{0,16},{16,0},{1,17},{17,1},{2,18},{18,2},{3,19},{19,3},{4,20},{20... | collective-permute-start | bytes 2580488 | tf_op jit(solution)/shard_map/ppermute | solution.py:82
  496.7 16.9 %collective-permute-start.83 = (bf16[48,8960]{1,0:T(8,128)(2,1)S(1)}, bf16[48,8960]{1,0:T(8,128)(2,1)S(1)}, u32[]{:S(2)}, u32[]{:S(2)}) collective-permute-start(bf16[48,8960]{1,0:T(8,128)(2,1)S(1)} %shard_map.194.up), channel_id=1, source_target_pairs={{0,16},{16,0},{1,17},{17,1},{2,18},{18,2},{3,19},{19,3},{4,20},{20... | collective-permute-start | bytes 2580488 | tf_op jit(solution)/shard_map/ppermute | solution.py:82
  (129 other events, 1155.5 us)

commit v3 on v2

--- a/solution.py
+++ b/solution.py
@@ -56,22 +56,20 @@
 
 class Lanes:
     def __init__(self):
-        self.moves, self.flying, self.ended, self.before, self.kernels = [], [], [], [], []
+        self.flying, self.ended, self.before, self.kernels = [], [], [], []
 
     def round(self, *entries):
-        for move in self.moves:
-            move.resume(self.kernels)
-        self.moves = []
         ended = [value for value, left in self.flying if left <= 1] + self.kernels
         self.before, self.ended = ended + self.ended, ended
         self.flying = [(value, left - 1) for value, left in self.flying if left > 1]
-        self.kernels = []
+        self.waited, self.kernels = self.kernels, []
         self.more(*entries)
 
     def more(self, *entries):
         size = lax.axis_size("fsdp")
         for entry in entries:
             move, lasts = entry if isinstance(entry, tuple) else (entry, 1)
+            move.resume(self.waited)
             if not move.wanted:
                 continue
             move.arrived = []
@@ -85,7 +83,6 @@
                 move.arrived.append(value)
                 self.flying.append((value, lasts))
             move.wanted = None
-            self.moves.append(move)
 
     def hold(self, value):
         return after(value, *self.before) if self.before else value
@@ -232,8 +229,8 @@
         (got,) = yield [(bit, state)]
         state = join(state, got)
         marks = marks + [f ^ bit for f in marks]
-    half = width // 2
-    first, second = state[:, :, :half], state[:, :, half:]
+    cut = width // 3 // 128 * 128
+    first, second = state[:, :, :cut], state[:, :, cut:]
     got = yield [(X, first), (Z, second)]
     first, second = join(first, got[0]), join(second, got[1])
     got = yield [(Z, first), (X, second)]
@@ -255,25 +252,30 @@
         out[where[i]] = source[i]
 
 
-def scatter_weight(left, right, me, s):
+def turn_rows(left, me, s):
     size = lax.axis_size("fsdp")
-    far = far_bits()
-    count = 1 << len(far)
-    rows, width = left.shape[1], right.shape[1]
-    half = rows // size // 2
-    turned = left.T.reshape(size * 2, half, left.shape[0])
+    count = size // 8
+    rows = left.shape[1]
+    turned = left.T.reshape(size * 2, rows // size // 2, left.shape[0])
     where = []
     for place in range(size):
         for h in range(2):
             k = me ^ place
             kept = ((k % 2) * 2 + (k // 2) % 2) * 2 + (k // 4) % 2
             where.append((kept * count + k // 8) * 2 + (s ^ h))
-    turned = whole_call(
+    return whole_call(
         order_kernel, jax.ShapeDtypeStruct(turned.shape, bf16), where, [turned]
     ).reshape(2, rows // 2, left.shape[0])
+
+
+def scatter_weight(turned, right, s, cut):
+    size = lax.axis_size("fsdp")
+    far = far_bits()
+    count = 1 << len(far)
+    half, width = turned.shape[1] // size, right.shape[1]
     (got,) = yield [(CORE, dot(turned[1], right).astype(bf16))]
     total = add(dot(turned[0], right), got).reshape(2, 2, count, 2, half, width)
-    low, high = total[..., : width // 2], total[..., width // 2 :]
+    low, high = total[..., :cut], total[..., cut:]
     got = yield [(X, low[1].astype(bf16)), (Z, high[:, 1].astype(bf16))]
     low, high = add(low[0], got[0]), add(high[:, 0], got[1])
     got = yield [(Z, low[1].astype(bf16)), (X, high[1].astype(bf16))]
@@ -817,12 +819,14 @@
         [early[3], last[3]], [lanes.hold(early[2]), lanes.hold(last[2])], me, s
     )
     up = Move(unshuffle_part(up_terms, [X, Z] + far, me))
+    attended_turned = turn_rows(lanes.hold(attended), me, s)
+    normed_turned = turn_rows(lanes.hold(normed), me, s)
     lanes.round(back, gate, result, up)
     down_terms = t_dot(lanes.hold(early[0]), early[4]) + t_dot(lanes.hold(last[0]), last[4])
     down_terms = down_terms[:unit].astype(bf16).reshape(2, unit // 2, D)
     down = Move(sum_down(down_terms, core))
     (grad_normed_two,) = lanes.drain(back)
-    lanes.round(result, (gate, 2), (up, 2))
+    lanes.round((gate, 2), (up, 2))
 
     grad_middle, grad_branch, gain_two_part, grad_queries, keep, give = whole_call(
         attend_back_kernel,
@@ -842,7 +846,7 @@
     other = Move(swap("y", give))
     lanes.more(other)
     (got,) = lanes.drain(other)
-    out = Move(scatter_weight(attended, grad_branch, me, s))
+    out = Move(scatter_weight(attended_turned, grad_branch, s, 1024))
     grad_projected, input_grad, gain_one_part, bias_part = whole_call(
         project_back_kernel,
         (
@@ -856,9 +860,9 @@
         flops=2 * tokens * D * (QW + 2 * KW),
     )
     lanes.beside(grad_projected)
-    qkv = Move(scatter_weight(normed, grad_projected, me, s))
+    qkv = Move(scatter_weight(normed_turned, grad_projected, s, 1280))
     sums = Move(sum_everywhere(join(gain_one_part[0], bias_part[0], gain_two_part[0])))
-    lanes.round(qkv, down)
+    lanes.round(qkv, down, result)
     lanes.round(qkv, (result, 2), out, down)
     lanes.round(qkv, gate, up, sums)
     lanes.round(qkv, gate, up, down, sums)

time: 529 us -> 512 us (0.968)
    unnamed x179 -> x211, local copies, waits for them, and re-layouts: 17.1 us -> 23.1 us
  transfers between devices with their start and end apart: 86 -> 86, of which waited for: 45 -> 43; matrix products, arithmetic and copies ran while one was open for 18% -> 14% of each run, Pallas kernels for 16% -> 16%
where the time goes in v3:
time: 512 us; the launch traced here: 508 us
  waiting for transfers between devices  219 us (43%)
  Pallas kernels  101 us (20%)
  starting transfers between devices  84.5 us (17%)
  other arithmetic  40.4 us (8%)
  local copies, waits for them, and re-layouts  38.9 us (8%)
  matrix products  21.2 us (4%)
    ppermute x68, waiting for transfers between devices, more(): value = lax.ppermute(value, 'fsdp', [(i, i ^ link) for i in range(size)])  188 us
    ppermute x68, starting transfers between devices, more(): value = lax.ppermute(value, 'fsdp', [(i, i ^ link) for i in range(size)])  64.9 us
    pallas_call x14, Pallas kernels, whole_call(): pl.pallas_call(kernel, out_shape=out_shape, in_specs=[pl.BlockSpec(memory...  50.7 us
    pallas_call x2, Pallas kernels, feed_forward(): pl.pallas_call(feed_kernel, grid=(steps,), out_shape=(units, units, units...  35 us
    ppermute x18, waiting for transfers between devices, more(): value = lax.ppermute(value, 'seq', [(0, 1), (1, 0)])  30.6 us
    unnamed x211, local copies, waits for them, and re-layouts  23.1 us
    ppermute x18, starting transfers between devices, more(): value = lax.ppermute(value, 'seq', [(0, 1), (1, 0)])  19.6 us
    pallas_call x2, Pallas kernels, gate_up_grad(): pl.pallas_call(functools.partial(grad_kernel, count, unit), out_shape=[ja...  15.6 us
  transfers between devices with their start and end apart: 86, of which 43 were waited for; matrix products, arithmetic and copies ran while one was open for 14% of the time, Pallas kernels for 16%

profile of v3, /device:TPU:0, one launch (start us, length us, event | category | flops | bytes accessed | tf_op | source)
XLA Modules:
  0.0 508.2 jit_solution(3137318489526881155)
XLA Ops:
  1.7 4.1 collective-permute-start
  12.0 2.9 collective-permute-done
  14.9 6.4 %collective-permute-done.1 = bf16[1,2,2,48,1120]{4,3,0,2,1:T(8,128)(2,1)S(1)} collective-permute-done((bf16[1,2,2,48,1120]{4,3,0,2,1:T(8,128)(2,1)S(1)}, bf16[1,2,2,48,1120]{4,3,0,2,1:T(8,128)(2,1)S(1)}, u32[]{:S(2)}, u32[]{:S(2)}) %collective-permute-start.1) | collective-permute-done | bytes 430112 | tf_op jit(solution)/shard_map/ppermute | solution.py:82
  26.9 7.7 %collective-permute-done.3 = bf16[2,48,640]{2,1,0:T(8,128)(2,1)S(1)} collective-permute-done((bf16[2,48,640]{2,1,0:T(8,128)(2,1)S(1)}, bf16[2,48,640]{2,1,0:T(8,128)(2,1)S(1)}, u32[]{:S(2)}, u32[]{:S(2)}) %collective-permute-start.3) | collective-permute-done | bytes 122912 | tf_op jit(solution)/shard_map/ppermute | solution.py:82
  41.1 3.2 collective-permute-done.6
  51.4 9.1 %collective-permute-done.11 = bf16[8,48,640]{2,1,0:T(8,128)(2,1)S(1)} collective-permute-done((bf16[8,48,640]{2,1,0:T(8,128)(2,1)S(1)}, bf16[8,48,640]{2,1,0:T(8,128)(2,1)S(1)}, u32[]{:S(2)}, u32[]{:S(2)}) %collective-permute-start.11) | collective-permute-done | bytes 491552 | tf_op jit(solution)/shard_map/ppermute | solution.py:82
  63.6 2.4 collective-permute-done.13
  75.7 5.1 %shard_map.179 = bf16[32,48,2048]{2,1,0:T(8,128)(2,1)} custom-call(s32[32]{0:T(128)S(1)} %stack.443.where, bf16[16,48,2048]{2,1,0:T(8,128)(2,1)S(1)} %pad_maximum_fusion.refs_0_, bf16[16,48,2048]{2,1,0:T(8,128)(2,1)} %collective-permute-done.15.refs_1_), custom_call_target="tpu_custom_call" | custom-call | bytes 12582912 | tf_op jit(solution)/shard_map/pallas_call | solution.py:131
  80.9 4.1 shard_map.180
  85.0 4.3 collective-permute-done.18
  91.7 6.4 %collective-permute-done.16 = bf16[2,2,48,1120]{3,2,0,1:T(8,128)(2,1)S(1)} collective-permute-done((bf16[2,2,48,1120]{3,2,0,1:T(8,128)(2,1)S(1)}, bf16[2,2,48,1120]{3,2,0,1:T(8,128)(2,1)S(1)}, u32[]{:S(2)}, u32[]{:S(2)}) %collective-permute-start.16) | collective-permute-done | bytes 430112 | tf_op jit(solution)/shard_map/ppermute | solution.py:82
  105.5 4.2 shard_map.181
  109.7 7.7 %shard_map.182 = (bf16[128,1536]{1,0:T(8,128)(2,1)S(1)}, f32[128,128]{1,0:T(8,128)S(1)}, f32[128,1536]{1,0:T(8,128)S(1)}, bf16[128,1536]{1,0:T(8,128)(2,1)S(1)}) custom-call(s32[1]{0:T(128)} %bitcast.at, bf16[128,1536]{1,0:T(8,128)(2,1)S(1)} %bitcast.321, bf16[128,1536]{1,0:T(8,128)(2,1)S(1)} %get-tuple-element.161.queries, ...), custom_call_target="tpu_custom_call" | custom-call | flops 1006632960 | bytes 7413248 | tf_op jit(solution)/shard_map/pallas_call | solution.py:131
  117.5 3.2 collective-permute-done.21
  121.9 4.3 collective-permute-done.23
  128.4 17.9 %collective-permute-done.22 = bf16[1,128,1536]{2,1,0:T(8,128)(2,1)S(1)} collective-permute-done((bf16[1,128,1536]{2,1,0:T(8,128)(2,1)S(1)}, bf16[1,128,1536]{2,1,0:T(8,128)(2,1)S(1)}, u32[]{:S(2)}, u32[]{:S(2)}) %collective-permute-start.22) | collective-permute-done | bytes 393248 | tf_op jit(solution)/shard_map/ppermute | solution.py:82
  148.7 9.3 %collective-permute-done.26 = bf16[2,64,1536]{2,1,0:T(8,128)(2,1)S(1)} collective-permute-done((bf16[2,64,1536]{2,1,0:T(8,128)(2,1)S(1)}, bf16[2,64,1536]{2,1,0:T(8,128)(2,1)S(1)}, u32[]{:S(2)}, u32[]{:S(2)}) %collective-permute-start.26) | collective-permute-done | bytes 393248 | tf_op jit(solution)/shard_map/ppermute | solution.py:82
  163.5 16.9 %collective-permute-done.29.refs_4_ = bf16[8,48,1120]{2,1,0:T(8,128)(2,1)S(1)} collective-permute-done((bf16[8,48,1120]{2,1,0:T(8,128)(2,1)S(1)}, bf16[8,48,1120]{2,1,0:T(8,128)(2,1)S(1)}, u32[]{:S(2)}, u32[]{:S(2)}) %collective-permute-start.29) | collective-permute-done | bytes 860192 | tf_op jit(solution)/shard_map/ppermute | solution.py:80
  181.8 5.8 %collective-permute-done.28 = bf16[1,128,1536]{2,1,0:T(8,128)(2,1)S(1)} collective-permute-done((bf16[1,128,1536]{2,1,0:T(8,128)(2,1)S(1)}, bf16[1,128,1536]{2,1,0:T(8,128)(2,1)S(1)}, u32[]{:S(2)}, u32[]{:S(2)}) %collective-permute-start.28) | collective-permute-done | bytes 393248 | tf_op jit(solution)/shard_map/ppermute | solution.py:82
  198.9 2.4 shard_map.184.down_weight
  201.3 2.8 collective-permute-done.34
  209.8 5.0 shard_map.183
  214.9 17.9 %shard_map.185 = (bf16[512,1152]{1,0:T(8,128)(2,1)S(1)}, bf16[512,1152]{1,0:T(8,128)(2,1)S(1)}, bf16[512,1152]{1,0:T(8,128)(2,1)}, bf16[512,1536]{1,0:T(8,128)(2...) custom-call(bf16[256,1536]{1,0:T(8,128)(2,1)S(1)} %bitcast.329, ...), custom_call_target="tpu_custom_call" | custom-call | flops 9059696640 | bytes 20447232 | tf_op jit(solution)/shard_map/pallas_call | solution.py:685
  232.8 17.2 %shard_map.186 = (bf16[512,1152]{1,0:T(8,128)(2,1)S(1)}, bf16[512,1152]{1,0:T(8,128)(2,1)}, bf16[512,1152]{1,0:T(8,128)(2,1)}, bf16[512,1536]{1,0:T(8,128)(2,1)}...) custom-call(bf16[256,1536]{1,0:T(8,128)(2,1)S(1)} %bitcast.341, ...), custom_call_target="tpu_custom_call" | custom-call | flops 9059696640 | bytes 20447232 | tf_op jit(solution)/shard_map/pallas_call | solution.py:685
  253.8 7.7 %shard_map.187 = (bf16[2,8,48,1120]{3,2,1,0:T(8,128)(2,1)}, bf16[2,8,48,1120]{3,2,1,0:T(8,128)(2,1)}) custom-call(s32[2]{0:T(128)S(1)} %get-tuple-element.331.at, bf16[512,1536]{1,0:T(8,128)(2,1)S(1)} %copy-done.51, bf16[512,1536]{1,0:T(8,128)(2,1)S(1)} %copy-done.53, bf16[512,1152]{1,0:T(8,128)(2,1)S(1)} %get-tuple-element.207.refs_2_, ...), custom_call_target="tpu_custom_call" | custom-call | flops 3623878656 | bytes 12386304 | tf_op jit(solution)/shard_map/pallas_call | solution.py:409
  265.7 3.0 collective-permute-done.40
  278.9 7.9 %shard_map.189 = (bf16[2,8,48,1120]{3,2,1,0:T(8,128)(2,1)}, bf16[2,8,48,1120]{3,2,1,0:T(8,128)(2,1)}) custom-call(s32[2]{0:T(128)S(1)} %get-tuple-element.331.at, bf16[512,1536]{1,0:T(8,128)(2,1)S(1)} %copy-done.52, bf16[512,1536]{1,0:T(8,128)(2,1)S(1)} %copy-done.54, bf16[512,1152]{1,0:T(8,128)(2,1)S(1)} %copy-done.55, bf16[512,1152]{1,0:T(8,128)(2,1)S(1)} %copy-done.56), custom_call_target="tpu_custom_call" | custom-call | flops 3623878656 | bytes 12386304 | tf_op jit(solution)/shard_map/pallas_call | solution.py:409
  297.4 4.9 fusion.80
  302.3 4.1 fusion
  311.1 8.5 %shard_map.188 = (f32[128,1536]{1,0:T(8,128)S(1)}, bf16[128,1536]{1,0:T(8,128)(2,1)S(1)}, f32[1,1536]{1,0:T(1,128)S(1)}, bf16[128,1536]{1,0:T(8,128)(2,1)S(1)}, ...) custom-call(s32[1]{0:T(128)} %bitcast.at, f32[128,1536]{1,0:T(8,128)S(1)} %fusion.21.grad_normed, ...), custom_call_target="tpu_custom_call" | custom-call | flops 1610612736 | bytes 9516544 | tf_op jit(solution)/shard_map/pallas_call | solution.py:131
  331.8 6.4 %shard_map.190 = (bf16[128,2048]{1,0:T(8,128)(2,1)S(1)}, f32[128,1536]{1,0:T(8,128)}, f32[1,1536]{1,0:T(1,128)S(1)}, f32[1,2048]{1,0:T(1,128)S(1)}) custom-call(s32[1]{0:T(128)} %bitcast.at, bf16[128,1536]{1,0:T(8,128)(2,1)S(1)} %copy-done.32, f32[128,512]{1,0:T(8,128)S(1)} %copy-done.38, bf16[128,512]{1,0:T(8,128)(2,1)S(1)} %collective-permute-done.49.got, ...), custom_call_target="tpu_custom_call" | custom-call | flops 805306368 | bytes 9719808 | tf_op jit(solution)/shard_map/pallas_call | solution.py:131
  340.7 2.8 convolution_add_fusion.1
  344.6 2.8 collective-permute-start.50
  350.7 6.8 %collective-permute-done.50 = bf16[2,64,1536]{2,1,0:T(8,128)(2,1)S(1)} collective-permute-done((bf16[2,64,1536]{2,1,0:T(8,128)(2,1)S(1)}, bf16[2,64,1536]{2,1,0:T(8,128)(2,1)S(1)}, u32[]{:S(2)}, u32[]{:S(2)}) %collective-permute-start.50) | collective-permute-done | bytes 393248 | tf_op jit(solution)/shard_map/ppermute | solution.py:82
  369.8 14.1 %collective-permute-done.56 = bf16[1,128,1536]{2,1,0:T(8,128)(2,1)S(1)} collective-permute-done((bf16[1,128,1536]{2,1,0:T(8,128)(2,1)S(1)}, bf16[1,128,1536]{2,1,0:T(8,128)(2,1)S(1)}, u32[]{:S(2)}, u32[]{:S(2)}) %collective-permute-start.56) | collective-permute-done | bytes 393248 | tf_op jit(solution)/shard_map/ppermute | solution.py:82
  384.8 5.8 %collective-permute-done.58 = bf16[2,2,2,48,768]{4,3,2,1,0:T(8,128)(2,1)S(1)} collective-permute-done((bf16[2,2,2,48,768]{4,3,2,1,0:T(8,128)(2,1)S(1)}, bf16[2,2,2,48,768]{4,3,2,1,0:T(8,128)(2,1)S(1)}, u32[]{:S(2)}, u32[]{:S(2)}) %collective-permute-start.58) | collective-permute-done | bytes 589856 | tf_op jit(solution)/shard_map/ppermute | solution.py:82
  398.5 5.6 %collective-permute-done.63 = bf16[2,2,48,768]{3,2,1,0:T(8,128)(2,1)S(1)} collective-permute-done((bf16[2,2,48,768]{3,2,1,0:T(8,128)(2,1)S(1)}, bf16[2,2,48,768]{3,2,1,0:T(8,128)(2,1)S(1)}, u32[]{:S(2)}, u32[]{:S(2)}) %collective-permute-start.63) | collective-permute-done | bytes 294944 | tf_op jit(solution)/shard_map/ppermute | solution.py:82
  404.1 4.7 collective-permute-done.62
  409.0 8.6 %collective-permute-done.64 = bf16[2,2,48,1120]{3,2,0,1:T(8,128)(2,1)S(1)} collective-permute-done((bf16[2,2,48,1120]{3,2,0,1:T(8,128)(2,1)S(1)}, bf16[2,2,48,1120]{3,2,0,1:T(8,128)(2,1)S(1)}, u32[]{:S(2)}, u32[]{:S(2)}) %collective-permute-start.64) | collective-permute-done | bytes 430112 | tf_op jit(solution)/shard_map/ppermute | solution.py:82
  423.7 13.6 %collective-permute-done.67 = bf16[1,2,48,2048]{3,2,1,0:T(8,128)(2,1)S(1)} collective-permute-done((bf16[1,2,48,2048]{3,2,1,0:T(8,128)(2,1)S(1)}, bf16[1,2,48,2048]{3,2,1,0:T(8,128)(2,1)S(1)}, u32[]{:S(2)}, u32[]{:S(2)}) %collective-permute-start.67) | collective-permute-done | bytes 393248 | tf_op jit(solution)/shard_map/ppermute | solution.py:82
  439.8 2.7 collective-permute-done.70
  451.2 5.3 %collective-permute-done.74 = bf16[2,2,2,48,512]{4,3,2,1,0:T(8,128)(2,1)S(1)} collective-permute-done((bf16[2,2,2,48,512]{4,3,2,1,0:T(8,128)(2,1)S(1)}, bf16[2,2,2,48,512]{4,3,2,1,0:T(8,128)(2,1)S(1)}, u32[]{:S(2)}, u32[]{:S(2)}) %collective-permute-start.74) | collective-permute-done | bytes 393248 | tf_op jit(solution)/shard_map/ppermute | solution.py:82
  456.6 7.7 %collective-permute-done.73 = bf16[2,2,2,48,1024]{4,3,2,1,0:T(8,128)(2,1)S(1)} collective-permute-done((bf16[2,2,2,48,1024]{4,3,2,1,0:T(8,128)(2,1)S(1)}, bf16[2,2,2,48,1024]{4,3,2,1,0:T(8,128)(2,1)S(1)}, u32[]{:S(2)}, u32[]{:S(2)}) %collective-permute-start.73) | collective-permute-done | bytes 786464 | tf_op jit(solution)/shard_map/ppermute | solution.py:82
  464.4 3.0 collective-permute-start.75
  473.1 5.3 %collective-permute-done.79 = bf16[2,2,48,1024]{3,2,1,0:T(8,128)(2,1)S(1)} collective-permute-done((bf16[2,2,48,1024]{3,2,1,0:T(8,128)(2,1)S(1)}, bf16[2,2,48,1024]{3,2,1,0:T(8,128)(2,1)S(1)}, u32[]{:S(2)}, u32[]{:S(2)}) %collective-permute-start.79) | collective-permute-done | bytes 393248 | tf_op jit(solution)/shard_map/ppermute | solution.py:82
  481.2 8.2 %collective-permute-done.82 = bf16[1,2,48,1536]{3,2,1,0:T(8,128)(2,1)S(1)} collective-permute-done((bf16[1,2,48,1536]{3,2,1,0:T(8,128)(2,1)S(1)}, bf16[1,2,48,1536]{3,2,1,0:T(8,128)(2,1)S(1)}, u32[]{:S(2)}, u32[]{:S(2)}) %collective-permute-start.82) | collective-permute-done | bytes 294944 | tf_op jit(solution)/shard_map/ppermute | solution.py:82
  489.5 7.0 %collective-permute-done.83.other_up = bf16[48,8960]{1,0:T(8,128)(2,1)S(1)} collective-permute-done((bf16[48,8960]{1,0:T(8,128)(2,1)S(1)}, bf16[48,8960]{1,0:T(8,128)(2,1)S(1)}, u32[]{:S(2)}, u32[]{:S(2)}) %collective-permute-start.83) | collective-permute-done | bytes 860192 | tf_op jit(solution)/shard_map/ppermute | solution.py:80
  503.7 3.3 shard_map.195
  (497 shorter events, 185.2 us)
Async XLA Ops:
  26.6 14.5 %collective-permute-start.7 = (bf16[1,96,1536]{2,1,0:T(8,128)(2,1)S(1)}, bf16[1,96,1536]{2,1,0:T(8,128)(2,1)S(1)}, u32[]{:S(2)}, u32[]{:S(2)}) collective-permute-start(bf16[1,96,1536]{2,1,0:T(8,128)(2,1)S(1)} %bitcast.375), channel_id=1, source_target_pairs={{0,8},{1,9},{2,10},{3,11},{4,12},{5,13},{6,14},{7,15},{8,0},{9,1},... | collective-permute-start | bytes 884744 | tf_op jit(solution)/shard_map/ppermute | solution.py:82
  46.5 14.1 %collective-permute-start.11 = (bf16[8,48,640]{2,1,0:T(8,128)(2,1)S(1)}, bf16[8,48,640]{2,1,0:T(8,128)(2,1)S(1)}, u32[]{:S(2)}, u32[]{:S(2)}) collective-permute-start(bf16[8,48,640]{2,1,0:T(8,128)(2,1)S(1)} %pad_maximum_fusion.20), channel_id=1, source_target_pairs={{0,4},{1,5},{2,6},{3,7},{4,0},{5,1},{6,2},{7,3},{8,12},{9,13},{10,... | collective-permute-start | bytes 1474568 | tf_op jit(solution)/shard_map/ppermute | solution.py:82
  46.5 16.3 %collective-permute-start.12 = (bf16[8,48,768]{2,1,0:T(8,128)(2,1)S(1)}, bf16[8,48,768]{2,1,0:T(8,128)(2,1)S(1)}, u32[]{:S(2)}, u32[]{:S(2)}) collective-permute-start(bf16[8,48,768]{2,1,0:T(8,128)(2,1)S(1)} %pad_maximum_fusion.18), channel_id=1, source_target_pairs={{0,2},{1,3},{2,0},{3,1},{4,6},{5,7},{6,4},{7,5},{8,10},{9,11},{10,... | collective-permute-start | bytes 1769480 | tf_op jit(solution)/shard_map/ppermute | solution.py:82
  48.2 14.8 %collective-permute-start.10 = (bf16[8,48,640]{2,1,0:T(8,128)(2,1)S(1)}, bf16[8,48,640]{2,1,0:T(8,128)(2,1)S(1)}, u32[]{:S(2)}, u32[]{:S(2)}) collective-permute-start(bf16[8,48,640]{2,1,0:T(8,128)(2,1)S(1)} %pad_maximum_fusion.19), channel_id=1, source_target_pairs={{0,16},{16,0},{1,17},{17,1},{2,18},{18,2},{3,19},{19,3},{4,20},{20... | collective-permute-start | bytes 1474568 | tf_op jit(solution)/shard_map/ppermute | solution.py:80
  48.8 17.2 %collective-permute-start.13 = (bf16[2,96,512]{2,1,0:T(8,128)(2,1)S(1)}, bf16[2,96,512]{2,1,0:T(8,128)(2,1)S(1)}, u32[]{:S(2)}, u32[]{:S(2)}) collective-permute-start(bf16[2,96,512]{2,1,0:T(8,128)(2,1)S(1)} %pad_maximum_fusion.35), channel_id=1, source_target_pairs={{0,2},{1,3},{2,0},{3,1},{4,6},{5,7},{6,4},{7,5},{8,10},{9,11},{10,... | collective-permute-start | bytes 589832 | tf_op jit(solution)/shard_map/ppermute | solution.py:82
  49.4 18.6 %collective-permute-start.14 = (bf16[2,96,1024]{2,1,0:T(8,128)(2,1)S(1)}, bf16[2,96,1024]{2,1,0:T(8,128)(2,1)S(1)}, u32[]{:S(2)}, u32[]{:S(2)}) collective-permute-start(bf16[2,96,1024]{2,1,0:T(8,128)(2,1)S(1)} %pad_maximum_fusion.30), channel_id=1, source_target_pairs={{0,4},{1,5},{2,6},{3,7},{4,0},{5,1},{6,2},{7,3},{8,12},{9,13},{10,... | collective-permute-start | bytes 1179656 | tf_op jit(solution)/shard_map/ppermute | solution.py:82
  69.0 20.2 %collective-permute-start.18 = (bf16[4,96,1024]{2,1,0:T(8,128)(2,1)}, bf16[4,96,1024]{2,1,0:T(8,128)(2,1)}, u32[]{:S(2)}, u32[]{:S(2)}) collective-permute-start(bf16[4,96,1024]{2,1,0:T(8,128)(2,1)} %pad_maximum_fusion.12), channel_id=1, source_target_pairs={{0,2},{1,3},{2,0},{3,1},{4,6},{5,7},{6,4},{7,5},{8,10},{9,11},{10,... | collective-permute-start | bytes 2359304 | tf_op jit(solution)/shard_map/ppermute | solution.py:82
  71.6 17.7 %collective-permute-start.17 = (bf16[4,96,512]{2,1,0:T(8,128)(2,1)}, bf16[4,96,512]{2,1,0:T(8,128)(2,1)}, u32[]{:S(2)}, u32[]{:S(2)}) collective-permute-start(bf16[4,96,512]{2,1,0:T(8,128)(2,1)} %pad_maximum_fusion.31), channel_id=1, source_target_pairs={{0,4},{1,5},{2,6},{3,7},{4,0},{5,1},{6,2},{7,3},{8,12},{9,13},{10,... | collective-permute-start | bytes 1179656 | tf_op jit(solution)/shard_map/ppermute | solution.py:82
  75.6 22.5 %collective-permute-start.16 = (bf16[2,2,48,1120]{3,2,0,1:T(8,128)(2,1)S(1)}, bf16[2,2,48,1120]{3,2,0,1:T(8,128)(2,1)S(1)}, u32[]{:S(2)}, u32[]{:S(2)}) collective-permute-start(bf16[2,2,48,1120]{3,2,0,1:T(8,128)(2,1)S(1)} %get-tuple-element.163), channel_id=1, source_target_pairs={{0,8},{1,9},{2,10},{3,11},{4,12},{5,13},{6,14},{7,15},{8,0},{9,1},... | collective-permute-start | bytes 1290248 | tf_op jit(solution)/shard_map/ppermute | solution.py:82
  101.2 19.5 %collective-permute-start.21 = (bf16[4,48,1120]{2,1,0:T(8,128)(2,1)}, bf16[4,48,1120]{2,1,0:T(8,128)(2,1)}, u32[]{:S(2)}, u32[]{:S(2)}) collective-permute-start(bf16[4,48,1120]{2,1,0:T(8,128)(2,1)} %get-tuple-element.173), channel_id=1, source_target_pairs={{0,4},{1,5},{2,6},{3,7},{4,0},{5,1},{6,2},{7,3},{8,12},{9,13},{10,... | collective-permute-start | bytes 1290248 | tf_op jit(solution)/shard_map/ppermute | solution.py:82
  103.4 22.8 %collective-permute-start.23 = (bf16[2,2,48,1120]{3,2,0,1:T(8,128)(2,1)S(1)}, bf16[2,2,48,1120]{3,2,0,1:T(8,128)(2,1)S(1)}, u32[]{:S(2)}, u32[]{:S(2)}) collective-permute-start(bf16[2,2,48,1120]{3,2,0,1:T(8,128)(2,1)S(1)} %get-tuple-element.176), channel_id=1, source_target_pairs={{0,8},{1,9},{2,10},{3,11},{4,12},{5,13},{6,14},{7,15},{8,0},{9,1},... | collective-permute-start | bytes 1290248 | tf_op jit(solution)/shard_map/ppermute | solution.py:82
  121.8 24.4 %collective-permute-start.24 = (bf16[8,48,1120]{2,1,0:T(8,128)(2,1)S(1)}, bf16[8,48,1120]{2,1,0:T(8,128)(2,1)S(1)}, u32[]{:S(2)}, u32[]{:S(2)}) collective-permute-start(bf16[8,48,1120]{2,1,0:T(8,128)(2,1)S(1)} %pad_maximum_fusion.5.refs_0_), channel_id=1, source_target_pairs={{0,16},{16,0},{1,17},{17,1},{2,18},{18,2},{3,19},{19,3},{4,20},{20... | collective-permute-start | bytes 2580488 | tf_op jit(solution)/shard_map/ppermute | solution.py:80
  126.3 20.0 %collective-permute-start.25 = (bf16[4,48,1120]{2,1,0:T(8,128)(2,1)S(1)}, bf16[4,48,1120]{2,1,0:T(8,128)(2,1)S(1)}, u32[]{:S(2)}, u32[]{:S(2)}) collective-permute-start(bf16[4,48,1120]{2,1,0:T(8,128)(2,1)S(1)} %get-tuple-element.180), channel_id=1, source_target_pairs={{0,4},{1,5},{2,6},{3,7},{4,0},{5,1},{6,2},{7,3},{8,12},{9,13},{10,... | collective-permute-start | bytes 1290248 | tf_op jit(solution)/shard_map/ppermute | solution.py:82
  126.3 19.9 %collective-permute-start.22 = (bf16[1,128,1536]{2,1,0:T(8,128)(2,1)S(1)}, bf16[1,128,1536]{2,1,0:T(8,128)(2,1)S(1)}, u32[]{:S(2)}, u32[]{:S(2)}) collective-permute-start(bf16[1,128,1536]{2,1,0:T(8,128)(2,1)S(1)} %bitcast.335), channel_id=1, source_target_pairs={{0,8},{1,9},{2,10},{3,11},{4,12},{5,13},{6,14},{7,15},{8,0},{9,1},... | collective-permute-start | bytes 1179656 | tf_op jit(solution)/shard_map/ppermute | solution.py:82
  158.1 31.3 %collective-permute-start.33 = (bf16[16,48,1120]{2,1,0:T(8,128)(2,1)S(1)}, bf16[16,48,1120]{2,1,0:T(8,128)(2,1)S(1)}, u32[]{:S(2)}, u32[]{:S(2)}) collective-permute-start(bf16[16,48,1120]{2,1,0:T(8,128)(2,1)S(1)} %pad_maximum_fusion.1), channel_id=1, source_target_pairs={{0,1},{1,0},{2,3},{3,2},{4,5},{5,4},{6,7},{7,6},{8,9},{9,8},{10,11... | collective-permute-start | bytes 5160968 | tf_op jit(solution)/shard_map/ppermute | solution.py:82
  158.3 22.1 %collective-permute-start.29 = (bf16[8,48,1120]{2,1,0:T(8,128)(2,1)S(1)}, bf16[8,48,1120]{2,1,0:T(8,128)(2,1)S(1)}, u32[]{:S(2)}, u32[]{:S(2)}) collective-permute-start(bf16[8,48,1120]{2,1,0:T(8,128)(2,1)S(1)} %pad_maximum_fusion.6.refs_3_), channel_id=1, source_target_pairs={{0,16},{16,0},{1,17},{17,1},{2,18},{18,2},{3,19},{19,3},{4,20},{20... | collective-permute-start | bytes 2580488 | tf_op jit(solution)/shard_map/ppermute | solution.py:80
  160.0 27.6 %collective-permute-start.31 = (bf16[4,64,1536]{2,1,0:T(8,128)(2,1)S(1)}, bf16[4,64,1536]{2,1,0:T(8,128)(2,1)S(1)}, u32[]{:S(2)}, u32[]{:S(2)}) collective-permute-start(bf16[4,64,1536]{2,1,0:T(8,128)(2,1)S(1)} %pad_maximum_fusion.13), channel_id=1, source_target_pairs={{0,2},{1,3},{2,0},{3,1},{4,6},{5,7},{6,4},{7,5},{8,10},{9,11},{10,... | collective-permute-start | bytes 2359304 | tf_op jit(solution)/shard_map/ppermute | solution.py:82
  160.6 27.8 %collective-permute-start.32 = (bf16[4,64,1536]{2,1,0:T(8,128)(2,1)S(1)}, bf16[4,64,1536]{2,1,0:T(8,128)(2,1)S(1)}, u32[]{:S(2)}, u32[]{:S(2)}) collective-permute-start(bf16[4,64,1536]{2,1,0:T(8,128)(2,1)S(1)} %pad_maximum_fusion.14), channel_id=1, source_target_pairs={{0,4},{1,5},{2,6},{3,7},{4,0},{5,1},{6,2},{7,3},{8,12},{9,13},{10,... | collective-permute-start | bytes 2359304 | tf_op jit(solution)/shard_map/ppermute | solution.py:82
  162.3 25.3 %collective-permute-start.28 = (bf16[1,128,1536]{2,1,0:T(8,128)(2,1)S(1)}, bf16[1,128,1536]{2,1,0:T(8,128)(2,1)S(1)}, u32[]{:S(2)}, u32[]{:S(2)}) collective-permute-start(bf16[1,128,1536]{2,1,0:T(8,128)(2,1)S(1)} %copy-done.14), channel_id=1, source_target_pairs={{0,8},{1,9},{2,10},{3,11},{4,12},{5,13},{6,14},{7,15},{8,0},{9,1},... | collective-permute-start | bytes 1179656 | tf_op jit(solution)/shard_map/ppermute | solution.py:82
  190.6 16.2 %collective-permute-start.36 = (bf16[16,48,1120]{2,1,0:T(8,128)(2,1)}, bf16[16,48,1120]{2,1,0:T(8,128)(2,1)}, u32[]{:S(2)}, u32[]{:S(2)}) collective-permute-start(bf16[16,48,1120]{2,1,0:T(8,128)(2,1)} %pad_maximum_fusion.2), channel_id=1, source_target_pairs={{0,1},{1,0},{2,3},{3,2},{4,5},{5,4},{6,7},{7,6},{8,9},{9,8},{10,11... | collective-permute-start | bytes 5160968 | tf_op jit(solution)/shard_map/ppermute | solution.py:82
  206.8 25.9 %collective-permute-start.37 = (bf16[4,64,1536]{2,1,0:T(8,128)(2,1)S(1)}, bf16[4,64,1536]{2,1,0:T(8,128)(2,1)S(1)}, u32[]{:S(2)}, u32[]{:S(2)}) collective-permute-start(bf16[4,64,1536]{2,1,0:T(8,128)(2,1)S(1)} %pad_maximum_fusion.15), channel_id=1, source_target_pairs={{0,2},{1,3},{2,0},{3,1},{4,6},{5,7},{6,4},{7,5},{8,10},{9,11},{10,... | collective-permute-start | bytes 2359304 | tf_op jit(solution)/shard_map/ppermute | solution.py:82
  208.4 24.4 %collective-permute-start.38 = (bf16[4,64,1536]{2,1,0:T(8,128)(2,1)S(1)}, bf16[4,64,1536]{2,1,0:T(8,128)(2,1)S(1)}, u32[]{:S(2)}, u32[]{:S(2)}) collective-permute-start(bf16[4,64,1536]{2,1,0:T(8,128)(2,1)S(1)} %pad_maximum_fusion.16), channel_id=1, source_target_pairs={{0,4},{1,5},{2,6},{3,7},{4,0},{5,1},{6,2},{7,3},{8,12},{9,13},{10,... | collective-permute-start | bytes 2359304 | tf_op jit(solution)/shard_map/ppermute | solution.py:82
  250.0 18.7 %collective-permute-start.40 = (bf16[256,1536]{1,0:T(8,128)(2,1)S(1)}, bf16[256,1536]{1,0:T(8,128)(2,1)S(1)}, u32[]{:S(2)}, u32[]{:S(2)}) collective-permute-start(bf16[256,1536]{1,0:T(8,128)(2,1)S(1)} %get-tuple-element.201), channel_id=1, source_target_pairs={{0,4},{1,5},{2,6},{3,7},{4,0},{5,1},{6,2},{7,3},{8,12},{9,13},{10,... | collective-permute-start | bytes 2359304 | tf_op jit(solution)/shard_map/ppermute | solution.py:82
  250.6 18.3 %collective-permute-start.39 = (bf16[256,1536]{1,0:T(8,128)(2,1)S(1)}, bf16[256,1536]{1,0:T(8,128)(2,1)S(1)}, u32[]{:S(2)}, u32[]{:S(2)}) collective-permute-start(bf16[256,1536]{1,0:T(8,128)(2,1)S(1)} %get-tuple-element.199), channel_id=1, source_target_pairs={{0,2},{1,3},{2,0},{3,1},{4,6},{5,7},{6,4},{7,5},{8,10},{9,11},{10,... | collective-permute-start | bytes 2359304 | tf_op jit(solution)/shard_map/ppermute | solution.py:82
  288.8 21.1 %collective-permute-start.45 = (bf16[1,128,1536]{2,1,0:T(8,128)(2,1)S(1)}, bf16[1,128,1536]{2,1,0:T(8,128)(2,1)}, u32[]{:S(2)}, u32[]{:S(2)}) collective-permute-start(bf16[1,128,1536]{2,1,0:T(8,128)(2,1)S(1)} %fusion.26), channel_id=1, source_target_pairs={{0,8},{1,9},{2,10},{3,11},{4,12},{5,13},{6,14},{7,15},{8,0},{9,1},... | collective-permute-start | bytes 1179656 | tf_op jit(solution)/shard_map/ppermute | solution.py:82
  290.4 35.9 %collective-permute-start.44 = (bf16[256,1536]{1,0:T(8,128)(2,1)}, bf16[256,1536]{1,0:T(8,128)(2,1)}, u32[]{:S(2)}, u32[]{:S(2)}) collective-permute-start(bf16[256,1536]{1,0:T(8,128)(2,1)} %convolution_convert_fusion.3), channel_id=1, source_target_pairs={{0,2},{1,3},{2,0},{3,1},{4,6},{5,7},{6,4},{7,5},{8,10},{9,11},{10,... | collective-permute-start | bytes 2359304 | tf_op jit(solution)/shard_map/ppermute | solution.py:82
  290.9 35.4 %collective-permute-start.47 = (bf16[256,1536]{1,0:T(8,128)(2,1)}, bf16[256,1536]{1,0:T(8,128)(2,1)}, u32[]{:S(2)}, u32[]{:S(2)}) collective-permute-start(bf16[256,1536]{1,0:T(8,128)(2,1)} %convolution_convert_fusion.2), channel_id=1, source_target_pairs={{0,4},{1,5},{2,6},{3,7},{4,0},{5,1},{6,2},{7,3},{8,12},{9,13},{10,... | collective-permute-start | bytes 2359304 | tf_op jit(solution)/shard_map/ppermute | solution.py:82
  293.8 29.5 %collective-permute-start.46 = (bf16[8,48,1120]{2,1,0:T(8,128)(2,1)}, bf16[8,48,1120]{2,1,0:T(8,128)(2,1)}, u32[]{:S(2)}, u32[]{:S(2)}) collective-permute-start(bf16[8,48,1120]{2,1,0:T(8,128)(2,1)} %fusion.10), channel_id=1, source_target_pairs={{0,16},{16,0},{1,17},{17,1},{2,18},{18,2},{3,19},{19,3},{4,20},{20... | collective-permute-start | bytes 2580488 | tf_op jit(solution)/shard_map/ppermute | solution.py:80
  294.3 32.0 %collective-permute-start.48 = (bf16[2,8,48,1120]{3,2,1,0:T(8,128)(2,1)}, bf16[2,8,48,1120]{3,2,1,0:T(8,128)(2,1)}, u32[]{:S(2)}, u32[]{:S(2)}) collective-permute-start(bf16[2,8,48,1120]{3,2,1,0:T(8,128)(2,1)} %get-tuple-element.225), channel_id=1, source_target_pairs={{0,1},{1,0},{2,3},{3,2},{4,5},{5,4},{6,7},{7,6},{8,9},{9,8},{10,11... | collective-permute-start | bytes 5160968 | tf_op jit(solution)/shard_map/ppermute | solution.py:82
  326.9 22.4 %collective-permute-start.52 = (bf16[1,2,2,48,1120]{4,3,0,2,1:T(8,128)(2,1)}, bf16[1,2,2,48,1120]{4,3,0,2,1:T(8,128)(2,1)}, u32[]{:S(2)}, u32[]{:S(2)}) collective-permute-start(bf16[1,2,2,48,1120]{4,3,0,2,1:T(8,128)(2,1)} %get-tuple-element.233), channel_id=1, source_target_pairs={{0,8},{1,9},{2,10},{3,11},{4,12},{5,13},{6,14},{7,15},{8,0},{9,1},... | collective-permute-start | bytes 1290248 | tf_op jit(solution)/shard_map/ppermute | solution.py:82
  330.0 27.8 %collective-permute-start.53 = (bf16[8,48,1120]{2,1,0:T(8,128)(2,1)}, bf16[8,48,1120]{2,1,0:T(8,128)(2,1)}, u32[]{:S(2)}, u32[]{:S(2)}) collective-permute-start(bf16[8,48,1120]{2,1,0:T(8,128)(2,1)} %fusion.11), channel_id=1, source_target_pairs={{0,16},{16,0},{1,17},{17,1},{2,18},{18,2},{3,19},{19,3},{4,20},{20... | collective-permute-start | bytes 2580488 | tf_op jit(solution)/shard_map/ppermute | solution.py:80
  348.9 15.6 %collective-permute-start.54 = (bf16[768,2048]{1,0:T(8,128)(2,1)S(1)}, bf16[768,2048]{1,0:T(8,128)(2,1)S(1)}, u32[]{:S(2)}, u32[]{:S(2)}) collective-permute-start(bf16[768,2048]{1,0:T(8,128)(2,1)S(1)} %convolution_convert_fusion.1), channel_id=1, source_target_pairs={{0,1},{1,0},{2,3},{3,2},{4,5},{5,4},{6,7},{7,6},{8,9},{9,8},{10,11... | collective-permute-start | bytes 9437192 | tf_op jit(solution)/shard_map/ppermute | solution.py:82
  364.4 19.5 %collective-permute-start.56 = (bf16[1,128,1536]{2,1,0:T(8,128)(2,1)S(1)}, bf16[1,128,1536]{2,1,0:T(8,128)(2,1)S(1)}, u32[]{:S(2)}, u32[]{:S(2)}) collective-permute-start(bf16[1,128,1536]{2,1,0:T(8,128)(2,1)S(1)} %fusion.25), channel_id=1, source_target_pairs={{0,8},{1,9},{2,10},{3,11},{4,12},{5,13},{6,14},{7,15},{8,0},{9,1},... | collective-permute-start | bytes 1179656 | tf_op jit(solution)/shard_map/ppermute | solution.py:82
  365.4 27.8 %collective-permute-start.59 = (bf16[768,1536]{1,0:T(8,128)(2,1)S(1)}, bf16[768,1536]{1,0:T(8,128)(2,1)S(1)}, u32[]{:S(2)}, u32[]{:S(2)}) collective-permute-start(bf16[768,1536]{1,0:T(8,128)(2,1)S(1)} %copy-done.72), channel_id=1, source_target_pairs={{0,1},{1,0},{2,3},{3,2},{4,5},{5,4},{6,7},{7,6},{8,9},{9,8},{10,11... | collective-permute-start | bytes 7077896 | tf_op jit(solution)/shard_map/ppermute | solution.py:82
  366.4 24.1 %collective-permute-start.58 = (bf16[2,2,2,48,768]{4,3,2,1,0:T(8,128)(2,1)S(1)}, bf16[2,2,2,48,768]{4,3,2,1,0:T(8,128)(2,1)S(1)}, u32[]{:S(2)}, u32[]{:S(2)}) collective-permute-start(bf16[2,2,2,48,768]{4,3,2,1,0:T(8,128)(2,1)S(1)} %slice_bitcast_fusion.11), channel_id=1, source_target_pairs={{0,4},{1,5},{2,6},{3,7},{4,0},{5,1},{6,2},{7,3},{8,12},{9,13},{10,... | collective-permute-start | bytes 1769480 | tf_op jit(solution)/shard_map/ppermute | solution.py:82
  367.7 26.4 %collective-permute-start.60 = (bf16[280,1536]{1,0:T(8,128)(2,1)S(1)}, bf16[280,1536]{1,0:T(8,128)(2,1)S(1)}, u32[]{:S(2)}, u32[]{:S(2)}) collective-permute-start(bf16[280,1536]{1,0:T(8,128)(2,1)S(1)} %get-tuple-element.255), channel_id=1, source_target_pairs={{0,16},{16,0},{1,17},{17,1},{2,18},{18,2},{3,19},{19,3},{4,20},{20... | collective-permute-start | bytes 2580488 | tf_op jit(solution)/shard_map/ppermute | solution.py:80
  369.2 23.6 %collective-permute-start.57 = (bf16[2,2,2,48,1280]{4,3,2,1,0:T(8,128)(2,1)S(1)}, bf16[2,2,2,48,1280]{4,3,2,1,0:T(8,128)(2,1)S(1)}, u32[]{:S(2)}, u32[]{:S(2)}) collective-permute-start(bf16[2,2,2,48,1280]{4,3,2,1,0:T(8,128)(2,1)S(1)} %slice_bitcast_fusion.6), channel_id=1, source_target_pairs={{0,2},{1,3},{2,0},{3,1},{4,6},{5,7},{6,4},{7,5},{8,10},{9,11},{10,... | collective-permute-start | bytes 2949128 | tf_op jit(solution)/shard_map/ppermute | solution.py:82
  394.8 14.1 %collective-permute-start.62 = (bf16[2,2,48,1280]{3,2,1,0:T(8,128)(2,1)S(1)}, bf16[2,2,48,1280]{3,2,1,0:T(8,128)(2,1)S(1)}, u32[]{:S(2)}, u32[]{:S(2)}) collective-permute-start(bf16[2,2,48,1280]{3,2,1,0:T(8,128)(2,1)S(1)} %fusion.35), channel_id=1, source_target_pairs={{0,4},{1,5},{2,6},{3,7},{4,0},{5,1},{6,2},{7,3},{8,12},{9,13},{10,... | collective-permute-start | bytes 1474568 | tf_op jit(solution)/shard_map/ppermute | solution.py:82
  395.8 21.7 %collective-permute-start.64 = (bf16[2,2,48,1120]{3,2,0,1:T(8,128)(2,1)S(1)}, bf16[2,2,48,1120]{3,2,0,1:T(8,128)(2,1)S(1)}, u32[]{:S(2)}, u32[]{:S(2)}) collective-permute-start(bf16[2,2,48,1120]{3,2,0,1:T(8,128)(2,1)S(1)} %get-tuple-element.259), channel_id=1, source_target_pairs={{0,4},{1,5},{2,6},{3,7},{4,0},{5,1},{6,2},{7,3},{8,12},{9,13},{10,... | collective-permute-start | bytes 1290248 | tf_op jit(solution)/shard_map/ppermute | solution.py:82
  396.9 20.6 %collective-permute-start.65 = (bf16[1,2,2,48,1120]{4,3,0,1,2:T(8,128)(2,1)S(1)}, bf16[1,2,2,48,1120]{4,3,0,1,2:T(8,128)(2,1)S(1)}, u32[]{:S(2)}, u32[]{:S(2)}) collective-permute-start(bf16[1,2,2,48,1120]{4,3,0,1,2:T(8,128)(2,1)S(1)} %bitcast.382), channel_id=1, source_target_pairs={{0,2},{1,3},{2,0},{3,1},{4,6},{5,7},{6,4},{7,5},{8,10},{9,11},{10,... | collective-permute-start | bytes 1290248 | tf_op jit(solution)/shard_map/ppermute | solution.py:82
  417.6 19.8 %collective-permute-start.67 = (bf16[1,2,48,2048]{3,2,1,0:T(8,128)(2,1)S(1)}, bf16[1,2,48,2048]{3,2,1,0:T(8,128)(2,1)S(1)}, u32[]{:S(2)}, u32[]{:S(2)}) collective-permute-start(bf16[1,2,48,2048]{3,2,1,0:T(8,128)(2,1)S(1)} %fusion.13), channel_id=1, source_target_pairs={{0,8},{1,9},{2,10},{3,11},{4,12},{5,13},{6,14},{7,15},{8,0},{9,1},... | collective-permute-start | bytes 1179656 | tf_op jit(solution)/shard_map/ppermute | solution.py:82
  420.6 16.9 %collective-permute-start.68 = (bf16[4,48,1120]{2,1,0:T(8,128)(2,1)S(1)}, bf16[4,48,1120]{2,1,0:T(8,128)(2,1)S(1)}, u32[]{:S(2)}, u32[]{:S(2)}) collective-permute-start(bf16[4,48,1120]{2,1,0:T(8,128)(2,1)S(1)} %get-tuple-element.263), channel_id=1, source_target_pairs={{0,2},{1,3},{2,0},{3,1},{4,6},{5,7},{6,4},{7,5},{8,10},{9,11},{10,... | collective-permute-start | bytes 1290248 | tf_op jit(solution)/shard_map/ppermute | solution.py:82
  421.2 18.5 %collective-permute-start.69 = (bf16[2,2,48,1120]{3,2,0,1:T(8,128)(2,1)S(1)}, bf16[2,2,48,1120]{3,2,0,1:T(8,128)(2,1)S(1)}, u32[]{:S(2)}, u32[]{:S(2)}) collective-permute-start(bf16[2,2,48,1120]{3,2,0,1:T(8,128)(2,1)S(1)} %get-tuple-element.264), channel_id=1, source_target_pairs={{0,4},{1,5},{2,6},{3,7},{4,0},{5,1},{6,2},{7,3},{8,12},{9,13},{10,... | collective-permute-start | bytes 1290248 | tf_op jit(solution)/shard_map/ppermute | solution.py:82
  422.9 19.5 %collective-permute-start.70 = (bf16[280,1536]{1,0:T(8,128)(2,1)}, bf16[280,1536]{1,0:T(8,128)(2,1)S(1)}, u32[]{:S(2)}, u32[]{:S(2)}) collective-permute-start(bf16[280,1536]{1,0:T(8,128)(2,1)} %get-tuple-element.265), channel_id=1, source_target_pairs={{0,16},{16,0},{1,17},{17,1},{2,18},{18,2},{3,19},{19,3},{4,20},{20... | collective-permute-start | bytes 2580488 | tf_op jit(solution)/shard_map/ppermute | solution.py:80
  447.5 21.6 %collective-permute-start.76 = (bf16[4,48,1120]{2,1,0:T(8,128)(2,1)S(1)}, bf16[4,48,1120]{2,1,0:T(8,128)(2,1)S(1)}, u32[]{:S(2)}, u32[]{:S(2)}) collective-permute-start(bf16[4,48,1120]{2,1,0:T(8,128)(2,1)S(1)} %get-tuple-element.271), channel_id=1, source_target_pairs={{0,8},{1,9},{2,10},{3,11},{4,12},{5,13},{6,14},{7,15},{8,0},{9,1},... | collective-permute-start | bytes 1290248 | tf_op jit(solution)/shard_map/ppermute | solution.py:82
  448.4 16.0 %collective-permute-start.73 = (bf16[2,2,2,48,1024]{4,3,2,1,0:T(8,128)(2,1)S(1)}, bf16[2,2,2,48,1024]{4,3,2,1,0:T(8,128)(2,1)S(1)}, u32[]{:S(2)}, u32[]{:S(2)}) collective-permute-start(bf16[2,2,2,48,1024]{4,3,2,1,0:T(8,128)(2,1)S(1)} %slice_bitcast_fusion.9), channel_id=1, source_target_pairs={{0,2},{1,3},{2,0},{3,1},{4,6},{5,7},{6,4},{7,5},{8,10},{9,11},{10,... | collective-permute-start | bytes 2359304 | tf_op jit(solution)/shard_map/ppermute | solution.py:82
  449.6 29.0 %collective-permute-start.77 = (bf16[48,8960]{1,0:T(8,128)(2,1)S(1)}, bf16[48,8960]{1,0:T(8,128)(2,1)S(1)}, u32[]{:S(2)}, u32[]{:S(2)}) collective-permute-start(bf16[48,8960]{1,0:T(8,128)(2,1)S(1)} %shard_map.193.gate), channel_id=1, source_target_pairs={{0,16},{16,0},{1,17},{17,1},{2,18},{18,2},{3,19},{19,3},{4,20},{20... | collective-permute-start | bytes 2580488 | tf_op jit(solution)/shard_map/ppermute | solution.py:80
  481.0 15.5 %collective-permute-start.83 = (bf16[48,8960]{1,0:T(8,128)(2,1)S(1)}, bf16[48,8960]{1,0:T(8,128)(2,1)S(1)}, u32[]{:S(2)}, u32[]{:S(2)}) collective-permute-start(bf16[48,8960]{1,0:T(8,128)(2,1)S(1)} %shard_map.194.up), channel_id=1, source_target_pairs={{0,16},{16,0},{1,17},{17,1},{2,18},{18,2},{3,19},{19,3},{4,20},{20... | collective-permute-start | bytes 2580488 | tf_op jit(solution)/shard_map/ppermute | solution.py:80
  (145 other events, 1165.0 us)

commit v4 on v3

--- a/solution.py
+++ b/solution.py
@@ -284,12 +284,12 @@
         count //= 2
         (got,) = yield [(bit, state[count:].astype(bf16))]
         state = add(state[:count], got)
-    (got,) = yield [("y", state[0, 1].astype(bf16))]
-    mine = add(state[0, 0], got).astype(bf16)
+    mine = state[0].astype(bf16)
     (other,) = yield [("y", mine)]
-    low = jnp.where(s == 0, mine, other)
-    high = jnp.where(s == 0, other, mine)
-    return join(low, high).astype(f32)
+    near, far_half = add(mine[0], other[1]), add(mine[1], other[0])
+    low = jnp.where(s == 0, near, far_half)
+    high = jnp.where(s == 0, far_half, near)
+    return join(low, high)
 
 
 def sum_everywhere(value):
@@ -326,18 +326,14 @@
 
 def weave_kernel(unit, where, *refs):
     out = refs[-1]
-    half, padded = out.shape[1], out.shape[2] // 2
+    half, padded = out.shape[1:]
     at = 0
-    for part in range(2):
-        low = part * padded
-        for ref in refs[3 * part : 3 * part + 3]:
-            for i in range(ref.shape[0]):
-                out[where[at], :, low : low + unit] = ref[i]
-                if padded > unit:
-                    out[where[at], :, low + unit : low + padded] = jnp.zeros(
-                        (half, padded - unit), out.dtype
-                    )
-                at += 1
+    for ref in refs[:-1]:
+        for i in range(ref.shape[0]):
+            out[where[at], :, :unit] = ref[i]
+            if padded > unit:
+                out[where[at], :, unit:] = jnp.zeros((half, padded - unit), out.dtype)
+            at += 1
 
 
 def split_gate_up(shard, me, s):
@@ -360,23 +356,21 @@
     return [mine, other, got], marks
 
 
-def weave_gate_up(parts, me, s):
+def weave_part(blocks, marks, me, s):
     size = lax.axis_size("fsdp")
-    half, unit = parts[0][0][0].shape[1:]
+    half, unit = blocks[0].shape[1:]
     padded = -(-unit // 384) * 384
-    pieces, where = [], []
-    for blocks, marks in parts:
-        pieces += blocks
-        for core in range(2):
-            for h in range(2):
-                where += [(me ^ f ^ core) * 2 + (s ^ h) for f in marks]
+    where = []
+    for core in range(2):
+        for h in range(2):
+            where += [(me ^ f ^ core) * 2 + (s ^ h) for f in marks]
     whole = whole_call(
         functools.partial(weave_kernel, unit),
-        jax.ShapeDtypeStruct((size * 2, half, 2 * padded), bf16),
+        jax.ShapeDtypeStruct((size * 2, half, padded), bf16),
         where,
-        pieces,
-    )
-    return whole.reshape(size * 2 * half, 2 * padded)
+        blocks,
+    )
+    return whole.reshape(size * 2 * half, padded)
 
 
 def grad_kernel(count, unit, at, *refs):
@@ -689,7 +683,7 @@
         in_specs=[piece] * 4
         + [
             pl.BlockSpec((D, tile), lambda j: (0, j)),
-            pl.BlockSpec((D, tile), lambda j: (0, j + steps)),
+            pl.BlockSpec((D, tile), lambda j: (0, j)),
             pl.BlockSpec((tile, D), lambda j: (j, 0)),
         ],
         out_specs=(part, part, part, whole, whole, piece, piece),
@@ -700,7 +694,7 @@
             bytes_accessed=6 * D * padded + 8 * rows * D + 6 * rows * padded,
             transcendentals=rows * padded,
         ),
-    )(*tokens, *cotangent, gate_up_weight, gate_up_weight, down_weight)
+    )(*tokens, *cotangent, *gate_up_weight, down_weight)
 
 
 def pair_kernel(at, own, other, out):
@@ -744,13 +738,13 @@
     cot_blocks, token_blocks = [], []
     qkv = Move(gather_weight(qkv_weight, me, s))
     out = Move(gather_weight_plain(out_weight, me))
-    gate = Move(shuffle_part(gate_blocks, [X] + far + [Z]))
-    up = Move(shuffle_part(up_blocks, [X] + far + [Z]))
+    gate = Move(shuffle_part(gate_blocks, [X, *far, Z]))
+    up = Move(shuffle_part(up_blocks, [X, *far, Z]))
     cot = Move(gather_tokens(grad_rows, cot_blocks))
     down = Move(swap(CORE, down_weight))
-    lanes.round(qkv, up)
-    lanes.round(qkv, (out, 2), gate)
-    lanes.round(qkv)
+    lanes.round(qkv, (up, 2))
+    lanes.round(qkv, (out, 2))
+    lanes.round(qkv, gate)
     lanes.round(qkv, out, (gate, 2))
     lanes.round(qkv, out)
     (qkv_full,) = lanes.drain(qkv)
@@ -785,11 +779,11 @@
     lanes.beside(normed_two)
     token = Move(gather_tokens(normed_two, token_blocks))
     lanes.round(token, gate, up)
-    lanes.round(token, (cot, 2), (up, 2), down)
-    lanes.round(token, gate)
+    lanes.round(down, (up, 2), (cot, 2))
+    lanes.round(token, (gate, 3))
     lanes.round(cot, up)
     parts = lanes.drain(gate, up)
-    gate_up_full = weave_gate_up(parts, me, s)
+    gate_full, up_full = [weave_part(*part, me, s) for part in parts]
     (other_down,) = lanes.drain(down)
     down_full = whole_call(
         pair_kernel,
@@ -798,11 +792,11 @@
         [down_weight, other_down],
     )
     lanes.drain(token, cot)
-    early = feed_forward(token_blocks[0], cot_blocks[0], gate_up_full, down_full, f32)
+    early = feed_forward(token_blocks[0], cot_blocks[0], (gate_full, up_full), down_full, f32)
     last = feed_forward(
         [after(token_blocks[1][0], early[5]), token_blocks[1][1]],
         cot_blocks[1],
-        gate_up_full,
+        (gate_full, up_full),
         down_full,
         bf16,
     )
@@ -812,13 +806,13 @@
     half = last[5].shape[0]
     gate_terms = gate_up_grad([early[3], last[3]], [early[1], last[1]], me, s)
     out_terms = [[dot(v[0][:half], down_full), dot(v[0][half:], down_full)] for v in (early, last)]
-    gate = Move(unshuffle_part(gate_terms, far + [Z, X], me))
+    gate = Move(unshuffle_part(gate_terms, [*far, Z, X], me))
     result = Move(scatter_tokens(out_terms[0], [term.astype(bf16) for term in out_terms[1]]))
     lanes.round(back, gate)
     up_terms = gate_up_grad(
         [early[3], last[3]], [lanes.hold(early[2]), lanes.hold(last[2])], me, s
     )
-    up = Move(unshuffle_part(up_terms, [X, Z] + far, me))
+    up = Move(unshuffle_part(up_terms, [X, Z, *far], me))
     attended_turned = turn_rows(lanes.hold(attended), me, s)
     normed_turned = turn_rows(lanes.hold(normed), me, s)
     lanes.round(back, gate, result, up)

time: 512 us -> 497 us (0.971)
  waiting for transfers between devices: 219 us -> 207 us
  local copies, waits for them, and re-layouts: 38.9 us -> 32.5 us
    ppermute x68, waiting for transfers between devices: 188 us -> 179 us  [more(): value = lax.ppermute(value, 'fsdp', [(i, i ^ link) for i in range(size)])]
    unnamed x211 -> x193, local copies, waits for them, and re-layouts: 23.1 us -> 16.7 us
    concatenate x27 -> x29, other arithmetic: 11.5 us -> 16.1 us  [join(): return jnp.concatenate(pieces, axis=axis)]
    ppermute x18 -> x16, starting transfers between devices: 19.6 us -> 17 us  [more(): value = lax.ppermute(value, 'seq', [(0, 1), (1, 0)])]
    pallas_call x14 -> x15, Pallas kernels: 50.7 us -> 53.1 us  [whole_call(): pl.pallas_call(kernel, out_shape=out_shape, in_specs=[pl.BlockSpec(memory...]
    ppermute x18 -> x16, waiting for transfers between devices: 30.6 us -> 28.8 us  [more(): value = lax.ppermute(value, 'seq', [(0, 1), (1, 0)])]
  transfers between devices with their start and end apart: 86 -> 84, of which waited for: 43 -> 43; matrix products, arithmetic and copies ran while one was open for 14% -> 16% of each run, Pallas kernels for 16% -> 17%
where the time goes in v4:
time: 497 us; the launch traced here: 493 us
  waiting for transfers between devices  207 us (42%)
  Pallas kernels  104 us (21%)
  starting transfers between devices  80.6 us (16%)
  other arithmetic  42.5 us (9%)
  local copies, waits for them, and re-layouts  32.5 us (7%)
  matrix products  23.4 us (5%)
    ppermute x68, waiting for transfers between devices, more(): value = lax.ppermute(value, 'fsdp', [(i, i ^ link) for i in range(size)])  179 us
    ppermute x68, starting transfers between devices, more(): value = lax.ppermute(value, 'fsdp', [(i, i ^ link) for i in range(size)])  63.6 us
    pallas_call x15, Pallas kernels, whole_call(): pl.pallas_call(kernel, out_shape=out_shape, in_specs=[pl.BlockSpec(memory...  53.1 us
    pallas_call x2, Pallas kernels, feed_forward(): pl.pallas_call(feed_kernel, grid=(steps,), out_shape=(units, units, units...  35.1 us
    ppermute x16, waiting for transfers between devices, more(): value = lax.ppermute(value, 'seq', [(0, 1), (1, 0)])  28.8 us
    ppermute x16, starting transfers between devices, more(): value = lax.ppermute(value, 'seq', [(0, 1), (1, 0)])  17 us
    unnamed x193, local copies, waits for them, and re-layouts  16.7 us
    dot_general x8, matrix products, dot(): return jnp.dot(left, right, preferred_element_type=f32)  16.4 us
  transfers between devices with their start and end apart: 84, of which 43 were waited for; matrix products, arithmetic and copies ran while one was open for 16% of the time, Pallas kernels for 17%

profile of v4, /device:TPU:0, one launch (start us, length us, event | category | flops | bytes accessed | tf_op | source)
XLA Modules:
  0.0 493.1 jit_solution(13772751024485487941)
XLA Ops:
  1.7 4.1 collective-permute-start
  11.1 3.7 collective-permute-done
  19.6 3.4 collective-permute-start.6
  30.6 4.9 collective-permute-done.6
  35.5 5.8 %collective-permute-done.5 = bf16[4,48,640]{2,1,0:T(8,128)(2,1)S(1)} collective-permute-done((bf16[4,48,640]{2,1,0:T(8,128)(2,1)S(1)}, bf16[4,48,640]{2,1,0:T(8,128)(2,1)S(1)}, u32[]{:S(2)}, u32[]{:S(2)}) %collective-permute-start.5) | collective-permute-done | bytes 245792 | tf_op jit(solution)/shard_map/ppermute | solution.py:82
  47.0 9.2 %collective-permute-done.11 = bf16[8,48,640]{2,1,0:T(8,128)(2,1)S(1)} collective-permute-done((bf16[8,48,640]{2,1,0:T(8,128)(2,1)S(1)}, bf16[8,48,640]{2,1,0:T(8,128)(2,1)S(1)}, u32[]{:S(2)}, u32[]{:S(2)}) %collective-permute-start.11) | collective-permute-done | bytes 491552 | tf_op jit(solution)/shard_map/ppermute | solution.py:82
  70.6 5.0 %shard_map.179 = bf16[32,48,2048]{2,1,0:T(8,128)(2,1)} custom-call(s32[32]{0:T(128)S(1)} %stack.444.where, bf16[16,48,2048]{2,1,0:T(8,128)(2,1)S(1)} %pad_maximum_fusion.refs_0_, bf16[16,48,2048]{2,1,0:T(8,128)(2,1)} %collective-permute-done.15.refs_1_), custom_call_target="tpu_custom_call" | custom-call | bytes 12582912 | tf_op jit(solution)/shard_map/pallas_call | solution.py:131
  75.7 4.1 shard_map.180
  79.8 2.7 collective-permute-done.18
  85.0 7.5 %collective-permute-done.16 = bf16[2,2,48,1120]{3,2,0,1:T(8,128)(2,1)S(1)} collective-permute-done((bf16[2,2,48,1120]{3,2,0,1:T(8,128)(2,1)S(1)}, bf16[2,2,48,1120]{3,2,0,1:T(8,128)(2,1)S(1)}, u32[]{:S(2)}, u32[]{:S(2)}) %collective-permute-start.16) | collective-permute-done | bytes 430112 | tf_op jit(solution)/shard_map/ppermute | solution.py:82
  93.2 2.3 fusion.60
  98.8 4.2 shard_map.181
  103.1 7.7 %shard_map.182 = (bf16[128,1536]{1,0:T(8,128)(2,1)S(1)}, f32[128,128]{1,0:T(8,128)S(1)}, f32[128,1536]{1,0:T(8,128)S(1)}, bf16[128,1536]{1,0:T(8,128)(2,1)S(1)}) custom-call(s32[1]{0:T(128)} %bitcast.at, bf16[128,1536]{1,0:T(8,128)(2,1)S(1)} %bitcast.344, bf16[128,1536]{1,0:T(8,128)(2,1)S(1)} %get-tuple-element.159.queries, ...), custom_call_target="tpu_custom_call" | custom-call | flops 1006632960 | bytes 7413248 | tf_op jit(solution)/shard_map/pallas_call | solution.py:131
  110.9 3.4 collective-permute-done.21
  115.5 5.0 %collective-permute-done.23 = bf16[2,2,48,1120]{3,2,0,1:T(8,128)(2,1)S(1)} collective-permute-done((bf16[2,2,48,1120]{3,2,0,1:T(8,128)(2,1)S(1)}, bf16[2,2,48,1120]{3,2,0,1:T(8,128)(2,1)S(1)}, u32[]{:S(2)}, u32[]{:S(2)}) %collective-permute-start.23) | collective-permute-done | bytes 430112 | tf_op jit(solution)/shard_map/ppermute | solution.py:82
  122.7 17.9 %collective-permute-done.22 = bf16[1,128,1536]{2,1,0:T(8,128)(2,1)S(1)} collective-permute-done((bf16[1,128,1536]{2,1,0:T(8,128)(2,1)S(1)}, bf16[1,128,1536]{2,1,0:T(8,128)(2,1)S(1)}, u32[]{:S(2)}, u32[]{:S(2)}) %collective-permute-start.22) | collective-permute-done | bytes 393248 | tf_op jit(solution)/shard_map/ppermute | solution.py:82
  149.4 14.7 %collective-permute-done.30.refs_1_ = bf16[8,48,1120]{2,1,0:T(8,128)(2,1)S(1)} collective-permute-done((bf16[8,48,1120]{2,1,0:T(8,128)(2,1)}, bf16[8,48,1120]{2,1,0:T(8,128)(2,1)S(1)}, u32[]{:S(2)}, u32[]{:S(2)}) %collective-permute-start.30) | collective-permute-done | bytes 860192 | tf_op jit(solution)/shard_map/ppermute | solution.py:80
  167.6 4.0 shard_map.185.down_weight
  174.6 8.7 %collective-permute-done.31 = bf16[2,64,1536]{2,1,0:T(8,128)(2,1)S(1)} collective-permute-done((bf16[2,64,1536]{2,1,0:T(8,128)(2,1)}, bf16[2,64,1536]{2,1,0:T(8,128)(2,1)S(1)}, u32[]{:S(2)}, u32[]{:S(2)}) %collective-permute-start.31) | collective-permute-done | bytes 393248 | tf_op jit(solution)/shard_map/ppermute | solution.py:82
  185.4 2.7 shard_map.183
  192.2 3.3 shard_map.184
  195.5 18.2 %shard_map.186 = (bf16[512,1152]{1,0:T(8,128)(2,1)S(1)}, bf16[512,1152]{1,0:T(8,128)(2,1)S(1)}, bf16[512,1152]{1,0:T(8,128)(2,1)}, bf16[512,1536]{1,0:T(8,128)(2...) custom-call(bf16[256,1536]{1,0:T(8,128)(2,1)S(1)} %bitcast.353, ...), custom_call_target="tpu_custom_call" | custom-call | flops 9059696640 | bytes 20447232 | tf_op jit(solution)/shard_map/pallas_call | solution.py:679
  214.7 9.4 %collective-permute-done.37 = bf16[4,64,1536]{2,1,0:T(8,128)(2,1)S(1)} collective-permute-done((bf16[4,64,1536]{2,1,0:T(8,128)(2,1)S(1)}, bf16[4,64,1536]{2,1,0:T(8,128)(2,1)S(1)}, u32[]{:S(2)}, u32[]{:S(2)}) %collective-permute-start.37) | collective-permute-done | bytes 786464 | tf_op jit(solution)/shard_map/ppermute | solution.py:82
  224.3 16.9 %shard_map.187 = (bf16[512,1152]{1,0:T(8,128)(2,1)S(1)}, bf16[512,1152]{1,0:T(8,128)(2,1)}, bf16[512,1152]{1,0:T(8,128)(2,1)}, bf16[512,1536]{1,0:T(8,128)(2,1)}...) custom-call(bf16[256,1536]{1,0:T(8,128)(2,1)S(1)} %bitcast.364, ...), custom_call_target="tpu_custom_call" | custom-call | flops 9059696640 | bytes 20447232 | tf_op jit(solution)/shard_map/pallas_call | solution.py:679
  245.8 7.7 %shard_map.188 = (bf16[2,8,48,1120]{3,2,1,0:T(8,128)(2,1)}, bf16[2,8,48,1120]{3,2,1,0:T(8,128)(2,1)}) custom-call(s32[2]{0:T(128)S(1)} %get-tuple-element.327.at, bf16[512,1536]{1,0:T(8,128)(2,1)S(1)} %copy-done.36, bf16[512,1536]{1,0:T(8,128)(2,1)S(1)} %copy-done.38, bf16[512,1152]{1,0:T(8,128)(2,1)S(1)} %copy-done.43, bf16[512,1152]{1,0:T(8,128)(2,1)S(1)} %copy-done.44), custom_call_target="tpu_custom_call" | custom-call | flops 3623878656 | bytes 12386304 | tf_op jit(solution)/shard_map/pallas_call | solution.py:403
  253.6 4.2 convolution_convert_fusion.2
  270.3 7.9 %shard_map.190 = (bf16[2,8,48,1120]{3,2,1,0:T(8,128)(2,1)}, bf16[2,8,48,1120]{3,2,1,0:T(8,128)(2,1)}) custom-call(s32[2]{0:T(128)S(1)} %get-tuple-element.327.at, bf16[512,1536]{1,0:T(8,128)(2,1)S(1)} %copy-done.37, bf16[512,1536]{1,0:T(8,128)(2,1)S(1)} %copy-done.39, bf16[512,1152]{1,0:T(8,128)(2,1)S(1)} %copy-done.40, bf16[512,1152]{1,0:T(8,128)(2,1)S(1)} %copy-done.41), custom_call_target="tpu_custom_call" | custom-call | flops 3623878656 | bytes 12386304 | tf_op jit(solution)/shard_map/pallas_call | solution.py:403
  288.0 4.9 %fusion.76 = f32[1152,1536]{1,0:T(8,128)} fusion(bf16[512,1152]{1,0:T(8,128)(2,1)S(1)} %copy-done.32, bf16[512,1536]{1,0:T(8,128)(2,1)S(1)} %copy-done.93), kind=kOutput, calls=%fused_computation.224 | convolution fusion | flops 1811939328 | bytes 9830400 | tf_op jit(solution)/shard_map/dot_general | solution.py:116
  292.9 4.1 fusion
  301.5 8.5 %shard_map.189 = (f32[128,1536]{1,0:T(8,128)S(1)}, bf16[128,1536]{1,0:T(8,128)(2,1)S(1)}, f32[1,1536]{1,0:T(1,128)S(1)}, bf16[128,1536]{1,0:T(8,128)(2,1)S(1)}, ...) custom-call(s32[1]{0:T(128)} %bitcast.at, f32[128,1536]{1,0:T(8,128)S(1)} %fusion.21.grad_normed, ...), custom_call_target="tpu_custom_call" | custom-call | flops 1610612736 | bytes 9516544 | tf_op jit(solution)/shard_map/pallas_call | solution.py:131
  322.5 6.4 %shard_map.191 = (bf16[128,2048]{1,0:T(8,128)(2,1)S(1)}, f32[128,1536]{1,0:T(8,128)}, f32[1,1536]{1,0:T(1,128)S(1)}, f32[1,2048]{1,0:T(1,128)S(1)}) custom-call(s32[1]{0:T(128)} %bitcast.at, bf16[128,1536]{1,0:T(8,128)(2,1)S(1)} %copy-done.20, f32[128,512]{1,0:T(8,128)S(1)} %copy-done.27, bf16[128,512]{1,0:T(8,128)(2,1)S(1)} %collective-permute-done.49.got, ...), custom_call_target="tpu_custom_call" | custom-call | flops 805306368 | bytes 9719808 | tf_op jit(solution)/shard_map/pallas_call | solution.py:131
  329.0 2.3 convolution_add_fusion
  331.4 2.8 convolution_add_fusion.1
  341.2 6.8 %collective-permute-done.50 = bf16[2,64,1536]{2,1,0:T(8,128)(2,1)S(1)} collective-permute-done((bf16[2,64,1536]{2,1,0:T(8,128)(2,1)S(1)}, bf16[2,64,1536]{2,1,0:T(8,128)(2,1)S(1)}, u32[]{:S(2)}, u32[]{:S(2)}) %collective-permute-start.50) | collective-permute-done | bytes 393248 | tf_op jit(solution)/shard_map/ppermute | solution.py:82
  361.2 13.9 %collective-permute-done.56 = bf16[1,128,1536]{2,1,0:T(8,128)(2,1)S(1)} collective-permute-done((bf16[1,128,1536]{2,1,0:T(8,128)(2,1)S(1)}, bf16[1,128,1536]{2,1,0:T(8,128)(2,1)S(1)}, u32[]{:S(2)}, u32[]{:S(2)}) %collective-permute-start.56) | collective-permute-done | bytes 393248 | tf_op jit(solution)/shard_map/ppermute | solution.py:82
  376.0 5.3 %collective-permute-done.58 = bf16[2,2,2,48,768]{4,3,2,1,0:T(8,128)(2,1)S(1)} collective-permute-done((bf16[2,2,2,48,768]{4,3,2,1,0:T(8,128)(2,1)S(1)}, bf16[2,2,2,48,768]{4,3,2,1,0:T(8,128)(2,1)S(1)}, u32[]{:S(2)}, u32[]{:S(2)}) %collective-permute-start.58) | collective-permute-done | bytes 589856 | tf_op jit(solution)/shard_map/ppermute | solution.py:82
  389.2 5.6 %collective-permute-done.63 = bf16[2,2,48,768]{3,2,1,0:T(8,128)(2,1)S(1)} collective-permute-done((bf16[2,2,48,768]{3,2,1,0:T(8,128)(2,1)S(1)}, bf16[2,2,48,768]{3,2,1,0:T(8,128)(2,1)S(1)}, u32[]{:S(2)}, u32[]{:S(2)}) %collective-permute-start.63) | collective-permute-done | bytes 294944 | tf_op jit(solution)/shard_map/ppermute | solution.py:82
  394.9 5.4 %collective-permute-done.62 = bf16[2,2,48,1280]{3,2,1,0:T(8,128)(2,1)S(1)} collective-permute-done((bf16[2,2,48,1280]{3,2,1,0:T(8,128)(2,1)S(1)}, bf16[2,2,48,1280]{3,2,1,0:T(8,128)(2,1)S(1)}, u32[]{:S(2)}, u32[]{:S(2)}) %collective-permute-start.62) | collective-permute-done | bytes 491552 | tf_op jit(solution)/shard_map/ppermute | solution.py:82
  400.4 8.6 %collective-permute-done.64 = bf16[2,2,48,1120]{3,2,0,1:T(8,128)(2,1)S(1)} collective-permute-done((bf16[2,2,48,1120]{3,2,0,1:T(8,128)(2,1)S(1)}, bf16[2,2,48,1120]{3,2,0,1:T(8,128)(2,1)S(1)}, u32[]{:S(2)}, u32[]{:S(2)}) %collective-permute-start.64) | collective-permute-done | bytes 430112 | tf_op jit(solution)/shard_map/ppermute | solution.py:82
  414.1 14.4 %collective-permute-done.67 = bf16[1,2,48,2048]{3,2,1,0:T(8,128)(2,1)S(1)} collective-permute-done((bf16[1,2,48,2048]{3,2,1,0:T(8,128)(2,1)S(1)}, bf16[1,2,48,2048]{3,2,1,0:T(8,128)(2,1)S(1)}, u32[]{:S(2)}, u32[]{:S(2)}) %collective-permute-start.67) | collective-permute-done | bytes 393248 | tf_op jit(solution)/shard_map/ppermute | solution.py:82
  441.1 4.9 collective-permute-done.74
  446.2 3.8 collective-permute-done.72
  450.0 2.6 collective-permute-done.73
  454.7 3.2 collective-permute-done.76
  459.0 4.7 collective-permute-done.75
  467.7 9.9 %collective-permute-done.81 = bf16[1,2,48,1536]{3,2,1,0:T(8,128)(2,1)S(1)} collective-permute-done((bf16[1,2,48,1536]{3,2,1,0:T(8,128)(2,1)S(1)}, bf16[1,2,48,1536]{3,2,1,0:T(8,128)(2,1)S(1)}, u32[]{:S(2)}, u32[]{:S(2)}) %collective-permute-start.81) | collective-permute-done | bytes 294944 | tf_op jit(solution)/shard_map/ppermute | solution.py:82
  477.6 7.1 %collective-permute-done.80 = f32[5120]{0:T(1024)S(1)} collective-permute-done((f32[5120]{0:T(1024)S(1)}, f32[5120]{0:T(1024)S(1)}, u32[]{:S(2)}, u32[]{:S(2)}) %collective-permute-start.80) | collective-permute-done | bytes 20512 | tf_op jit(solution)/shard_map/ppermute | solution.py:80
  488.6 3.3 shard_map.196
  (472 shorter events, 172.9 us)
Async XLA Ops:
  19.6 15.9 %collective-permute-start.6 = (bf16[1,96,1536]{2,1,0:T(8,128)(2,1)S(1)}, bf16[1,96,1536]{2,1,0:T(8,128)(2,1)S(1)}, u32[]{:S(2)}, u32[]{:S(2)}) collective-permute-start(bf16[1,96,1536]{2,1,0:T(8,128)(2,1)S(1)} %bitcast.399), channel_id=1, source_target_pairs={{0,8},{1,9},{2,10},{3,11},{4,12},{5,13},{6,14},{7,15},{8,0},{9,1},... | collective-permute-start | bytes 884744 | tf_op jit(solution)/shard_map/ppermute | solution.py:82
  25.6 15.7 %collective-permute-start.9 = (bf16[1,2,2,48,1120]{4,3,0,2,1:T(8,128)(2,1)S(1)}, bf16[1,2,2,48,1120]{4,3,0,2,1:T(8,128)(2,1)S(1)}, u32[]{:S(2)}, u32[]{:S(2)}) collective-permute-start(bf16[1,2,2,48,1120]{4,3,0,2,1:T(8,128)(2,1)S(1)} %get-tuple-element.152), channel_id=1, source_target_pairs={{0,2},{1,3},{2,0},{3,1},{4,6},{5,7},{6,4},{7,5},{8,10},{9,11},{10,... | collective-permute-start | bytes 1290248 | tf_op jit(solution)/shard_map/ppermute | solution.py:82
  43.7 14.6 %collective-permute-start.12 = (bf16[8,48,768]{2,1,0:T(8,128)(2,1)S(1)}, bf16[8,48,768]{2,1,0:T(8,128)(2,1)S(1)}, u32[]{:S(2)}, u32[]{:S(2)}) collective-permute-start(bf16[8,48,768]{2,1,0:T(8,128)(2,1)S(1)} %pad_maximum_fusion.19), channel_id=1, source_target_pairs={{0,2},{1,3},{2,0},{3,1},{4,6},{5,7},{6,4},{7,5},{8,10},{9,11},{10,... | collective-permute-start | bytes 1769480 | tf_op jit(solution)/shard_map/ppermute | solution.py:82
  46.6 14.7 %collective-permute-start.14 = (bf16[2,96,1024]{2,1,0:T(8,128)(2,1)S(1)}, bf16[2,96,1024]{2,1,0:T(8,128)(2,1)S(1)}, u32[]{:S(2)}, u32[]{:S(2)}) collective-permute-start(bf16[2,96,1024]{2,1,0:T(8,128)(2,1)S(1)} %pad_maximum_fusion.32), channel_id=1, source_target_pairs={{0,4},{1,5},{2,6},{3,7},{4,0},{5,1},{6,2},{7,3},{8,12},{9,13},{10,... | collective-permute-start | bytes 1179656 | tf_op jit(solution)/shard_map/ppermute | solution.py:82
  62.3 20.2 %collective-permute-start.18 = (bf16[4,96,1024]{2,1,0:T(8,128)(2,1)}, bf16[4,96,1024]{2,1,0:T(8,128)(2,1)}, u32[]{:S(2)}, u32[]{:S(2)}) collective-permute-start(bf16[4,96,1024]{2,1,0:T(8,128)(2,1)} %pad_maximum_fusion.12), channel_id=1, source_target_pairs={{0,2},{1,3},{2,0},{3,1},{4,6},{5,7},{6,4},{7,5},{8,10},{9,11},{10,... | collective-permute-start | bytes 2359304 | tf_op jit(solution)/shard_map/ppermute | solution.py:82
  64.6 17.9 %collective-permute-start.17 = (bf16[4,96,512]{2,1,0:T(8,128)(2,1)}, bf16[4,96,512]{2,1,0:T(8,128)(2,1)}, u32[]{:S(2)}, u32[]{:S(2)}) collective-permute-start(bf16[4,96,512]{2,1,0:T(8,128)(2,1)} %pad_maximum_fusion.33), channel_id=1, source_target_pairs={{0,4},{1,5},{2,6},{3,7},{4,0},{5,1},{6,2},{7,3},{8,12},{9,13},{10,... | collective-permute-start | bytes 1179656 | tf_op jit(solution)/shard_map/ppermute | solution.py:82
  69.9 22.5 %collective-permute-start.16 = (bf16[2,2,48,1120]{3,2,0,1:T(8,128)(2,1)S(1)}, bf16[2,2,48,1120]{3,2,0,1:T(8,128)(2,1)S(1)}, u32[]{:S(2)}, u32[]{:S(2)}) collective-permute-start(bf16[2,2,48,1120]{3,2,0,1:T(8,128)(2,1)S(1)} %get-tuple-element.161), channel_id=1, source_target_pairs={{0,8},{1,9},{2,10},{3,11},{4,12},{5,13},{6,14},{7,15},{8,0},{9,1},... | collective-permute-start | bytes 1290248 | tf_op jit(solution)/shard_map/ppermute | solution.py:82
  95.5 18.8 %collective-permute-start.21 = (bf16[4,48,1120]{2,1,0:T(8,128)(2,1)}, bf16[4,48,1120]{2,1,0:T(8,128)(2,1)}, u32[]{:S(2)}, u32[]{:S(2)}) collective-permute-start(bf16[4,48,1120]{2,1,0:T(8,128)(2,1)} %get-tuple-element.171), channel_id=1, source_target_pairs={{0,4},{1,5},{2,6},{3,7},{4,0},{5,1},{6,2},{7,3},{8,12},{9,13},{10,... | collective-permute-start | bytes 1290248 | tf_op jit(solution)/shard_map/ppermute | solution.py:82
  97.7 22.8 %collective-permute-start.23 = (bf16[2,2,48,1120]{3,2,0,1:T(8,128)(2,1)S(1)}, bf16[2,2,48,1120]{3,2,0,1:T(8,128)(2,1)S(1)}, u32[]{:S(2)}, u32[]{:S(2)}) collective-permute-start(bf16[2,2,48,1120]{3,2,0,1:T(8,128)(2,1)S(1)} %get-tuple-element.174), channel_id=1, source_target_pairs={{0,8},{1,9},{2,10},{3,11},{4,12},{5,13},{6,14},{7,15},{8,0},{9,1},... | collective-permute-start | bytes 1290248 | tf_op jit(solution)/shard_map/ppermute | solution.py:82
  115.4 25.2 %collective-permute-start.24 = (bf16[8,48,1120]{2,1,0:T(8,128)(2,1)S(1)}, bf16[8,48,1120]{2,1,0:T(8,128)(2,1)S(1)}, u32[]{:S(2)}, u32[]{:S(2)}) collective-permute-start(bf16[8,48,1120]{2,1,0:T(8,128)(2,1)S(1)} %pad_maximum_fusion.5.refs_0_), channel_id=1, source_target_pairs={{0,16},{16,0},{1,17},{17,1},{2,18},{18,2},{3,19},{19,3},{4,20},{20... | collective-permute-start | bytes 2580488 | tf_op jit(solution)/shard_map/ppermute | solution.py:80
  120.6 20.0 %collective-permute-start.25 = (bf16[4,48,1120]{2,1,0:T(8,128)(2,1)S(1)}, bf16[4,48,1120]{2,1,0:T(8,128)(2,1)S(1)}, u32[]{:S(2)}, u32[]{:S(2)}) collective-permute-start(bf16[4,48,1120]{2,1,0:T(8,128)(2,1)S(1)} %get-tuple-element.178), channel_id=1, source_target_pairs={{0,4},{1,5},{2,6},{3,7},{4,0},{5,1},{6,2},{7,3},{8,12},{9,13},{10,... | collective-permute-start | bytes 1290248 | tf_op jit(solution)/shard_map/ppermute | solution.py:82
  120.7 19.9 %collective-permute-start.22 = (bf16[1,128,1536]{2,1,0:T(8,128)(2,1)S(1)}, bf16[1,128,1536]{2,1,0:T(8,128)(2,1)S(1)}, u32[]{:S(2)}, u32[]{:S(2)}) collective-permute-start(bf16[1,128,1536]{2,1,0:T(8,128)(2,1)S(1)} %bitcast.358), channel_id=1, source_target_pairs={{0,8},{1,9},{2,10},{3,11},{4,12},{5,13},{6,14},{7,15},{8,0},{9,1},... | collective-permute-start | bytes 1179656 | tf_op jit(solution)/shard_map/ppermute | solution.py:82
  141.8 22.3 %collective-permute-start.30 = (bf16[8,48,1120]{2,1,0:T(8,128)(2,1)}, bf16[8,48,1120]{2,1,0:T(8,128)(2,1)S(1)}, u32[]{:S(2)}, u32[]{:S(2)}) collective-permute-start(bf16[8,48,1120]{2,1,0:T(8,128)(2,1)} %pad_maximum_fusion.6.refs_0_), channel_id=1, source_target_pairs={{0,16},{16,0},{1,17},{17,1},{2,18},{18,2},{3,19},{19,3},{4,20},{20... | collective-permute-start | bytes 2580488 | tf_op jit(solution)/shard_map/ppermute | solution.py:80
  145.6 20.8 %collective-permute-start.29 = (bf16[1,128,1536]{2,1,0:T(8,128)(2,1)S(1)}, bf16[1,128,1536]{2,1,0:T(8,128)(2,1)S(1)}, u32[]{:S(2)}, u32[]{:S(2)}) collective-permute-start(bf16[1,128,1536]{2,1,0:T(8,128)(2,1)S(1)} %copy-done.6), channel_id=1, source_target_pairs={{0,8},{1,9},{2,10},{3,11},{4,12},{5,13},{6,14},{7,15},{8,0},{9,1},... | collective-permute-start | bytes 1179656 | tf_op jit(solution)/shard_map/ppermute | solution.py:82
  146.9 19.6 %collective-permute-start.27 = (bf16[2,64,1536]{2,1,0:T(8,128)(2,1)S(1)}, bf16[2,64,1536]{2,1,0:T(8,128)(2,1)S(1)}, u32[]{:S(2)}, u32[]{:S(2)}) collective-permute-start(bf16[2,64,1536]{2,1,0:T(8,128)(2,1)S(1)} %get-tuple-element.180), channel_id=1, source_target_pairs={{0,4},{1,5},{2,6},{3,7},{4,0},{5,1},{6,2},{7,3},{8,12},{9,13},{10,... | collective-permute-start | bytes 1179656 | tf_op jit(solution)/shard_map/ppermute | solution.py:82
  147.6 18.9 %collective-permute-start.28 = (bf16[2,64,1536]{2,1,0:T(8,128)(2,1)S(1)}, bf16[2,64,1536]{2,1,0:T(8,128)(2,1)S(1)}, u32[]{:S(2)}, u32[]{:S(2)}) collective-permute-start(bf16[2,64,1536]{2,1,0:T(8,128)(2,1)S(1)} %get-tuple-element.181), channel_id=1, source_target_pairs={{0,2},{1,3},{2,0},{3,1},{4,6},{5,7},{6,4},{7,5},{8,10},{9,11},{10,... | collective-permute-start | bytes 1179656 | tf_op jit(solution)/shard_map/ppermute | solution.py:82
  164.3 21.1 %collective-permute-start.33 = (bf16[16,48,1120]{2,1,0:T(8,128)(2,1)S(1)}, bf16[16,48,1120]{2,1,0:T(8,128)(2,1)S(1)}, u32[]{:S(2)}, u32[]{:S(2)}) collective-permute-start(bf16[16,48,1120]{2,1,0:T(8,128)(2,1)S(1)} %pad_maximum_fusion.1), channel_id=1, source_target_pairs={{0,1},{1,0},{2,3},{3,2},{4,5},{5,4},{6,7},{7,6},{8,9},{9,8},{10,11... | collective-permute-start | bytes 5160968 | tf_op jit(solution)/shard_map/ppermute | solution.py:82
  166.5 21.6 %collective-permute-start.34 = (bf16[16,48,1120]{2,1,0:T(8,128)(2,1)S(1)}, bf16[16,48,1120]{2,1,0:T(8,128)(2,1)S(1)}, u32[]{:S(2)}, u32[]{:S(2)}) collective-permute-start(bf16[16,48,1120]{2,1,0:T(8,128)(2,1)S(1)} %pad_maximum_fusion.2), channel_id=1, source_target_pairs={{0,1},{1,0},{2,3},{3,2},{4,5},{5,4},{6,7},{7,6},{8,9},{9,8},{10,11... | collective-permute-start | bytes 5160968 | tf_op jit(solution)/shard_map/ppermute | solution.py:82
  188.1 26.6 %collective-permute-start.35 = (bf16[4,64,1536]{2,1,0:T(8,128)(2,1)S(1)}, bf16[4,64,1536]{2,1,0:T(8,128)(2,1)S(1)}, u32[]{:S(2)}, u32[]{:S(2)}) collective-permute-start(bf16[4,64,1536]{2,1,0:T(8,128)(2,1)S(1)} %pad_maximum_fusion.13), channel_id=1, source_target_pairs={{0,2},{1,3},{2,0},{3,1},{4,6},{5,7},{6,4},{7,5},{8,10},{9,11},{10,... | collective-permute-start | bytes 2359304 | tf_op jit(solution)/shard_map/ppermute | solution.py:82
  188.6 26.0 %collective-permute-start.36 = (bf16[4,64,1536]{2,1,0:T(8,128)(2,1)S(1)}, bf16[4,64,1536]{2,1,0:T(8,128)(2,1)S(1)}, u32[]{:S(2)}, u32[]{:S(2)}) collective-permute-start(bf16[4,64,1536]{2,1,0:T(8,128)(2,1)S(1)} %pad_maximum_fusion.14), channel_id=1, source_target_pairs={{0,4},{1,5},{2,6},{3,7},{4,0},{5,1},{6,2},{7,3},{8,12},{9,13},{10,... | collective-permute-start | bytes 2359304 | tf_op jit(solution)/shard_map/ppermute | solution.py:82
  189.3 34.7 %collective-permute-start.37 = (bf16[4,64,1536]{2,1,0:T(8,128)(2,1)S(1)}, bf16[4,64,1536]{2,1,0:T(8,128)(2,1)S(1)}, u32[]{:S(2)}, u32[]{:S(2)}) collective-permute-start(bf16[4,64,1536]{2,1,0:T(8,128)(2,1)S(1)} %pad_maximum_fusion.15), channel_id=1, source_target_pairs={{0,2},{1,3},{2,0},{3,1},{4,6},{5,7},{6,4},{7,5},{8,10},{9,11},{10,... | collective-permute-start | bytes 2359304 | tf_op jit(solution)/shard_map/ppermute | solution.py:82
  190.8 33.5 %collective-permute-start.38 = (bf16[4,64,1536]{2,1,0:T(8,128)(2,1)S(1)}, bf16[4,64,1536]{2,1,0:T(8,128)(2,1)S(1)}, u32[]{:S(2)}, u32[]{:S(2)}) collective-permute-start(bf16[4,64,1536]{2,1,0:T(8,128)(2,1)S(1)} %pad_maximum_fusion.16), channel_id=1, source_target_pairs={{0,4},{1,5},{2,6},{3,7},{4,0},{5,1},{6,2},{7,3},{8,12},{9,13},{10,... | collective-permute-start | bytes 2359304 | tf_op jit(solution)/shard_map/ppermute | solution.py:82
  241.2 18.7 %collective-permute-start.40 = (bf16[256,1536]{1,0:T(8,128)(2,1)S(1)}, bf16[256,1536]{1,0:T(8,128)(2,1)S(1)}, u32[]{:S(2)}, u32[]{:S(2)}) collective-permute-start(bf16[256,1536]{1,0:T(8,128)(2,1)S(1)} %get-tuple-element.199), channel_id=1, source_target_pairs={{0,4},{1,5},{2,6},{3,7},{4,0},{5,1},{6,2},{7,3},{8,12},{9,13},{10,... | collective-permute-start | bytes 2359304 | tf_op jit(solution)/shard_map/ppermute | solution.py:82
  241.6 18.3 %collective-permute-start.39 = (bf16[256,1536]{1,0:T(8,128)(2,1)S(1)}, bf16[256,1536]{1,0:T(8,128)(2,1)S(1)}, u32[]{:S(2)}, u32[]{:S(2)}) collective-permute-start(bf16[256,1536]{1,0:T(8,128)(2,1)S(1)} %get-tuple-element.197), channel_id=1, source_target_pairs={{0,2},{1,3},{2,0},{3,1},{4,6},{5,7},{6,4},{7,5},{8,10},{9,11},{10,... | collective-permute-start | bytes 2359304 | tf_op jit(solution)/shard_map/ppermute | solution.py:82
  280.1 20.2 %collective-permute-start.45 = (bf16[1,128,1536]{2,1,0:T(8,128)(2,1)S(1)}, bf16[1,128,1536]{2,1,0:T(8,128)(2,1)}, u32[]{:S(2)}, u32[]{:S(2)}) collective-permute-start(bf16[1,128,1536]{2,1,0:T(8,128)(2,1)S(1)} %fusion.27), channel_id=1, source_target_pairs={{0,8},{1,9},{2,10},{3,11},{4,12},{5,13},{6,14},{7,15},{8,0},{9,1},... | collective-permute-start | bytes 1179656 | tf_op jit(solution)/shard_map/ppermute | solution.py:82
  280.6 36.1 %collective-permute-start.44 = (bf16[256,1536]{1,0:T(8,128)(2,1)}, bf16[256,1536]{1,0:T(8,128)(2,1)}, u32[]{:S(2)}, u32[]{:S(2)}) collective-permute-start(bf16[256,1536]{1,0:T(8,128)(2,1)} %convolution_convert_fusion.3), channel_id=1, source_target_pairs={{0,2},{1,3},{2,0},{3,1},{4,6},{5,7},{6,4},{7,5},{8,10},{9,11},{10,... | collective-permute-start | bytes 2359304 | tf_op jit(solution)/shard_map/ppermute | solution.py:82
  281.3 35.5 %collective-permute-start.47 = (bf16[256,1536]{1,0:T(8,128)(2,1)}, bf16[256,1536]{1,0:T(8,128)(2,1)}, u32[]{:S(2)}, u32[]{:S(2)}) collective-permute-start(bf16[256,1536]{1,0:T(8,128)(2,1)} %convolution_convert_fusion.2), channel_id=1, source_target_pairs={{0,4},{1,5},{2,6},{3,7},{4,0},{5,1},{6,2},{7,3},{8,12},{9,13},{10,... | collective-permute-start | bytes 2359304 | tf_op jit(solution)/shard_map/ppermute | solution.py:82
  284.4 29.4 %collective-permute-start.46 = (bf16[8,48,1120]{2,1,0:T(8,128)(2,1)}, bf16[8,48,1120]{2,1,0:T(8,128)(2,1)}, u32[]{:S(2)}, u32[]{:S(2)}) collective-permute-start(bf16[8,48,1120]{2,1,0:T(8,128)(2,1)} %fusion.10), channel_id=1, source_target_pairs={{0,16},{16,0},{1,17},{17,1},{2,18},{18,2},{3,19},{19,3},{4,20},{20... | collective-permute-start | bytes 2580488 | tf_op jit(solution)/shard_map/ppermute | solution.py:80
  285.9 30.9 %collective-permute-start.48 = (bf16[2,8,48,1120]{3,2,1,0:T(8,128)(2,1)}, bf16[2,8,48,1120]{3,2,1,0:T(8,128)(2,1)}, u32[]{:S(2)}, u32[]{:S(2)}) collective-permute-start(bf16[2,8,48,1120]{3,2,1,0:T(8,128)(2,1)} %get-tuple-element.223), channel_id=1, source_target_pairs={{0,1},{1,0},{2,3},{3,2},{4,5},{5,4},{6,7},{7,6},{8,9},{9,8},{10,11... | collective-permute-start | bytes 5160968 | tf_op jit(solution)/shard_map/ppermute | solution.py:82
  318.4 21.4 %collective-permute-start.52 = (bf16[1,2,2,48,1120]{4,3,0,2,1:T(8,128)(2,1)}, bf16[1,2,2,48,1120]{4,3,0,2,1:T(8,128)(2,1)}, u32[]{:S(2)}, u32[]{:S(2)}) collective-permute-start(bf16[1,2,2,48,1120]{4,3,0,2,1:T(8,128)(2,1)} %get-tuple-element.231), channel_id=1, source_target_pairs={{0,8},{1,9},{2,10},{3,11},{4,12},{5,13},{6,14},{7,15},{8,0},{9,1},... | collective-permute-start | bytes 1290248 | tf_op jit(solution)/shard_map/ppermute | solution.py:82
  321.5 26.8 %collective-permute-start.53 = (bf16[8,48,1120]{2,1,0:T(8,128)(2,1)}, bf16[8,48,1120]{2,1,0:T(8,128)(2,1)}, u32[]{:S(2)}, u32[]{:S(2)}) collective-permute-start(bf16[8,48,1120]{2,1,0:T(8,128)(2,1)} %fusion.11), channel_id=1, source_target_pairs={{0,16},{16,0},{1,17},{17,1},{2,18},{18,2},{3,19},{19,3},{4,20},{20... | collective-permute-start | bytes 2580488 | tf_op jit(solution)/shard_map/ppermute | solution.py:80
  339.3 15.6 %collective-permute-start.54 = (bf16[768,2048]{1,0:T(8,128)(2,1)S(1)}, bf16[768,2048]{1,0:T(8,128)(2,1)S(1)}, u32[]{:S(2)}, u32[]{:S(2)}) collective-permute-start(bf16[768,2048]{1,0:T(8,128)(2,1)S(1)} %convolution_convert_fusion.1), channel_id=1, source_target_pairs={{0,1},{1,0},{2,3},{3,2},{4,5},{5,4},{6,7},{7,6},{8,9},{9,8},{10,11... | collective-permute-start | bytes 9437192 | tf_op jit(solution)/shard_map/ppermute | solution.py:82
  354.9 20.1 %collective-permute-start.56 = (bf16[1,128,1536]{2,1,0:T(8,128)(2,1)S(1)}, bf16[1,128,1536]{2,1,0:T(8,128)(2,1)S(1)}, u32[]{:S(2)}, u32[]{:S(2)}) collective-permute-start(bf16[1,128,1536]{2,1,0:T(8,128)(2,1)S(1)} %fusion.26), channel_id=1, source_target_pairs={{0,8},{1,9},{2,10},{3,11},{4,12},{5,13},{6,14},{7,15},{8,0},{9,1},... | collective-permute-start | bytes 1179656 | tf_op jit(solution)/shard_map/ppermute | solution.py:82
  355.9 28.0 %collective-permute-start.59 = (bf16[768,1536]{1,0:T(8,128)(2,1)S(1)}, bf16[768,1536]{1,0:T(8,128)(2,1)S(1)}, u32[]{:S(2)}, u32[]{:S(2)}) collective-permute-start(bf16[768,1536]{1,0:T(8,128)(2,1)S(1)} %copy-done.62), channel_id=1, source_target_pairs={{0,1},{1,0},{2,3},{3,2},{4,5},{5,4},{6,7},{7,6},{8,9},{9,8},{10,11... | collective-permute-start | bytes 7077896 | tf_op jit(solution)/shard_map/ppermute | solution.py:82
  357.0 24.3 %collective-permute-start.58 = (bf16[2,2,2,48,768]{4,3,2,1,0:T(8,128)(2,1)S(1)}, bf16[2,2,2,48,768]{4,3,2,1,0:T(8,128)(2,1)S(1)}, u32[]{:S(2)}, u32[]{:S(2)}) collective-permute-start(bf16[2,2,2,48,768]{4,3,2,1,0:T(8,128)(2,1)S(1)} %slice_bitcast_fusion.11), channel_id=1, source_target_pairs={{0,4},{1,5},{2,6},{3,7},{4,0},{5,1},{6,2},{7,3},{8,12},{9,13},{10,... | collective-permute-start | bytes 1769480 | tf_op jit(solution)/shard_map/ppermute | solution.py:82
  359.1 25.8 %collective-permute-start.60 = (bf16[280,1536]{1,0:T(8,128)(2,1)S(1)}, bf16[280,1536]{1,0:T(8,128)(2,1)S(1)}, u32[]{:S(2)}, u32[]{:S(2)}) collective-permute-start(bf16[280,1536]{1,0:T(8,128)(2,1)S(1)} %get-tuple-element.253), channel_id=1, source_target_pairs={{0,16},{16,0},{1,17},{17,1},{2,18},{18,2},{3,19},{19,3},{4,20},{20... | collective-permute-start | bytes 2580488 | tf_op jit(solution)/shard_map/ppermute | solution.py:80
  360.0 23.6 %collective-permute-start.57 = (bf16[2,2,2,48,1280]{4,3,2,1,0:T(8,128)(2,1)S(1)}, bf16[2,2,2,48,1280]{4,3,2,1,0:T(8,128)(2,1)S(1)}, u32[]{:S(2)}, u32[]{:S(2)}) collective-permute-start(bf16[2,2,2,48,1280]{4,3,2,1,0:T(8,128)(2,1)S(1)} %slice_bitcast_fusion.6), channel_id=1, source_target_pairs={{0,2},{1,3},{2,0},{3,1},{4,6},{5,7},{6,4},{7,5},{8,10},{9,11},{10,... | collective-permute-start | bytes 2949128 | tf_op jit(solution)/shard_map/ppermute | solution.py:82
  386.5 22.4 %collective-permute-start.64 = (bf16[2,2,48,1120]{3,2,0,1:T(8,128)(2,1)S(1)}, bf16[2,2,48,1120]{3,2,0,1:T(8,128)(2,1)S(1)}, u32[]{:S(2)}, u32[]{:S(2)}) collective-permute-start(bf16[2,2,48,1120]{3,2,0,1:T(8,128)(2,1)S(1)} %get-tuple-element.257), channel_id=1, source_target_pairs={{0,4},{1,5},{2,6},{3,7},{4,0},{5,1},{6,2},{7,3},{8,12},{9,13},{10,... | collective-permute-start | bytes 1290248 | tf_op jit(solution)/shard_map/ppermute | solution.py:82
  388.3 20.6 %collective-permute-start.65 = (bf16[1,2,2,48,1120]{4,3,0,1,2:T(8,128)(2,1)S(1)}, bf16[1,2,2,48,1120]{4,3,0,1,2:T(8,128)(2,1)S(1)}, u32[]{:S(2)}, u32[]{:S(2)}) collective-permute-start(bf16[1,2,2,48,1120]{4,3,0,1,2:T(8,128)(2,1)S(1)} %bitcast.407), channel_id=1, source_target_pairs={{0,2},{1,3},{2,0},{3,1},{4,6},{5,7},{6,4},{7,5},{8,10},{9,11},{10,... | collective-permute-start | bytes 1290248 | tf_op jit(solution)/shard_map/ppermute | solution.py:82
  409.0 19.5 %collective-permute-start.67 = (bf16[1,2,48,2048]{3,2,1,0:T(8,128)(2,1)S(1)}, bf16[1,2,48,2048]{3,2,1,0:T(8,128)(2,1)S(1)}, u32[]{:S(2)}, u32[]{:S(2)}) collective-permute-start(bf16[1,2,48,2048]{3,2,1,0:T(8,128)(2,1)S(1)} %fusion.13), channel_id=1, source_target_pairs={{0,8},{1,9},{2,10},{3,11},{4,12},{5,13},{6,14},{7,15},{8,0},{9,1},... | collective-permute-start | bytes 1179656 | tf_op jit(solution)/shard_map/ppermute | solution.py:82
  411.0 17.6 %collective-permute-start.68 = (bf16[4,48,1120]{2,1,0:T(8,128)(2,1)S(1)}, bf16[4,48,1120]{2,1,0:T(8,128)(2,1)S(1)}, u32[]{:S(2)}, u32[]{:S(2)}) collective-permute-start(bf16[4,48,1120]{2,1,0:T(8,128)(2,1)S(1)} %get-tuple-element.261), channel_id=1, source_target_pairs={{0,2},{1,3},{2,0},{3,1},{4,6},{5,7},{6,4},{7,5},{8,10},{9,11},{10,... | collective-permute-start | bytes 1290248 | tf_op jit(solution)/shard_map/ppermute | solution.py:82
  412.3 18.9 %collective-permute-start.69 = (bf16[2,2,48,1120]{3,2,0,1:T(8,128)(2,1)S(1)}, bf16[2,2,48,1120]{3,2,0,1:T(8,128)(2,1)S(1)}, u32[]{:S(2)}, u32[]{:S(2)}) collective-permute-start(bf16[2,2,48,1120]{3,2,0,1:T(8,128)(2,1)S(1)} %get-tuple-element.262), channel_id=1, source_target_pairs={{0,4},{1,5},{2,6},{3,7},{4,0},{5,1},{6,2},{7,3},{8,12},{9,13},{10,... | collective-permute-start | bytes 1290248 | tf_op jit(solution)/shard_map/ppermute | solution.py:82
  413.4 19.5 %collective-permute-start.70 = (bf16[280,1536]{1,0:T(8,128)(2,1)}, bf16[280,1536]{1,0:T(8,128)(2,1)S(1)}, u32[]{:S(2)}, u32[]{:S(2)}) collective-permute-start(bf16[280,1536]{1,0:T(8,128)(2,1)} %get-tuple-element.263), channel_id=1, source_target_pairs={{0,16},{16,0},{1,17},{17,1},{2,18},{18,2},{3,19},{19,3},{4,20},{20... | collective-permute-start | bytes 2580488 | tf_op jit(solution)/shard_map/ppermute | solution.py:80
  434.9 17.7 %collective-permute-start.73 = (bf16[2,2,2,48,1024]{4,3,2,1,0:T(8,128)(2,1)S(1)}, bf16[2,2,2,48,1024]{4,3,2,1,0:T(8,128)(2,1)S(1)}, u32[]{:S(2)}, u32[]{:S(2)}) collective-permute-start(bf16[2,2,2,48,1024]{4,3,2,1,0:T(8,128)(2,1)S(1)} %slice_bitcast_fusion.9), channel_id=1, source_target_pairs={{0,2},{1,3},{2,0},{3,1},{4,6},{5,7},{6,4},{7,5},{8,10},{9,11},{10,... | collective-permute-start | bytes 2359304 | tf_op jit(solution)/shard_map/ppermute | solution.py:82
  439.2 18.7 %collective-permute-start.76 = (bf16[4,48,1120]{2,1,0:T(8,128)(2,1)S(1)}, bf16[4,48,1120]{2,1,0:T(8,128)(2,1)S(1)}, u32[]{:S(2)}, u32[]{:S(2)}) collective-permute-start(bf16[4,48,1120]{2,1,0:T(8,128)(2,1)S(1)} %get-tuple-element.269), channel_id=1, source_target_pairs={{0,8},{1,9},{2,10},{3,11},{4,12},{5,13},{6,14},{7,15},{8,0},{9,1},... | collective-permute-start | bytes 1290248 | tf_op jit(solution)/shard_map/ppermute | solution.py:82
  440.3 23.5 %collective-permute-start.77 = (bf16[48,8960]{1,0:T(8,128)(2,1)S(1)}, bf16[48,8960]{1,0:T(8,128)(2,1)S(1)}, u32[]{:S(2)}, u32[]{:S(2)}) collective-permute-start(bf16[48,8960]{1,0:T(8,128)(2,1)S(1)} %shard_map.194.gate), channel_id=1, source_target_pairs={{0,16},{16,0},{1,17},{17,1},{2,18},{18,2},{3,19},{19,3},{4,20},{20... | collective-permute-start | bytes 2580488 | tf_op jit(solution)/shard_map/ppermute | solution.py:80
  465.4 19.3 %collective-permute-start.82 = (bf16[48,8960]{1,0:T(8,128)(2,1)S(1)}, bf16[48,8960]{1,0:T(8,128)(2,1)S(1)}, u32[]{:S(2)}, u32[]{:S(2)}) collective-permute-start(bf16[48,8960]{1,0:T(8,128)(2,1)S(1)} %shard_map.195.up), channel_id=1, source_target_pairs={{0,16},{16,0},{1,17},{17,1},{2,18},{18,2},{3,19},{19,3},{4,20},{20... | collective-permute-start | bytes 2580488 | tf_op jit(solution)/shard_map/ppermute | solution.py:80
  466.9 17.9 %collective-permute-start.80 = (f32[5120]{0:T(1024)S(1)}, f32[5120]{0:T(1024)S(1)}, u32[]{:S(2)}, u32[]{:S(2)}) collective-permute-start(f32[5120]{0:T(1024)S(1)} %add.1244), channel_id=1, source_target_pairs={{0,16},{16,0},{1,17},{17,1},{2,18},{18,2},{3,19},{19,3},{4,20},{20... | collective-permute-start | bytes 61448 | tf_op jit(solution)/shard_map/ppermute | solution.py:80
  (134 other events, 1103.0 us)

commit v5 on v4

--- a/solution.py
+++ b/solution.py
@@ -779,8 +779,7 @@
     lanes.beside(normed_two)
     token = Move(gather_tokens(normed_two, token_blocks))
     lanes.round(token, gate, up)
-    lanes.round(down, (up, 2), (cot, 2))
-    lanes.round(token, (gate, 3))
+    lanes.round(token, (gate, 3), down, (up, 2), (cot, 2))
     lanes.round(cot, up)
     parts = lanes.drain(gate, up)
     gate_full, up_full = [weave_part(*part, me, s) for part in parts]
@@ -840,7 +839,7 @@
     other = Move(swap("y", give))
     lanes.more(other)
     (got,) = lanes.drain(other)
-    out = Move(scatter_weight(attended_turned, grad_branch, s, 1024))
+    out = Move(scatter_weight(attended_turned, grad_branch, s, 768))
     grad_projected, input_grad, gain_one_part, bias_part = whole_call(
         project_back_kernel,
         (
@@ -857,8 +856,8 @@
     qkv = Move(scatter_weight(normed_turned, grad_projected, s, 1280))
     sums = Move(sum_everywhere(join(gain_one_part[0], bias_part[0], gain_two_part[0])))
     lanes.round(qkv, down, result)
-    lanes.round(qkv, (result, 2), out, down)
-    lanes.round(qkv, gate, up, sums)
+    lanes.round(down, qkv, out, (result, 2))
+    lanes.round(qkv, sums, up, gate)
     lanes.round(qkv, gate, up, down, sums)
     lanes.round(qkv, out, (up, 2), (gate, 2), sums)
     lanes.round(qkv, out, sums)

time: 497 us -> 488 us (0.982)
  waiting for transfers between devices: 207 us -> 194 us
    ppermute x68, waiting for transfers between devices: 179 us -> 167 us  [more(): value = lax.ppermute(value, 'fsdp', [(i, i ^ link) for i in range(size)])]
    unnamed x193 -> x189, local copies, waits for them, and re-layouts: 16.7 us -> 18.7 us
  transfers between devices with their start and end apart: 84 -> 84, of which waited for: 43 -> 38; matrix products, arithmetic and copies ran while one was open for 16% -> 16% of each run, Pallas kernels for 17% -> 18%
where the time goes in v5:
time: 488 us; the launch traced here: 484 us
  waiting for transfers between devices  194 us (40%)
  Pallas kernels  104 us (21%)
  starting transfers between devices  84.6 us (17%)
  other arithmetic  42.4 us (9%)
  local copies, waits for them, and re-layouts  34.4 us (7%)
  matrix products  21.2 us (4%)
    ppermute x68, waiting for transfers between devices, more(): value = lax.ppermute(value, 'fsdp', [(i, i ^ link) for i in range(size)])  167 us
    ppermute x68, starting transfers between devices, more(): value = lax.ppermute(value, 'fsdp', [(i, i ^ link) for i in range(size)])  66.5 us
    pallas_call x15, Pallas kernels, whole_call(): pl.pallas_call(kernel, out_shape=out_shape, in_specs=[pl.BlockSpec(memory...  53.4 us
    pallas_call x2, Pallas kernels, feed_forward(): pl.pallas_call(feed_kernel, grid=(steps,), out_shape=(units, units, units...  35 us
    ppermute x16, waiting for transfers between devices, more(): value = lax.ppermute(value, 'seq', [(0, 1), (1, 0)])  26.5 us
    unnamed x189, local copies, waits for them, and re-layouts  18.7 us
    ppermute x16, starting transfers between devices, more(): value = lax.ppermute(value, 'seq', [(0, 1), (1, 0)])  18.1 us
    pallas_call x2, Pallas kernels, gate_up_grad(): pl.pallas_call(functools.partial(grad_kernel, count, unit), out_shape=[ja...  15.6 us
  transfers between devices with their start and end apart: 84, of which 38 were waited for; matrix products, arithmetic and copies ran while one was open for 16% of the time, Pallas kernels for 18%

profile of v5, /device:TPU:0, one launch (start us, length us, event | category | flops | bytes accessed | tf_op | source)
XLA Modules:
  0.0 484.4 jit_solution(11208240217744183679)
XLA Ops:
  1.7 4.1 collective-permute-start
  11.1 3.7 collective-permute-done
  19.6 3.4 collective-permute-start.6
  30.6 4.9 %collective-permute-done.6 = bf16[1,96,1536]{2,1,0:T(8,128)(2,1)S(1)} collective-permute-done((bf16[1,96,1536]{2,1,0:T(8,128)(2,1)S(1)}, bf16[1,96,1536]{2,1,0:T(8,128)(2,1)S(1)}, u32[]{:S(2)}, u32[]{:S(2)}) %collective-permute-start.6) | collective-permute-done | bytes 294944 | tf_op jit(solution)/shard_map/ppermute | solution.py:82
  35.5 5.8 %collective-permute-done.5 = bf16[4,48,640]{2,1,0:T(8,128)(2,1)S(1)} collective-permute-done((bf16[4,48,640]{2,1,0:T(8,128)(2,1)S(1)}, bf16[4,48,640]{2,1,0:T(8,128)(2,1)S(1)}, u32[]{:S(2)}, u32[]{:S(2)}) %collective-permute-start.5) | collective-permute-done | bytes 245792 | tf_op jit(solution)/shard_map/ppermute | solution.py:82
  47.0 9.2 %collective-permute-done.11 = bf16[8,48,640]{2,1,0:T(8,128)(2,1)S(1)} collective-permute-done((bf16[8,48,640]{2,1,0:T(8,128)(2,1)S(1)}, bf16[8,48,640]{2,1,0:T(8,128)(2,1)S(1)}, u32[]{:S(2)}, u32[]{:S(2)}) %collective-permute-start.11) | collective-permute-done | bytes 491552 | tf_op jit(solution)/shard_map/ppermute | solution.py:82
  70.6 5.0 %shard_map.179 = bf16[32,48,2048]{2,1,0:T(8,128)(2,1)} custom-call(s32[32]{0:T(128)S(1)} %stack.444.where, bf16[16,48,2048]{2,1,0:T(8,128)(2,1)S(1)} %pad_maximum_fusion.refs_0_, bf16[16,48,2048]{2,1,0:T(8,128)(2,1)} %collective-permute-done.15.refs_1_), custom_call_target="tpu_custom_call" | custom-call | bytes 12582912 | tf_op jit(solution)/shard_map/pallas_call | solution.py:131
  75.7 4.1 shard_map.180
  79.8 2.8 collective-permute-done.18
  85.0 7.4 %collective-permute-done.16 = bf16[2,2,48,1120]{3,2,0,1:T(8,128)(2,1)S(1)} collective-permute-done((bf16[2,2,48,1120]{3,2,0,1:T(8,128)(2,1)S(1)}, bf16[2,2,48,1120]{3,2,0,1:T(8,128)(2,1)S(1)}, u32[]{:S(2)}, u32[]{:S(2)}) %collective-permute-start.16) | collective-permute-done | bytes 430112 | tf_op jit(solution)/shard_map/ppermute | solution.py:82
  93.2 2.3 fusion.61
  98.8 4.2 shard_map.181
  103.1 7.7 %shard_map.182 = (bf16[128,1536]{1,0:T(8,128)(2,1)S(1)}, f32[128,128]{1,0:T(8,128)S(1)}, f32[128,1536]{1,0:T(8,128)S(1)}, bf16[128,1536]{1,0:T(8,128)(2,1)S(1)}) custom-call(s32[1]{0:T(128)} %bitcast.at, bf16[128,1536]{1,0:T(8,128)(2,1)S(1)} %bitcast.344, bf16[128,1536]{1,0:T(8,128)(2,1)S(1)} %get-tuple-element.159.queries, ...), custom_call_target="tpu_custom_call" | custom-call | flops 1006632960 | bytes 7413248 | tf_op jit(solution)/shard_map/pallas_call | solution.py:131
  110.8 3.4 collective-permute-done.21
  115.5 5.0 %collective-permute-done.23 = bf16[2,2,48,1120]{3,2,0,1:T(8,128)(2,1)S(1)} collective-permute-done((bf16[2,2,48,1120]{3,2,0,1:T(8,128)(2,1)S(1)}, bf16[2,2,48,1120]{3,2,0,1:T(8,128)(2,1)S(1)}, u32[]{:S(2)}, u32[]{:S(2)}) %collective-permute-start.23) | collective-permute-done | bytes 430112 | tf_op jit(solution)/shard_map/ppermute | solution.py:82
  122.7 17.9 %collective-permute-done.22 = bf16[1,128,1536]{2,1,0:T(8,128)(2,1)S(1)} collective-permute-done((bf16[1,128,1536]{2,1,0:T(8,128)(2,1)S(1)}, bf16[1,128,1536]{2,1,0:T(8,128)(2,1)S(1)}, u32[]{:S(2)}, u32[]{:S(2)}) %collective-permute-start.22) | collective-permute-done | bytes 393248 | tf_op jit(solution)/shard_map/ppermute | solution.py:82
  146.5 2.5 pad_maximum_fusion.1
  149.0 13.9 %collective-permute-done.33.refs_1_ = bf16[8,48,1120]{2,1,0:T(8,128)(2,1)S(1)} collective-permute-done((bf16[8,48,1120]{2,1,0:T(8,128)(2,1)S(1)}, bf16[8,48,1120]{2,1,0:T(8,128)(2,1)S(1)}, u32[]{:S(2)}, u32[]{:S(2)}) %collective-permute-start.33) | collective-permute-done | bytes 860192 | tf_op jit(solution)/shard_map/ppermute | solution.py:80
  171.8 4.0 shard_map.185.down_weight
  175.8 3.6 shard_map.183
  185.1 2.7 shard_map.184
  187.8 18.1 %shard_map.186 = (bf16[512,1152]{1,0:T(8,128)(2,1)S(1)}, bf16[512,1152]{1,0:T(8,128)(2,1)S(1)}, bf16[512,1152]{1,0:T(8,128)(2,1)}, bf16[512,1536]{1,0:T(8,128)(2...) custom-call(bf16[256,1536]{1,0:T(8,128)(2,1)S(1)} %bitcast.352, ...), custom_call_target="tpu_custom_call" | custom-call | flops 9059696640 | bytes 20447232 | tf_op jit(solution)/shard_map/pallas_call | solution.py:679
  205.9 10.3 %collective-permute-done.37 = bf16[4,64,1536]{2,1,0:T(8,128)(2,1)S(1)} collective-permute-done((bf16[4,64,1536]{2,1,0:T(8,128)(2,1)S(1)}, bf16[4,64,1536]{2,1,0:T(8,128)(2,1)S(1)}, u32[]{:S(2)}, u32[]{:S(2)}) %collective-permute-start.37) | collective-permute-done | bytes 786464 | tf_op jit(solution)/shard_map/ppermute | solution.py:82
  216.6 16.9 %shard_map.187 = (bf16[512,1152]{1,0:T(8,128)(2,1)S(1)}, bf16[512,1152]{1,0:T(8,128)(2,1)}, bf16[512,1152]{1,0:T(8,128)(2,1)}, bf16[512,1536]{1,0:T(8,128)(2,1)}...) custom-call(bf16[256,1536]{1,0:T(8,128)(2,1)S(1)} %bitcast.364, ...), custom_call_target="tpu_custom_call" | custom-call | flops 9059696640 | bytes 20447232 | tf_op jit(solution)/shard_map/pallas_call | solution.py:679
  239.2 7.7 %shard_map.188 = (bf16[2,8,48,1120]{3,2,1,0:T(8,128)(2,1)}, bf16[2,8,48,1120]{3,2,1,0:T(8,128)(2,1)}) custom-call(s32[2]{0:T(128)S(1)} %get-tuple-element.329.at, bf16[512,1536]{1,0:T(8,128)(2,1)S(1)} %copy-done.37, bf16[512,1536]{1,0:T(8,128)(2,1)S(1)} %copy-done.39, bf16[512,1152]{1,0:T(8,128)(2,1)S(1)} %get-tuple-element.205.refs_2_, ...), custom_call_target="tpu_custom_call" | custom-call | flops 3623878656 | bytes 12386304 | tf_op jit(solution)/shard_map/pallas_call | solution.py:403
  261.3 7.9 %shard_map.190 = (bf16[2,8,48,1120]{3,2,1,0:T(8,128)(2,1)}, bf16[2,8,48,1120]{3,2,1,0:T(8,128)(2,1)}) custom-call(s32[2]{0:T(128)S(1)} %get-tuple-element.329.at, bf16[512,1536]{1,0:T(8,128)(2,1)S(1)} %copy-done.38, bf16[512,1536]{1,0:T(8,128)(2,1)S(1)} %copy-done.40, bf16[512,1152]{1,0:T(8,128)(2,1)S(1)} %copy-done.41, bf16[512,1152]{1,0:T(8,128)(2,1)S(1)} %copy-done.42), custom_call_target="tpu_custom_call" | custom-call | flops 3623878656 | bytes 12386304 | tf_op jit(solution)/shard_map/pallas_call | solution.py:403
  280.1 5.0 %fusion.76 = f32[1152,1536]{1,0:T(8,128)} fusion(bf16[512,1152]{1,0:T(8,128)(2,1)S(1)} %copy-done.33, bf16[512,1536]{1,0:T(8,128)(2,1)S(1)} %copy-done.91), kind=kOutput, calls=%fused_computation.224 | convolution fusion | flops 1811939328 | bytes 9830400 | tf_op jit(solution)/shard_map/dot_general | solution.py:116
  285.1 4.1 fusion
  293.6 8.5 %shard_map.189 = (f32[128,1536]{1,0:T(8,128)S(1)}, bf16[128,1536]{1,0:T(8,128)(2,1)S(1)}, f32[1,1536]{1,0:T(1,128)S(1)}, bf16[128,1536]{1,0:T(8,128)(2,1)S(1)}, ...) custom-call(s32[1]{0:T(128)} %bitcast.at, f32[128,1536]{1,0:T(8,128)S(1)} %fusion.22.grad_normed, ...), custom_call_target="tpu_custom_call" | custom-call | flops 1610612736 | bytes 9516544 | tf_op jit(solution)/shard_map/pallas_call | solution.py:131
  315.0 6.4 %shard_map.191 = (bf16[128,2048]{1,0:T(8,128)(2,1)S(1)}, f32[128,1536]{1,0:T(8,128)}, f32[1,1536]{1,0:T(1,128)S(1)}, f32[1,2048]{1,0:T(1,128)S(1)}) custom-call(s32[1]{0:T(128)} %bitcast.at, bf16[128,1536]{1,0:T(8,128)(2,1)S(1)} %copy-done.22, f32[128,512]{1,0:T(8,128)S(1)} %copy-done.28, bf16[128,512]{1,0:T(8,128)(2,1)S(1)} %collective-permute-done.49.got, ...), custom_call_target="tpu_custom_call" | custom-call | flops 805306368 | bytes 9719808 | tf_op jit(solution)/shard_map/pallas_call | solution.py:131
  321.5 2.3 convolution_add_fusion
  323.8 2.8 convolution_add_fusion.1
  333.8 6.6 %collective-permute-done.50 = bf16[2,64,1536]{2,1,0:T(8,128)(2,1)S(1)} collective-permute-done((bf16[2,64,1536]{2,1,0:T(8,128)(2,1)S(1)}, bf16[2,64,1536]{2,1,0:T(8,128)(2,1)S(1)}, u32[]{:S(2)}, u32[]{:S(2)}) %collective-permute-start.50) | collective-permute-done | bytes 393248 | tf_op jit(solution)/shard_map/ppermute | solution.py:82
  352.6 13.6 %collective-permute-done.56 = bf16[1,128,1536]{2,1,0:T(8,128)(2,1)S(1)} collective-permute-done((bf16[1,128,1536]{2,1,0:T(8,128)(2,1)S(1)}, bf16[1,128,1536]{2,1,0:T(8,128)(2,1)S(1)}, u32[]{:S(2)}, u32[]{:S(2)}) %collective-permute-start.56) | collective-permute-done | bytes 393248 | tf_op jit(solution)/shard_map/ppermute | solution.py:82
  367.1 6.0 %collective-permute-done.59 = bf16[2,2,2,48,768]{4,3,2,1,0:T(8,128)(2,1)S(1)} collective-permute-done((bf16[2,2,2,48,768]{4,3,2,1,0:T(8,128)(2,1)S(1)}, bf16[2,2,2,48,768]{4,3,2,1,0:T(8,128)(2,1)S(1)}, u32[]{:S(2)}, u32[]{:S(2)}) %collective-permute-start.59) | collective-permute-done | bytes 589856 | tf_op jit(solution)/shard_map/ppermute | solution.py:82
  381.4 13.1 %collective-permute-done.63 = bf16[2,2,48,768]{3,2,1,0:T(8,128)(2,1)S(1)} collective-permute-done((bf16[2,2,48,768]{3,2,1,0:T(8,128)(2,1)S(1)}, bf16[2,2,48,768]{3,2,1,0:T(8,128)(2,1)S(1)}, u32[]{:S(2)}, u32[]{:S(2)}) %collective-permute-start.63) | collective-permute-done | bytes 294944 | tf_op jit(solution)/shard_map/ppermute | solution.py:82
  394.8 4.6 collective-permute-done.62
  405.2 7.9 %collective-permute-done.66 = f32[5120]{0:T(1024)S(1)} collective-permute-done((f32[5120]{0:T(1024)S(1)}, f32[5120]{0:T(1024)S(1)}, u32[]{:S(2)}, u32[]{:S(2)}) %collective-permute-start.66) | collective-permute-done | bytes 20512 | tf_op jit(solution)/shard_map/ppermute | solution.py:82
  413.1 6.8 %collective-permute-done.67 = bf16[1,2,48,2048]{3,2,1,0:T(8,128)(2,1)S(1)} collective-permute-done((bf16[1,2,48,2048]{3,2,1,0:T(8,128)(2,1)S(1)}, bf16[1,2,48,2048]{3,2,1,0:T(8,128)(2,1)S(1)}, u32[]{:S(2)}, u32[]{:S(2)}) %collective-permute-start.67) | collective-permute-done | bytes 393248 | tf_op jit(solution)/shard_map/ppermute | solution.py:82
  427.3 7.1 %collective-permute-done.73 = bf16[2,2,2,48,768]{4,3,2,1,0:T(8,128)(2,1)S(1)} collective-permute-done((bf16[2,2,2,48,768]{4,3,2,1,0:T(8,128)(2,1)S(1)}, bf16[2,2,2,48,768]{4,3,2,1,0:T(8,128)(2,1)S(1)}, u32[]{:S(2)}, u32[]{:S(2)}) %collective-permute-start.73) | collective-permute-done | bytes 589856 | tf_op jit(solution)/shard_map/ppermute | solution.py:82
  436.4 7.9 %collective-permute-done.74 = bf16[2,2,2,48,768]{4,3,2,1,0:T(8,128)(2,1)S(1)} collective-permute-done((bf16[2,2,2,48,768]{4,3,2,1,0:T(8,128)(2,1)}, bf16[2,2,2,48,768]{4,3,2,1,0:T(8,128)(2,1)S(1)}, u32[]{:S(2)}, u32[]{:S(2)}) %collective-permute-start.74) | collective-permute-done | bytes 589856 | tf_op jit(solution)/shard_map/ppermute | solution.py:82
  446.1 2.2 convert_add_fusion.5
  448.4 3.5 collective-permute-start.75
  452.9 3.9 collective-permute-done.75
  457.1 2.5 collective-permute-start.82
  459.8 6.2 %collective-permute-done.81 = bf16[1,2,48,1536]{3,2,1,0:T(8,128)(2,1)S(1)} collective-permute-done((bf16[1,2,48,1536]{3,2,1,0:T(8,128)(2,1)S(1)}, bf16[1,2,48,1536]{3,2,1,0:T(8,128)(2,1)S(1)}, u32[]{:S(2)}, u32[]{:S(2)}) %collective-permute-start.81) | collective-permute-done | bytes 294944 | tf_op jit(solution)/shard_map/ppermute | solution.py:82
  466.1 10.4 %collective-permute-done.80 = f32[5120]{0:T(1024)S(1)} collective-permute-done((f32[5120]{0:T(1024)S(1)}, f32[5120]{0:T(1024)S(1)}, u32[]{:S(2)}, u32[]{:S(2)}) %collective-permute-start.80) | collective-permute-done | bytes 20512 | tf_op jit(solution)/shard_map/ppermute | solution.py:80
  478.9 3.3 shard_map.196
  (467 shorter events, 167.2 us)
Async XLA Ops:
  19.6 15.9 %collective-permute-start.6 = (bf16[1,96,1536]{2,1,0:T(8,128)(2,1)S(1)}, bf16[1,96,1536]{2,1,0:T(8,128)(2,1)S(1)}, u32[]{:S(2)}, u32[]{:S(2)}) collective-permute-start(bf16[1,96,1536]{2,1,0:T(8,128)(2,1)S(1)} %bitcast.398), channel_id=1, source_target_pairs={{0,8},{1,9},{2,10},{3,11},{4,12},{5,13},{6,14},{7,15},{8,0},{9,1},... | collective-permute-start | bytes 884744 | tf_op jit(solution)/shard_map/ppermute | solution.py:82
  62.3 20.2 %collective-permute-start.18 = (bf16[4,96,1024]{2,1,0:T(8,128)(2,1)}, bf16[4,96,1024]{2,1,0:T(8,128)(2,1)}, u32[]{:S(2)}, u32[]{:S(2)}) collective-permute-start(bf16[4,96,1024]{2,1,0:T(8,128)(2,1)} %pad_maximum_fusion.12), channel_id=1, source_target_pairs={{0,2},{1,3},{2,0},{3,1},{4,6},{5,7},{6,4},{7,5},{8,10},{9,11},{10,... | collective-permute-start | bytes 2359304 | tf_op jit(solution)/shard_map/ppermute | solution.py:82
  64.6 17.9 %collective-permute-start.17 = (bf16[4,96,512]{2,1,0:T(8,128)(2,1)}, bf16[4,96,512]{2,1,0:T(8,128)(2,1)}, u32[]{:S(2)}, u32[]{:S(2)}) collective-permute-start(bf16[4,96,512]{2,1,0:T(8,128)(2,1)} %pad_maximum_fusion.33), channel_id=1, source_target_pairs={{0,4},{1,5},{2,6},{3,7},{4,0},{5,1},{6,2},{7,3},{8,12},{9,13},{10,... | collective-permute-start | bytes 1179656 | tf_op jit(solution)/shard_map/ppermute | solution.py:82
  69.9 22.5 %collective-permute-start.16 = (bf16[2,2,48,1120]{3,2,0,1:T(8,128)(2,1)S(1)}, bf16[2,2,48,1120]{3,2,0,1:T(8,128)(2,1)S(1)}, u32[]{:S(2)}, u32[]{:S(2)}) collective-permute-start(bf16[2,2,48,1120]{3,2,0,1:T(8,128)(2,1)S(1)} %get-tuple-element.161), channel_id=1, source_target_pairs={{0,8},{1,9},{2,10},{3,11},{4,12},{5,13},{6,14},{7,15},{8,0},{9,1},... | collective-permute-start | bytes 1290248 | tf_op jit(solution)/shard_map/ppermute | solution.py:82
  95.5 18.8 %collective-permute-start.21 = (bf16[4,48,1120]{2,1,0:T(8,128)(2,1)}, bf16[4,48,1120]{2,1,0:T(8,128)(2,1)}, u32[]{:S(2)}, u32[]{:S(2)}) collective-permute-start(bf16[4,48,1120]{2,1,0:T(8,128)(2,1)} %get-tuple-element.171), channel_id=1, source_target_pairs={{0,4},{1,5},{2,6},{3,7},{4,0},{5,1},{6,2},{7,3},{8,12},{9,13},{10,... | collective-permute-start | bytes 1290248 | tf_op jit(solution)/shard_map/ppermute | solution.py:82
  97.7 22.8 %collective-permute-start.23 = (bf16[2,2,48,1120]{3,2,0,1:T(8,128)(2,1)S(1)}, bf16[2,2,48,1120]{3,2,0,1:T(8,128)(2,1)S(1)}, u32[]{:S(2)}, u32[]{:S(2)}) collective-permute-start(bf16[2,2,48,1120]{3,2,0,1:T(8,128)(2,1)S(1)} %get-tuple-element.174), channel_id=1, source_target_pairs={{0,8},{1,9},{2,10},{3,11},{4,12},{5,13},{6,14},{7,15},{8,0},{9,1},... | collective-permute-start | bytes 1290248 | tf_op jit(solution)/shard_map/ppermute | solution.py:82
  115.4 25.2 %collective-permute-start.24 = (bf16[8,48,1120]{2,1,0:T(8,128)(2,1)S(1)}, bf16[8,48,1120]{2,1,0:T(8,128)(2,1)S(1)}, u32[]{:S(2)}, u32[]{:S(2)}) collective-permute-start(bf16[8,48,1120]{2,1,0:T(8,128)(2,1)S(1)} %pad_maximum_fusion.5.refs_0_), channel_id=1, source_target_pairs={{0,16},{16,0},{1,17},{17,1},{2,18},{18,2},{3,19},{19,3},{4,20},{20... | collective-permute-start | bytes 2580488 | tf_op jit(solution)/shard_map/ppermute | solution.py:80
  120.6 20.0 %collective-permute-start.25 = (bf16[4,48,1120]{2,1,0:T(8,128)(2,1)S(1)}, bf16[4,48,1120]{2,1,0:T(8,128)(2,1)S(1)}, u32[]{:S(2)}, u32[]{:S(2)}) collective-permute-start(bf16[4,48,1120]{2,1,0:T(8,128)(2,1)S(1)} %get-tuple-element.178), channel_id=1, source_target_pairs={{0,4},{1,5},{2,6},{3,7},{4,0},{5,1},{6,2},{7,3},{8,12},{9,13},{10,... | collective-permute-start | bytes 1290248 | tf_op jit(solution)/shard_map/ppermute | solution.py:82
  120.7 19.9 %collective-permute-start.22 = (bf16[1,128,1536]{2,1,0:T(8,128)(2,1)S(1)}, bf16[1,128,1536]{2,1,0:T(8,128)(2,1)S(1)}, u32[]{:S(2)}, u32[]{:S(2)}) collective-permute-start(bf16[1,128,1536]{2,1,0:T(8,128)(2,1)S(1)} %bitcast.358), channel_id=1, source_target_pairs={{0,8},{1,9},{2,10},{3,11},{4,12},{5,13},{6,14},{7,15},{8,0},{9,1},... | collective-permute-start | bytes 1179656 | tf_op jit(solution)/shard_map/ppermute | solution.py:82
  140.6 26.2 %collective-permute-start.29 = (bf16[560,1536]{1,0:T(8,128)(2,1)}, bf16[560,1536]{1,0:T(8,128)(2,1)}, u32[]{:S(2)}, u32[]{:S(2)}) collective-permute-start(bf16[560,1536]{1,0:T(8,128)(2,1)} %own.1), channel_id=1, source_target_pairs={{0,1},{1,0},{2,3},{3,2},{4,5},{5,4},{6,7},{7,6},{8,9},{9,8},{10,11... | collective-permute-start | bytes 5160968 | tf_op jit(solution)/shard_map/ppermute | solution.py:82
  141.5 21.4 %collective-permute-start.33 = (bf16[8,48,1120]{2,1,0:T(8,128)(2,1)S(1)}, bf16[8,48,1120]{2,1,0:T(8,128)(2,1)S(1)}, u32[]{:S(2)}, u32[]{:S(2)}) collective-permute-start(bf16[8,48,1120]{2,1,0:T(8,128)(2,1)S(1)} %pad_maximum_fusion.6.refs_0_), channel_id=1, source_target_pairs={{0,16},{16,0},{1,17},{17,1},{2,18},{18,2},{3,19},{19,3},{4,20},{20... | collective-permute-start | bytes 2580488 | tf_op jit(solution)/shard_map/ppermute | solution.py:80
  144.0 22.7 %collective-permute-start.26 = (bf16[2,64,1536]{2,1,0:T(8,128)(2,1)}, bf16[2,64,1536]{2,1,0:T(8,128)(2,1)}, u32[]{:S(2)}, u32[]{:S(2)}) collective-permute-start(bf16[2,64,1536]{2,1,0:T(8,128)(2,1)} %get-tuple-element.179), channel_id=1, source_target_pairs={{0,4},{1,5},{2,6},{3,7},{4,0},{5,1},{6,2},{7,3},{8,12},{9,13},{10,... | collective-permute-start | bytes 1179656 | tf_op jit(solution)/shard_map/ppermute | solution.py:82
  144.4 22.4 %collective-permute-start.27 = (bf16[2,64,1536]{2,1,0:T(8,128)(2,1)}, bf16[2,64,1536]{2,1,0:T(8,128)(2,1)}, u32[]{:S(2)}, u32[]{:S(2)}) collective-permute-start(bf16[2,64,1536]{2,1,0:T(8,128)(2,1)} %get-tuple-element.180), channel_id=1, source_target_pairs={{0,2},{1,3},{2,0},{3,1},{4,6},{5,7},{6,4},{7,5},{8,10},{9,11},{10,... | collective-permute-start | bytes 1179656 | tf_op jit(solution)/shard_map/ppermute | solution.py:82
  144.9 22.4 %collective-permute-start.28 = (bf16[1,128,1536]{2,1,0:T(8,128)(2,1)S(1)}, bf16[1,128,1536]{2,1,0:T(8,128)(2,1)}, u32[]{:S(2)}, u32[]{:S(2)}) collective-permute-start(bf16[1,128,1536]{2,1,0:T(8,128)(2,1)S(1)} %copy-done.8), channel_id=1, source_target_pairs={{0,8},{1,9},{2,10},{3,11},{4,12},{5,13},{6,14},{7,15},{8,0},{9,1},... | collective-permute-start | bytes 1179656 | tf_op jit(solution)/shard_map/ppermute | solution.py:82
  181.0 24.9 %collective-permute-start.35 = (bf16[4,64,1536]{2,1,0:T(8,128)(2,1)S(1)}, bf16[4,64,1536]{2,1,0:T(8,128)(2,1)S(1)}, u32[]{:S(2)}, u32[]{:S(2)}) collective-permute-start(bf16[4,64,1536]{2,1,0:T(8,128)(2,1)S(1)} %pad_maximum_fusion.13), channel_id=1, source_target_pairs={{0,2},{1,3},{2,0},{3,1},{4,6},{5,7},{6,4},{7,5},{8,10},{9,11},{10,... | collective-permute-start | bytes 2359304 | tf_op jit(solution)/shard_map/ppermute | solution.py:82
  181.6 24.3 %collective-permute-start.36 = (bf16[4,64,1536]{2,1,0:T(8,128)(2,1)S(1)}, bf16[4,64,1536]{2,1,0:T(8,128)(2,1)S(1)}, u32[]{:S(2)}, u32[]{:S(2)}) collective-permute-start(bf16[4,64,1536]{2,1,0:T(8,128)(2,1)S(1)} %pad_maximum_fusion.14), channel_id=1, source_target_pairs={{0,4},{1,5},{2,6},{3,7},{4,0},{5,1},{6,2},{7,3},{8,12},{9,13},{10,... | collective-permute-start | bytes 2359304 | tf_op jit(solution)/shard_map/ppermute | solution.py:82
  183.2 33.0 %collective-permute-start.37 = (bf16[4,64,1536]{2,1,0:T(8,128)(2,1)S(1)}, bf16[4,64,1536]{2,1,0:T(8,128)(2,1)S(1)}, u32[]{:S(2)}, u32[]{:S(2)}) collective-permute-start(bf16[4,64,1536]{2,1,0:T(8,128)(2,1)S(1)} %pad_maximum_fusion.15), channel_id=1, source_target_pairs={{0,2},{1,3},{2,0},{3,1},{4,6},{5,7},{6,4},{7,5},{8,10},{9,11},{10,... | collective-permute-start | bytes 2359304 | tf_op jit(solution)/shard_map/ppermute | solution.py:82
  184.7 31.9 %collective-permute-start.38 = (bf16[4,64,1536]{2,1,0:T(8,128)(2,1)S(1)}, bf16[4,64,1536]{2,1,0:T(8,128)(2,1)S(1)}, u32[]{:S(2)}, u32[]{:S(2)}) collective-permute-start(bf16[4,64,1536]{2,1,0:T(8,128)(2,1)S(1)} %pad_maximum_fusion.16), channel_id=1, source_target_pairs={{0,4},{1,5},{2,6},{3,7},{4,0},{5,1},{6,2},{7,3},{8,12},{9,13},{10,... | collective-permute-start | bytes 2359304 | tf_op jit(solution)/shard_map/ppermute | solution.py:82
  233.5 17.6 %collective-permute-start.40 = (bf16[256,1536]{1,0:T(8,128)(2,1)S(1)}, bf16[256,1536]{1,0:T(8,128)(2,1)S(1)}, u32[]{:S(2)}, u32[]{:S(2)}) collective-permute-start(bf16[256,1536]{1,0:T(8,128)(2,1)S(1)} %get-tuple-element.199), channel_id=1, source_target_pairs={{0,4},{1,5},{2,6},{3,7},{4,0},{5,1},{6,2},{7,3},{8,12},{9,13},{10,... | collective-permute-start | bytes 2359304 | tf_op jit(solution)/shard_map/ppermute | solution.py:82
  235.3 17.0 %collective-permute-start.39 = (bf16[256,1536]{1,0:T(8,128)(2,1)S(1)}, bf16[256,1536]{1,0:T(8,128)(2,1)S(1)}, u32[]{:S(2)}, u32[]{:S(2)}) collective-permute-start(bf16[256,1536]{1,0:T(8,128)(2,1)S(1)} %get-tuple-element.197), channel_id=1, source_target_pairs={{0,2},{1,3},{2,0},{3,1},{4,6},{5,7},{6,4},{7,5},{8,10},{9,11},{10,... | collective-permute-start | bytes 2359304 | tf_op jit(solution)/shard_map/ppermute | solution.py:82
  271.3 21.1 %collective-permute-start.45 = (bf16[1,128,1536]{2,1,0:T(8,128)(2,1)S(1)}, bf16[1,128,1536]{2,1,0:T(8,128)(2,1)}, u32[]{:S(2)}, u32[]{:S(2)}) collective-permute-start(bf16[1,128,1536]{2,1,0:T(8,128)(2,1)S(1)} %fusion.26), channel_id=1, source_target_pairs={{0,8},{1,9},{2,10},{3,11},{4,12},{5,13},{6,14},{7,15},{8,0},{9,1},... | collective-permute-start | bytes 1179656 | tf_op jit(solution)/shard_map/ppermute | solution.py:82
  272.7 36.0 %collective-permute-start.44 = (bf16[256,1536]{1,0:T(8,128)(2,1)}, bf16[256,1536]{1,0:T(8,128)(2,1)}, u32[]{:S(2)}, u32[]{:S(2)}) collective-permute-start(bf16[256,1536]{1,0:T(8,128)(2,1)} %convolution_convert_fusion.3), channel_id=1, source_target_pairs={{0,2},{1,3},{2,0},{3,1},{4,6},{5,7},{6,4},{7,5},{8,10},{9,11},{10,... | collective-permute-start | bytes 2359304 | tf_op jit(solution)/shard_map/ppermute | solution.py:82
  273.8 35.0 %collective-permute-start.47 = (bf16[256,1536]{1,0:T(8,128)(2,1)}, bf16[256,1536]{1,0:T(8,128)(2,1)}, u32[]{:S(2)}, u32[]{:S(2)}) collective-permute-start(bf16[256,1536]{1,0:T(8,128)(2,1)} %convolution_convert_fusion.2), channel_id=1, source_target_pairs={{0,4},{1,5},{2,6},{3,7},{4,0},{5,1},{6,2},{7,3},{8,12},{9,13},{10,... | collective-permute-start | bytes 2359304 | tf_op jit(solution)/shard_map/ppermute | solution.py:82
  276.5 29.3 %collective-permute-start.46 = (bf16[8,48,1120]{2,1,0:T(8,128)(2,1)}, bf16[8,48,1120]{2,1,0:T(8,128)(2,1)}, u32[]{:S(2)}, u32[]{:S(2)}) collective-permute-start(bf16[8,48,1120]{2,1,0:T(8,128)(2,1)} %fusion.11), channel_id=1, source_target_pairs={{0,16},{16,0},{1,17},{17,1},{2,18},{18,2},{3,19},{19,3},{4,20},{20... | collective-permute-start | bytes 2580488 | tf_op jit(solution)/shard_map/ppermute | solution.py:80
  278.0 30.8 %collective-permute-start.48 = (bf16[2,8,48,1120]{3,2,1,0:T(8,128)(2,1)}, bf16[2,8,48,1120]{3,2,1,0:T(8,128)(2,1)}, u32[]{:S(2)}, u32[]{:S(2)}) collective-permute-start(bf16[2,8,48,1120]{3,2,1,0:T(8,128)(2,1)} %get-tuple-element.223), channel_id=1, source_target_pairs={{0,1},{1,0},{2,3},{3,2},{4,5},{5,4},{6,7},{7,6},{8,9},{9,8},{10,11... | collective-permute-start | bytes 5160968 | tf_op jit(solution)/shard_map/ppermute | solution.py:82
  310.4 21.8 %collective-permute-start.52 = (bf16[1,2,2,48,1120]{4,3,0,2,1:T(8,128)(2,1)}, bf16[1,2,2,48,1120]{4,3,0,2,1:T(8,128)(2,1)}, u32[]{:S(2)}, u32[]{:S(2)}) collective-permute-start(bf16[1,2,2,48,1120]{4,3,0,2,1:T(8,128)(2,1)} %get-tuple-element.231), channel_id=1, source_target_pairs={{0,8},{1,9},{2,10},{3,11},{4,12},{5,13},{6,14},{7,15},{8,0},{9,1},... | collective-permute-start | bytes 1290248 | tf_op jit(solution)/shard_map/ppermute | solution.py:82
  314.0 26.7 %collective-permute-start.53 = (bf16[8,48,1120]{2,1,0:T(8,128)(2,1)}, bf16[8,48,1120]{2,1,0:T(8,128)(2,1)}, u32[]{:S(2)}, u32[]{:S(2)}) collective-permute-start(bf16[8,48,1120]{2,1,0:T(8,128)(2,1)} %fusion.12), channel_id=1, source_target_pairs={{0,16},{16,0},{1,17},{17,1},{2,18},{18,2},{3,19},{19,3},{4,20},{20... | collective-permute-start | bytes 2580488 | tf_op jit(solution)/shard_map/ppermute | solution.py:80
  346.4 19.8 %collective-permute-start.56 = (bf16[1,128,1536]{2,1,0:T(8,128)(2,1)S(1)}, bf16[1,128,1536]{2,1,0:T(8,128)(2,1)S(1)}, u32[]{:S(2)}, u32[]{:S(2)}) collective-permute-start(bf16[1,128,1536]{2,1,0:T(8,128)(2,1)S(1)} %fusion.25), channel_id=1, source_target_pairs={{0,8},{1,9},{2,10},{3,11},{4,12},{5,13},{6,14},{7,15},{8,0},{9,1},... | collective-permute-start | bytes 1179656 | tf_op jit(solution)/shard_map/ppermute | solution.py:82
  348.0 27.5 %collective-permute-start.60 = (bf16[768,1536]{1,0:T(8,128)(2,1)S(1)}, bf16[768,1536]{1,0:T(8,128)(2,1)S(1)}, u32[]{:S(2)}, u32[]{:S(2)}) collective-permute-start(bf16[768,1536]{1,0:T(8,128)(2,1)S(1)} %copy-done.59), channel_id=1, source_target_pairs={{0,1},{1,0},{2,3},{3,2},{4,5},{5,4},{6,7},{7,6},{8,9},{9,8},{10,11... | collective-permute-start | bytes 7077896 | tf_op jit(solution)/shard_map/ppermute | solution.py:82
  349.0 24.1 %collective-permute-start.59 = (bf16[2,2,2,48,768]{4,3,2,1,0:T(8,128)(2,1)S(1)}, bf16[2,2,2,48,768]{4,3,2,1,0:T(8,128)(2,1)S(1)}, u32[]{:S(2)}, u32[]{:S(2)}) collective-permute-start(bf16[2,2,2,48,768]{4,3,2,1,0:T(8,128)(2,1)S(1)} %slice_bitcast_fusion.13), channel_id=1, source_target_pairs={{0,4},{1,5},{2,6},{3,7},{4,0},{5,1},{6,2},{7,3},{8,12},{9,13},{10,... | collective-permute-start | bytes 1769480 | tf_op jit(solution)/shard_map/ppermute | solution.py:82
  350.2 25.3 %collective-permute-start.57 = (bf16[280,1536]{1,0:T(8,128)(2,1)S(1)}, bf16[280,1536]{1,0:T(8,128)(2,1)S(1)}, u32[]{:S(2)}, u32[]{:S(2)}) collective-permute-start(bf16[280,1536]{1,0:T(8,128)(2,1)S(1)} %get-tuple-element.247), channel_id=1, source_target_pairs={{0,16},{16,0},{1,17},{17,1},{2,18},{18,2},{3,19},{19,3},{4,20},{20... | collective-permute-start | bytes 2580488 | tf_op jit(solution)/shard_map/ppermute | solution.py:80
  351.5 23.6 %collective-permute-start.58 = (bf16[2,2,2,48,1280]{4,3,2,1,0:T(8,128)(2,1)S(1)}, bf16[2,2,2,48,1280]{4,3,2,1,0:T(8,128)(2,1)S(1)}, u32[]{:S(2)}, u32[]{:S(2)}) collective-permute-start(bf16[2,2,2,48,1280]{4,3,2,1,0:T(8,128)(2,1)S(1)} %slice_bitcast_fusion.7), channel_id=1, source_target_pairs={{0,2},{1,3},{2,0},{3,1},{4,6},{5,7},{6,4},{7,5},{8,10},{9,11},{10,... | collective-permute-start | bytes 2949128 | tf_op jit(solution)/shard_map/ppermute | solution.py:82
  375.5 19.3 %collective-permute-start.61 = (f32[5120]{0:T(1024)S(1)}, f32[5120]{0:T(1024)S(1)}, u32[]{:S(2)}, u32[]{:S(2)}) collective-permute-start(f32[5120]{0:T(1024)S(1)} %pad_maximum_fusion.43), channel_id=1, source_target_pairs={{0,1},{1,0},{2,3},{3,2},{4,5},{5,4},{6,7},{7,6},{8,9},{9,8},{10,11... | collective-permute-start | bytes 61448 | tf_op jit(solution)/shard_map/ppermute | solution.py:82
  375.6 19.0 %collective-permute-start.64 = (bf16[1,2,2,48,1120]{4,3,0,1,2:T(8,128)(2,1)S(1)}, bf16[1,2,2,48,1120]{4,3,0,1,2:T(8,128)(2,1)S(1)}, u32[]{:S(2)}, u32[]{:S(2)}) collective-permute-start(bf16[1,2,2,48,1120]{4,3,0,1,2:T(8,128)(2,1)S(1)} %bitcast.406), channel_id=1, source_target_pairs={{0,2},{1,3},{2,0},{3,1},{4,6},{5,7},{6,4},{7,5},{8,10},{9,11},{10,... | collective-permute-start | bytes 1290248 | tf_op jit(solution)/shard_map/ppermute | solution.py:82
  376.7 18.0 %collective-permute-start.65 = (bf16[2,2,48,1120]{3,2,0,1:T(8,128)(2,1)S(1)}, bf16[2,2,48,1120]{3,2,0,1:T(8,128)(2,1)S(1)}, u32[]{:S(2)}, u32[]{:S(2)}) collective-permute-start(bf16[2,2,48,1120]{3,2,0,1:T(8,128)(2,1)S(1)} %get-tuple-element.258), channel_id=1, source_target_pairs={{0,4},{1,5},{2,6},{3,7},{4,0},{5,1},{6,2},{7,3},{8,12},{9,13},{10,... | collective-permute-start | bytes 1290248 | tf_op jit(solution)/shard_map/ppermute | solution.py:82
  377.2 17.3 %collective-permute-start.63 = (bf16[2,2,48,768]{3,2,1,0:T(8,128)(2,1)S(1)}, bf16[2,2,48,768]{3,2,1,0:T(8,128)(2,1)S(1)}, u32[]{:S(2)}, u32[]{:S(2)}) collective-permute-start(bf16[2,2,48,768]{3,2,1,0:T(8,128)(2,1)S(1)} %fusion.65), channel_id=1, source_target_pairs={{0,2},{1,3},{2,0},{3,1},{4,6},{5,7},{6,4},{7,5},{8,10},{9,11},{10,... | collective-permute-start | bytes 884744 | tf_op jit(solution)/shard_map/ppermute | solution.py:82
  378.3 21.2 %collective-permute-start.62 = (bf16[2,2,48,1280]{3,2,1,0:T(8,128)(2,1)S(1)}, bf16[2,2,48,1280]{3,2,1,0:T(8,128)(2,1)S(1)}, u32[]{:S(2)}, u32[]{:S(2)}) collective-permute-start(bf16[2,2,48,1280]{3,2,1,0:T(8,128)(2,1)S(1)} %fusion.38), channel_id=1, source_target_pairs={{0,4},{1,5},{2,6},{3,7},{4,0},{5,1},{6,2},{7,3},{8,12},{9,13},{10,... | collective-permute-start | bytes 1474568 | tf_op jit(solution)/shard_map/ppermute | solution.py:82
  399.5 21.7 %collective-permute-start.70 = (bf16[280,1536]{1,0:T(8,128)(2,1)S(1)}, bf16[280,1536]{1,0:T(8,128)(2,1)S(1)}, u32[]{:S(2)}, u32[]{:S(2)}) collective-permute-start(bf16[280,1536]{1,0:T(8,128)(2,1)S(1)} %get-tuple-element.263), channel_id=1, source_target_pairs={{0,16},{16,0},{1,17},{17,1},{2,18},{18,2},{3,19},{19,3},{4,20},{20... | collective-permute-start | bytes 2580488 | tf_op jit(solution)/shard_map/ppermute | solution.py:80
  400.3 19.6 %collective-permute-start.67 = (bf16[1,2,48,2048]{3,2,1,0:T(8,128)(2,1)S(1)}, bf16[1,2,48,2048]{3,2,1,0:T(8,128)(2,1)S(1)}, u32[]{:S(2)}, u32[]{:S(2)}) collective-permute-start(bf16[1,2,48,2048]{3,2,1,0:T(8,128)(2,1)S(1)} %fusion.14), channel_id=1, source_target_pairs={{0,8},{1,9},{2,10},{3,11},{4,12},{5,13},{6,14},{7,15},{8,0},{9,1},... | collective-permute-start | bytes 1179656 | tf_op jit(solution)/shard_map/ppermute | solution.py:82
  401.8 18.1 %collective-permute-start.68 = (bf16[4,48,1120]{2,1,0:T(8,128)(2,1)S(1)}, bf16[4,48,1120]{2,1,0:T(8,128)(2,1)S(1)}, u32[]{:S(2)}, u32[]{:S(2)}) collective-permute-start(bf16[4,48,1120]{2,1,0:T(8,128)(2,1)S(1)} %get-tuple-element.261), channel_id=1, source_target_pairs={{0,2},{1,3},{2,0},{3,1},{4,6},{5,7},{6,4},{7,5},{8,10},{9,11},{10,... | collective-permute-start | bytes 1290248 | tf_op jit(solution)/shard_map/ppermute | solution.py:82
  402.9 18.3 %collective-permute-start.69 = (bf16[2,2,48,1120]{3,2,0,1:T(8,128)(2,1)S(1)}, bf16[2,2,48,1120]{3,2,0,1:T(8,128)(2,1)S(1)}, u32[]{:S(2)}, u32[]{:S(2)}) collective-permute-start(bf16[2,2,48,1120]{3,2,0,1:T(8,128)(2,1)S(1)} %get-tuple-element.262), channel_id=1, source_target_pairs={{0,4},{1,5},{2,6},{3,7},{4,0},{5,1},{6,2},{7,3},{8,12},{9,13},{10,... | collective-permute-start | bytes 1290248 | tf_op jit(solution)/shard_map/ppermute | solution.py:82
  422.2 22.1 %collective-permute-start.74 = (bf16[2,2,2,48,768]{4,3,2,1,0:T(8,128)(2,1)}, bf16[2,2,2,48,768]{4,3,2,1,0:T(8,128)(2,1)S(1)}, u32[]{:S(2)}, u32[]{:S(2)}) collective-permute-start(bf16[2,2,2,48,768]{4,3,2,1,0:T(8,128)(2,1)} %slice_bitcast_fusion.10), channel_id=1, source_target_pairs={{0,4},{1,5},{2,6},{3,7},{4,0},{5,1},{6,2},{7,3},{8,12},{9,13},{10,... | collective-permute-start | bytes 1769480 | tf_op jit(solution)/shard_map/ppermute | solution.py:82
  423.7 21.1 %collective-permute-start.71 = (f32[5120]{0:T(1024)S(1)}, f32[5120]{0:T(1024)S(1)}, u32[]{:S(2)}, u32[]{:S(2)}) collective-permute-start(f32[5120]{0:T(1024)S(1)} %add.1238), channel_id=1, source_target_pairs={{0,4},{1,5},{2,6},{3,7},{4,0},{5,1},{6,2},{7,3},{8,12},{9,13},{10,... | collective-permute-start | bytes 61448 | tf_op jit(solution)/shard_map/ppermute | solution.py:82
  425.5 19.2 %collective-permute-start.72 = (bf16[2,48,2048]{2,1,0:T(8,128)(2,1)S(1)}, bf16[2,48,2048]{2,1,0:T(8,128)(2,1)S(1)}, u32[]{:S(2)}, u32[]{:S(2)}) collective-permute-start(bf16[2,48,2048]{2,1,0:T(8,128)(2,1)S(1)} %bitcast.397), channel_id=1, source_target_pairs={{0,16},{16,0},{1,17},{17,1},{2,18},{18,2},{3,19},{19,3},{4,20},{20... | collective-permute-start | bytes 1179656 | tf_op jit(solution)/shard_map/ppermute | solution.py:80
  427.3 24.6 %collective-permute-start.76 = (bf16[4,48,1120]{2,1,0:T(8,128)(2,1)S(1)}, bf16[4,48,1120]{2,1,0:T(8,128)(2,1)S(1)}, u32[]{:S(2)}, u32[]{:S(2)}) collective-permute-start(bf16[4,48,1120]{2,1,0:T(8,128)(2,1)S(1)} %get-tuple-element.269), channel_id=1, source_target_pairs={{0,8},{1,9},{2,10},{3,11},{4,12},{5,13},{6,14},{7,15},{8,0},{9,1},... | collective-permute-start | bytes 1290248 | tf_op jit(solution)/shard_map/ppermute | solution.py:82
  434.5 22.3 %collective-permute-start.77 = (bf16[48,8960]{1,0:T(8,128)(2,1)S(1)}, bf16[48,8960]{1,0:T(8,128)(2,1)S(1)}, u32[]{:S(2)}, u32[]{:S(2)}) collective-permute-start(bf16[48,8960]{1,0:T(8,128)(2,1)S(1)} %shard_map.194.gate), channel_id=1, source_target_pairs={{0,16},{16,0},{1,17},{17,1},{2,18},{18,2},{3,19},{19,3},{4,20},{20... | collective-permute-start | bytes 2580488 | tf_op jit(solution)/shard_map/ppermute | solution.py:80
  457.1 19.3 %collective-permute-start.82 = (bf16[48,8960]{1,0:T(8,128)(2,1)S(1)}, bf16[48,8960]{1,0:T(8,128)(2,1)S(1)}, u32[]{:S(2)}, u32[]{:S(2)}) collective-permute-start(bf16[48,8960]{1,0:T(8,128)(2,1)S(1)} %shard_map.195.up), channel_id=1, source_target_pairs={{0,16},{16,0},{1,17},{17,1},{2,18},{18,2},{3,19},{19,3},{4,20},{20... | collective-permute-start | bytes 2580488 | tf_op jit(solution)/shard_map/ppermute | solution.py:80
  459.7 16.7 %collective-permute-start.80 = (f32[5120]{0:T(1024)S(1)}, f32[5120]{0:T(1024)S(1)}, u32[]{:S(2)}, u32[]{:S(2)}) collective-permute-start(f32[5120]{0:T(1024)S(1)} %add.1244), channel_id=1, source_target_pairs={{0,16},{16,0},{1,17},{17,1},{2,18},{18,2},{3,19},{19,3},{4,20},{20... | collective-permute-start | bytes 61448 | tf_op jit(solution)/shard_map/ppermute | solution.py:80
  (132 other events, 1097.2 us)
